TPU v7x, 512 devices: a whole 4x4x16 slice. The times are simulated.
512 devices in a mesh: dp: 8 (over y, core), expert: 64 (over x, z).
Axes of the slice: x: 4, y: 4, z: 16, core: 2. Of those that a mesh axis runs over, the one named last changes fastest.
Arguments:
- activations: bfloat16 [1024, 8, 1536], P('expert', None, 'dp'), may hold values from -6 to 6
- w_down: bfloat16 [64, 1536, 4096], P('expert', 'dp'), may hold values from -0.15625 to 0.15625
- gate_weights: float32 [1024, 8], P('expert'), may hold values from 0.05 to 1
- cotangent: bfloat16 [1024, 4096], P('expert', 'dp'), may hold values from -0.59765625 to 0.59765625
- expert_ids: int32 [1024, 8], P('expert'), may hold values from 0 to 63, as said below
- replica_pick: int32 [1024, 8], P('expert'), may hold values from 0 to 1, as said below
- placement: int32 [16, 2], replicated, may hold values from 0 to 63, as said below
- group_cap: int32 [64], replicated, may hold values from 1 to 3, as said below
Outputs:
- combined: bfloat16 [1024, 4096], P('expert', 'dp')
- act_grad: bfloat16 [1024, 8, 1536], P('expert', None, 'dp')
- weight_grad: bfloat16 [64, 1536, 4096], P('expert', 'dp')
- gate_grad: float32 [1024, 8], P('expert')
Inputs may be any that keep to these rules, and one draw needn't show every extreme that they name: `expert_ids`: each row names 8 different experts. One expert, drawn from the seed and without a replica, is named by every token; replicated experts are named more often than the others. `replica_pick`: read only for rows whose expert has a replica. `placement`: column 0 holds distinct experts, column 1 distinct indices of expert; no index hosts a replica of the expert it owns, and no expert owned by a host is itself replicated. `group_cap`: the expert named by every token has its owner's entry equal to 3.
All inputs are finite; a program needn't handle non-finite values.
Results may differ from a plain program's by a relative error of at most 0.02.
Values may be sent and summed in bfloat16 or wider, within the bound.
No kernel may reach another device: no remote copies, remote signals or barrier semaphores. Data moves between devices by JAX's collectives and lax.ppermute only.
A program may use at most 64 MiB of HBM per device.

v0:
```python
import jax
import jax.numpy as jnp
from jax import lax
from jax.sharding import PartitionSpec as P


def routing_table(block_ids, block_pick, placement, group_cap):
    n_dev = group_cap.shape[0]
    flat_ids = block_ids.reshape(-1)
    flat_pick = block_pick.reshape(-1)
    match_copy = (flat_ids[:, None] == placement[None, :, 0]).astype(jnp.int32)
    has_copy = jnp.sum(match_copy, axis=1, dtype=jnp.int32)
    host_dev = jnp.sum(match_copy * placement[None, :, 1], axis=1, dtype=jnp.int32)
    to_copy = (has_copy > 0) & (flat_pick == 1)
    destination = jnp.where(to_copy, host_dev, flat_ids)
    row_kind = jnp.where(to_copy, 2, 1).astype(jnp.int32)
    onehot_dest = (destination[:, None] == jnp.arange(n_dev, dtype=jnp.int32)[None, :]).astype(
        jnp.int32
    )
    earlier = jnp.cumsum(onehot_dest, axis=0, dtype=jnp.int32) - onehot_dest
    row_rank = jnp.sum(earlier * onehot_dest, axis=1, dtype=jnp.int32)
    row_limit = jnp.sum(onehot_dest * group_cap[None, :], axis=1, dtype=jnp.int32)
    row_kept = row_rank < row_limit
    return (destination, row_kind, row_rank, row_kept)


def hosted(placement, n_dev):
    at_dev = (placement[:, 1][:, None] == jnp.arange(n_dev, dtype=jnp.int32)[None, :]).astype(
        jnp.int32
    )
    has_at = jnp.sum(at_dev, axis=0, dtype=jnp.int32)
    rep_at = jnp.sum(at_dev * placement[:, 0][:, None], axis=0, dtype=jnp.int32)
    return (has_at, rep_at)


def on_device(
    activations, w_down, gate_weights, cotangent, expert_ids, replica_pick, placement, group_cap
):
    n_dev = lax.axis_size("expert")
    tok_count, top_count, hidden_part = activations.shape
    width = w_down.shape[2]
    capacity = min(tok_count, 3 * tok_count * top_count // (2 * n_dev))
    slot_count = n_dev * capacity
    row_count = tok_count * top_count
    destination, row_kind, row_rank, row_kept = routing_table(
        expert_ids, replica_pick, placement, group_cap
    )
    slot_index = jnp.where(row_kept, destination * capacity + row_rank, slot_count)
    row_numbers = jnp.arange(row_count, dtype=jnp.int32)
    inverse = (
        jnp.full((slot_count + 1,), -1, jnp.int32).at[slot_index].set(row_numbers)[:slot_count]
    )
    slot_valid = inverse >= 0
    slot_rows = jnp.maximum(inverse, 0)
    slot_kind = jnp.where(slot_valid, jnp.take(row_kind, slot_rows, axis=0), 0).reshape(
        n_dev, capacity
    )
    safe_slot = jnp.minimum(slot_index, slot_count - 1)

    def to_slots(values):
        return jnp.where(
            slot_valid[:, None], jnp.take(values, slot_rows, axis=0), jnp.zeros((), values.dtype)
        )

    def to_rows(values):
        return jnp.where(
            row_kept[:, None], jnp.take(values, safe_slot, axis=0), jnp.zeros((), values.dtype)
        )

    has_at, rep_at = hosted(placement, n_dev)
    my_index = lax.axis_index("expert")
    is_host = jnp.take(has_at, my_index) > 0
    choose = (
        (has_at[:, None] > 0) & (rep_at[:, None] == jnp.arange(n_dev, dtype=jnp.int32)[None, :])
    ).astype(jnp.bfloat16)
    local_w = w_down[0]
    pieces = lax.all_to_all(local_w[None], "expert", split_axis=2, concat_axis=0, tiled=True)
    outgoing = jnp.einsum("de,ehc->dhc", choose, pieces, preferred_element_type=jnp.float32).astype(
        jnp.bfloat16
    )
    copy_w = lax.all_to_all(outgoing, "expert", split_axis=0, concat_axis=2, tiled=True)[0]
    flat_act = activations.reshape(row_count, hidden_part)
    sent = to_slots(flat_act).reshape(n_dev, capacity, hidden_part)
    arrived, arrived_kind = (
        lax.all_to_all(sent, "expert", split_axis=0, concat_axis=0, tiled=True),
        lax.all_to_all(slot_kind, "expert", split_axis=0, concat_axis=0, tiled=True),
    )
    inputs = arrived.reshape(slot_count, hidden_part)
    slot_kinds = arrived_kind.reshape(slot_count)
    own_mask = (slot_kinds == 1)[:, None]
    copy_mask = (slot_kinds == 2)[:, None]
    own_in = jnp.where(own_mask, inputs, jnp.zeros_like(inputs))
    copy_in = jnp.where(copy_mask, inputs, jnp.zeros_like(inputs))

    def forward_both(operands):
        return jnp.dot(operands[0], local_w, preferred_element_type=jnp.float32) + jnp.dot(
            operands[1], copy_w, preferred_element_type=jnp.float32
        )

    def forward_owned(operands):
        return jnp.dot(operands[0], local_w, preferred_element_type=jnp.float32)

    partial_value = lax.cond(is_host, forward_both, forward_owned, (own_in, copy_in))
    cotangent_full = lax.all_gather(cotangent, "dp", axis=1, tiled=True)
    returned = lax.all_to_all(
        partial_value.astype(jnp.bfloat16).reshape(n_dev, capacity, width),
        "expert",
        split_axis=0,
        concat_axis=0,
        tiled=True,
    )
    row_values = (
        to_rows(returned.reshape(slot_count, width))
        .astype(jnp.float32)
        .reshape(tok_count, top_count, width)
    )
    mixed_part = jnp.sum(gate_weights[:, :, None] * row_values, axis=1)
    combined = lax.psum_scatter(
        mixed_part.astype(jnp.bfloat16), "dp", scatter_dimension=1, tiled=True
    )
    gate_part = jnp.sum(cotangent_full.astype(jnp.float32)[:, None, :] * row_values, axis=2)
    gate_grad = lax.psum(gate_part, "dp")
    grad_tok = (
        (gate_weights[:, :, None] * cotangent_full.astype(jnp.float32)[:, None, :])
        .astype(jnp.bfloat16)
        .reshape(row_count, width)
    )
    grad_sent = to_slots(grad_tok).reshape(n_dev, capacity, width)
    grad_in = lax.all_to_all(grad_sent, "expert", split_axis=0, concat_axis=0, tiled=True)
    grad_in = grad_in.reshape(slot_count, width)

    def backward_both(operand):
        back_own = lax.dot_general(
            operand, local_w, (((1,), (1,)), ((), ())), preferred_element_type=jnp.float32
        )
        back_copy = lax.dot_general(
            operand, copy_w, (((1,), (1,)), ((), ())), preferred_element_type=jnp.float32
        )
        return jnp.where(own_mask, back_own, jnp.where(copy_mask, back_copy, 0.0)).astype(
            jnp.bfloat16
        )

    def backward_owned(operand):
        back_own = lax.dot_general(
            operand, local_w, (((1,), (1,)), ((), ())), preferred_element_type=jnp.float32
        )
        return jnp.where(own_mask, back_own, 0.0).astype(jnp.bfloat16)

    input_back = lax.cond(is_host, backward_both, backward_owned, grad_in)
    returned_grads = lax.all_to_all(
        input_back.reshape(n_dev, capacity, hidden_part),
        "expert",
        split_axis=0,
        concat_axis=0,
        tiled=True,
    )
    act_grad = to_rows(returned_grads.reshape(slot_count, hidden_part)).reshape(
        tok_count, top_count, hidden_part
    )
    own_grad = lax.dot_general(
        own_in, grad_in, (((0,), (0,)), ((), ())), preferred_element_type=jnp.float32
    )

    def copy_product(operands):
        return lax.dot_general(
            operands[0], operands[1], (((0,), (0,)), ((), ())), preferred_element_type=jnp.float32
        ).astype(jnp.bfloat16)

    def copy_nothing(operands):
        return jnp.zeros((operands[0].shape[1], operands[1].shape[1]), jnp.bfloat16)

    copy_grad = lax.cond(is_host, copy_product, copy_nothing, (copy_in, grad_in))
    grad_pieces = lax.all_to_all(copy_grad[None], "expert", split_axis=2, concat_axis=0, tiled=True)
    homeward = jnp.einsum(
        "de,dhc->ehc", choose, grad_pieces, preferred_element_type=jnp.float32
    ).astype(jnp.bfloat16)
    home_grad = lax.all_to_all(homeward, "expert", split_axis=0, concat_axis=2, tiled=True)[0]
    weight_grad = (own_grad + home_grad.astype(jnp.float32)).astype(jnp.bfloat16)[None]
    return (combined, act_grad, weight_grad, gate_grad)


def solution(mesh):
    return jax.shard_map(
        on_device,
        mesh=mesh,
        in_specs=(
            P("expert", None, "dp"),
            P("expert", "dp", None),
            P("expert", None),
            P("expert", "dp"),
            P("expert", None),
            P("expert", None),
            P(),
            P(),
        ),
        out_specs=(
            P("expert", "dp"),
            P("expert", None, "dp"),
            P("expert", "dp", None),
            P("expert", None),
        ),
        check_vma=False,
    )
```

profile of v0, /device:TPU:6, one launch (start us, length us, event | category | flops | bytes accessed | tf_op | source)
XLA Modules:
  0.0 809.0 jit_solution(3717038787633869883)
XLA Ops:
  7.2 9.9 %copy.94 = bf16[1,192,4096]{1,0,2:T(2,128)(2,1)} copy(bf16[1,192,4096]{2,1,0:T(8,128)(2,1)} %param.15) | data formatting | bytes 3145728 | tf_op args[1]
  17.6 23.5 %reduce.14 = bf16[4096,192]{1,0:T(8,128)(2,1)S(1)} reduce(bf16[4096,1,192]{2,1,0:T(2,128)(2,1)} %bitcast.115, bf16[]{:T(256)} %broadcast.341), dimensions={1}, to_apply=%bitcast.90.reduce_sub_computation | reduce | bytes 3145730
  41.1 3.3 reshape.474
  44.5 18.9 %all-to-all-start.2 = ((bf16[64,2,6144]{2,1,0:T(2,128)(2,1)}), bf16[64,2,6144]{2,1,0:T(2,128)(2,1)S(1)}, u32[]{:S(2)}, u32[]{:S(2)}) async-start(bf16[64,2,6144]{2,1,0:T(2,128)(2,1)} %reshape.474), calls=%async_computation.2 | async-start | bytes 3145728 | tf_op jit(solution)/shard_map/all_to_all | solution.py:77
  71.2 68.4 %all-to-all-done.2 = bf16[64,2,6144]{2,1,0:T(2,128)(2,1)S(1)} async-done(((bf16[64,2,6144]{2,1,0:T(2,128)(2,1)}), bf16[64,2,6144]{2,1,0:T(2,128)(2,1)S(1)}, u32[]{:S(2)}, u32[]{:S(2)}) %all-to-all-start.2) | async-done | bytes 1572896 | tf_op jit(solution)/shard_map/all_to_all | solution.py:77
  139.6 6.9 all-to-all-start
  146.5 7.2 reshape.475
  159.0 12.7 %all-to-all-start.1 = ((bf16[64,3,192]{2,1,0:T(4,128)(2,1)}), bf16[64,3,192]{2,1,0:T(4,128)(2,1)S(1)}, u32[]{:S(2)}, u32[]{:S(2)}) async-start(bf16[64,3,192]{2,1,0:T(4,128)(2,1)} %select_select_fusion.1), calls=%async_computation.1 | async-start | bytes 262144 | tf_op jit(solution)/shard_map/all_to_all | solution.py:85
  176.0 10.5 %all-to-all-done.1 = bf16[64,3,192]{2,1,0:T(4,128)(2,1)S(1)} async-done(((bf16[64,3,192]{2,1,0:T(4,128)(2,1)}), bf16[64,3,192]{2,1,0:T(4,128)(2,1)S(1)}, u32[]{:S(2)}, u32[]{:S(2)}) %all-to-all-start.1) | async-done | bytes 73760 | tf_op jit(solution)/shard_map/all_to_all | solution.py:85
  186.5 6.7 all-to-all-start.3
  195.2 95.2 %all-to-all-done.3 = bf16[64,192,64]{1,2,0:T(8,128)(2,1)} async-done(((bf16[64,192,64]{1,2,0:T(8,128)(2,1)}), bf16[64,192,64]{1,2,0:T(8,128)(2,1)}, u32[]{:S(2)}, u32[]{:S(2)}) %all-to-all-start.3) | async-done | bytes 1572896 | tf_op jit(solution)/shard_map/all_to_all | solution.py:81
  293.4 10.0 %all-to-all-start.4 = ((bf16[64,3,4096]{2,1,0:T(4,128)(2,1)}), bf16[64,3,4096]{2,1,0:T(4,128)(2,1)}, u32[]{:S(2)}, u32[]{:S(2)}) async-start(bf16[64,3,4096]{2,1,0:T(4,128)(2,1)} %reshape.365), calls=%async_computation.4 | async-start | bytes 4194304 | tf_op jit(solution)/shard_map/all_to_all | solution.py:105
  304.2 13.3 %all_gather.3 = bf16[16,4096]{1,0:T(8,128)(2,1)S(1)} all-gather(bf16[16,512]{1,0:T(8,128)(2,1)S(1)} %copy-done.17), channel_id=1, replica_groups=mesh['dp'=8,'expert'=64] {'dp'}, dimensions={1}, use_global_device_ids=true | all-gather | bytes 147456 | tf_op jit(solution)/shard_map/all_gather | solution.py:104
  317.5 83.6 %all-to-all-done.4 = bf16[64,3,4096]{2,1,0:T(4,128)(2,1)} async-done(((bf16[64,3,4096]{2,1,0:T(4,128)(2,1)}), bf16[64,3,4096]{2,1,0:T(4,128)(2,1)}, u32[]{:S(2)}, u32[]{:S(2)}) %all-to-all-start.4) | async-done | bytes 1572896 | tf_op jit(solution)/shard_map/all_to_all | solution.py:105
  401.1 3.1 reshape.366
  406.0 2.8 gather_fusion.3
  408.8 2.8 gather.39
  414.1 7.4 all-to-all-start.5
  421.4 97.6 %all-to-all-done.5 = bf16[64,3,4096]{2,1,0:T(4,128)(2,1)S(1)} async-done(((bf16[64,3,4096]{2,1,0:T(4,128)(2,1)}), bf16[64,3,4096]{2,1,0:T(4,128)(2,1)S(1)}, u32[]{:S(2)}, u32[]{:S(2)}) %all-to-all-start.5) | async-done | bytes 1572896 | tf_op jit(solution)/shard_map/all_to_all | solution.py:129
  522.9 9.9 %copy.105 = bf16[1,192,4096]{1,0,2:T(2,128)(2,1)} copy(bf16[1,192,4096]{2,1,0:T(8,128)(2,1)} %bitcast.125) | data formatting | bytes 3145728 | tf_op jit(solution)/shard_map/broadcast_in_dim | solution.py:173
  532.7 24.9 %reduce.15 = bf16[4096,192]{1,0:T(8,128)(2,1)} reduce(bf16[4096,1,192]{2,1,0:T(2,128)(2,1)} %bitcast.116, bf16[]{:T(256)} %broadcast.341), dimensions={1}, to_apply=%bitcast.92.reduce_sub_computation | reduce | bytes 3145730
  557.6 5.5 reshape.476
  563.2 9.9 %all-to-all-start.7 = ((bf16[64,2,6144]{2,1,0:T(2,128)(2,1)}), bf16[64,2,6144]{2,1,0:T(2,128)(2,1)}, u32[]{:S(2)}, u32[]{:S(2)}) async-start(bf16[64,2,6144]{2,1,0:T(2,128)(2,1)} %reshape.476), calls=%async_computation.8 | async-start | bytes 3145728 | tf_op jit(solution)/shard_map/all_to_all | solution.py:173
  579.4 70.0 %all-to-all-done.7 = bf16[64,2,6144]{2,1,0:T(2,128)(2,1)} async-done(((bf16[64,2,6144]{2,1,0:T(2,128)(2,1)}), bf16[64,2,6144]{2,1,0:T(2,128)(2,1)}, u32[]{:S(2)}, u32[]{:S(2)}) %all-to-all-start.7) | async-done | bytes 1572896 | tf_op jit(solution)/shard_map/all_to_all | solution.py:173
  649.3 7.3 all-to-all-start.6
  656.6 10.7 %reshape.477 = bf16[4096,1,192]{2,1,0:T(2,128)(2,1)} reshape(bf16[64,2,6144]{2,1,0:T(2,128)(2,1)} %all-to-all-done.7) | data formatting | bytes 3145728
  674.1 15.5 %all-to-all-start.8 = ((bf16[64,192,64]{1,2,0:T(8,128)(2,1)}), bf16[64,192,64]{1,2,0:T(8,128)(2,1)}, u32[]{:S(2)}, u32[]{:S(2)}) async-start(bf16[64,192,64]{1,2,0:T(8,128)(2,1)} %copy.107), calls=%async_computation.9 | async-start | bytes 4194304 | tf_op jit(solution)/shard_map/all_to_all | solution.py:177
  692.4 14.8 %psum.7 = f32[16,8]{1,0:T(8,128)S(1)} all-reduce(f32[16,8]{1,0:T(8,128)S(1)} %reduce_sum.100), channel_id=1, replica_groups=mesh['dp'=8,'expert'=64] {'dp'}, use_global_device_ids=true, to_apply=%region_17.18 | all-reduce | flops 128 | bytes 1024 | tf_op jit(solution)/shard_map/psum | solution.py:122
  709.5 77.6 %all-to-all-done.8 = bf16[64,192,64]{1,2,0:T(8,128)(2,1)} async-done(((bf16[64,192,64]{1,2,0:T(8,128)(2,1)}), bf16[64,192,64]{1,2,0:T(8,128)(2,1)}, u32[]{:S(2)}, u32[]{:S(2)}) %all-to-all-start.8) | async-done | bytes 1572896 | tf_op jit(solution)/shard_map/all_to_all | solution.py:177
  787.1 4.1 bitcast_convert_fusion
  791.2 5.3 copy.108
  796.5 5.1 fusion.2
  (157 shorter events, 53.1 us)
Async XLA Ops:
  7.2 62.0 %copy-start = (bf16[16,8,192]{2,1,0:T(8,128)(2,1)S(1)}, bf16[16,8,192]{2,1,0:T(8,128)(2,1)}, u32[]{:S(2)}) copy-start(bf16[16,8,192]{2,1,0:T(8,128)(2,1)} %param.14) | copy-start | bytes 147460
  44.5 19.0 %copy-start.29 = (s32[16,8]{0,1:T(8,128)S(1)}, s32[16,8]{0,1:T(8,128)}, u32[]{:S(2)}) copy-start(s32[16,8]{0,1:T(8,128)} %param.18) | copy-start | bytes 1540
  44.5 19.2 %copy-start.30 = (s32[16,8]{0,1:T(8,128)S(1)}, s32[16,8]{0,1:T(8,128)}, u32[]{:S(2)}) copy-start(s32[16,8]{0,1:T(8,128)} %param.19) | copy-start | bytes 1540
  44.5 19.5 %copy-start.35 = (s32[16,2]{0,1:T(2,128)S(1)}, s32[16,2]{0,1:T(2,128)}, u32[]{:S(2)}) copy-start(s32[16,2]{0,1:T(2,128)} %param.20) | copy-start | bytes 388
  44.5 20.2 %copy-start.36 = (s32[64]{0:T(128)S(1)}, s32[64]{0:T(128)}, u32[]{:S(2)}) copy-start(s32[64]{0:T(128)} %param.21) | copy-start | bytes 772
  44.5 95.1 %all-to-all-start.2 = ((bf16[64,2,6144]{2,1,0:T(2,128)(2,1)}), bf16[64,2,6144]{2,1,0:T(2,128)(2,1)S(1)}, u32[]{:S(2)}, u32[]{:S(2)}) async-start(bf16[64,2,6144]{2,1,0:T(2,128)(2,1)} %reshape.474), calls=%async_computation.2 | async-start | bytes 3145728 | tf_op jit(solution)/shard_map/all_to_all | solution.py:77
  68.3 85.4 %copy-start.7 = (pred[64,3]{1,0:T(8,128)(4,1)}, pred[64,3]{1,0:T(8,128)(4,1)S(1)}, u32[]{:S(2)}) copy-start(pred[64,3]{1,0:T(8,128)(4,1)S(1)} %le.50) | copy-start | bytes 580
  70.3 101.4 %copy-start.21 = (s32[64]{0:T(128)}, s32[64]{0:T(128)S(1)}, u32[]{:S(2)}) copy-start(s32[64]{0:T(128)S(1)} %get-tuple-element.144) | copy-start | bytes 772
  139.6 19.4 %all-to-all-start = ((s32[64,1,3]{2,1,0:T(1,128)}), s32[64,1,3]{2,1,0:T(1,128)S(1)}, u32[]{:S(2)}, u32[]{:S(2)}) async-start(s32[64,1,3]{2,1,0:T(1,128)} %bitcast.9), calls=%async_computation | async-start | bytes 65536 | tf_op jit(solution)/shard_map/all_to_all | solution.py:86
  146.5 25.2 %copy-start.32 = (pred[64]{0:T(512)(128)(4,1)}, pred[64]{0:T(512)(128)(4,1)S(1)}, u32[]{:S(2)}) copy-start(pred[64]{0:T(512)(128)(4,1)S(1)} %broadcast_compare_fusion.4) | copy-start | bytes 196
  159.0 27.5 %all-to-all-start.1 = ((bf16[64,3,192]{2,1,0:T(4,128)(2,1)}), bf16[64,3,192]{2,1,0:T(4,128)(2,1)S(1)}, u32[]{:S(2)}, u32[]{:S(2)}) async-start(bf16[64,3,192]{2,1,0:T(4,128)(2,1)} %select_select_fusion.1), calls=%async_computation.1 | async-start | bytes 262144 | tf_op jit(solution)/shard_map/all_to_all | solution.py:85
  176.0 114.5 %copy-start.2 = (bf16[1,192,4096]{2,1,0:T(8,128)(2,1)S(1)}, bf16[1,192,4096]{2,1,0:T(8,128)(2,1)}, u32[]{:S(2)}) copy-start(bf16[1,192,4096]{2,1,0:T(8,128)(2,1)} %param.15) | copy-start | bytes 4718596
  186.5 103.9 %all-to-all-start.3 = ((bf16[64,192,64]{1,2,0:T(8,128)(2,1)}), bf16[64,192,64]{1,2,0:T(8,128)(2,1)}, u32[]{:S(2)}, u32[]{:S(2)}) async-start(bf16[64,192,64]{1,2,0:T(8,128)(2,1)} %copy.97), calls=%async_computation.3 | async-start | bytes 4194304 | tf_op jit(solution)/shard_map/all_to_all | solution.py:81
  293.3 10.2 %copy-start.24 = (s32[128]{0:T(128)S(1)}, s32[128]{0:T(128)}, u32[]{:S(2)}) copy-start(s32[128]{0:T(128)} %copy-done.23) | copy-start | bytes 1540
  293.3 10.3 %copy-start.28 = (s32[128]{0:T(128)S(1)}, s32[128]{0:T(128)}, u32[]{:S(2)}) copy-start(s32[128]{0:T(128)} %copy-done.27) | copy-start | bytes 1540
  293.3 10.4 %copy-start.31 = (f32[16,8]{0,1:T(8,128)S(1)}, f32[16,8]{0,1:T(8,128)}, u32[]{:S(2)}) copy-start(f32[16,8]{0,1:T(8,128)} %param.16) | copy-start | bytes 1540
  293.3 10.6 %copy-start.12 = (s32[16,8]{1,0:T(8,128)S(1)}, s32[16,8]{1,0:T(8,128)}, u32[]{:S(2)}) copy-start(s32[16,8]{1,0:T(8,128)} %copy-done.11) | copy-start | bytes 1540
  293.4 10.8 %copy-start.17 = (bf16[16,512]{1,0:T(8,128)(2,1)S(1)}, bf16[16,512]{1,0:T(8,128)(2,1)}, u32[]{:S(2)}) copy-start(bf16[16,512]{1,0:T(8,128)(2,1)} %param.17) | copy-start | bytes 49156
  293.4 24.1 %copy-start.34 = (s32[128]{0:T(128)S(1)}, s32[128]{0:T(128)}, u32[]{:S(2)}) copy-start(s32[128]{0:T(128)} %get-tuple-element.150) | copy-start | bytes 1540
  293.4 107.7 %all-to-all-start.4 = ((bf16[64,3,4096]{2,1,0:T(4,128)(2,1)}), bf16[64,3,4096]{2,1,0:T(4,128)(2,1)}, u32[]{:S(2)}, u32[]{:S(2)}) async-start(bf16[64,3,4096]{2,1,0:T(4,128)(2,1)} %reshape.365), calls=%async_computation.4 | async-start | bytes 4194304 | tf_op jit(solution)/shard_map/all_to_all | solution.py:105
  303.8 100.4 %copy-start.9 = (f32[16,8]{1,0:T(8,128)}, f32[16,8]{1,0:T(8,128)S(1)}, u32[]{:S(2)}) copy-start(f32[16,8]{1,0:T(8,128)S(1)} %copy.88) | copy-start | bytes 1540
  304.0 100.3 %copy-start.13 = (pred[16,8]{1,0:T(8,128)(4,1)}, pred[16,8]{1,0:T(8,128)(4,1)S(1)}, u32[]{:S(2)}) copy-start(pred[16,8]{1,0:T(8,128)(4,1)S(1)} %get-tuple-element.148) | copy-start | bytes 388
  304.0 100.3 %copy-start.15 = (pred[16,8]{1,0:T(8,128)(4,1)}, pred[16,8]{1,0:T(8,128)(4,1)S(1)}, u32[]{:S(2)}) copy-start(pred[16,8]{1,0:T(8,128)(4,1)S(1)} %get-tuple-element.149) | copy-start | bytes 388
  414.1 105.0 %all-to-all-start.5 = ((bf16[64,3,4096]{2,1,0:T(4,128)(2,1)}), bf16[64,3,4096]{2,1,0:T(4,128)(2,1)S(1)}, u32[]{:S(2)}, u32[]{:S(2)}) async-start(bf16[64,3,4096]{2,1,0:T(4,128)(2,1)} %select_select_fusion), calls=%async_computation.6 | async-start | bytes 4194304 | tf_op jit(solution)/shard_map/all_to_all | solution.py:129
  563.2 86.1 %all-to-all-start.7 = ((bf16[64,2,6144]{2,1,0:T(2,128)(2,1)}), bf16[64,2,6144]{2,1,0:T(2,128)(2,1)}, u32[]{:S(2)}, u32[]{:S(2)}) async-start(bf16[64,2,6144]{2,1,0:T(2,128)(2,1)} %reshape.476), calls=%async_computation.8 | async-start | bytes 3145728 | tf_op jit(solution)/shard_map/all_to_all | solution.py:173
  649.3 24.8 %all-to-all-start.6 = ((bf16[64,3,192]{2,1,0:T(4,128)(2,1)}), bf16[64,3,192]{2,1,0:T(4,128)(2,1)S(1)}, u32[]{:S(2)}, u32[]{:S(2)}) async-start(bf16[64,3,192]{2,1,0:T(4,128)(2,1)} %reshape.369), calls=%async_computation.7 | async-start | bytes 262144 | tf_op jit(solution)/shard_map/all_to_all | solution.py:150
  674.1 16.6 %copy-start.10 = (f32[16,8]{1,0:T(8,128)S(1)}, f32[16,8]{1,0:T(8,128)}, u32[]{:S(2)}) copy-start(f32[16,8]{1,0:T(8,128)} %copy-done.9) | copy-start | bytes 1540
  674.1 16.6 %copy-start.14 = (pred[16,8]{1,0:T(8,128)(4,1)S(1)}, pred[16,8]{1,0:T(8,128)(4,1)}, u32[]{:S(2)}) copy-start(pred[16,8]{1,0:T(8,128)(4,1)} %copy-done.13) | copy-start | bytes 388
  674.1 16.6 %copy-start.16 = (pred[16,8]{1,0:T(8,128)(4,1)S(1)}, pred[16,8]{1,0:T(8,128)(4,1)}, u32[]{:S(2)}) copy-start(pred[16,8]{1,0:T(8,128)(4,1)} %copy-done.15) | copy-start | bytes 388
  674.1 113.0 %all-to-all-start.8 = ((bf16[64,192,64]{1,2,0:T(8,128)(2,1)}), bf16[64,192,64]{1,2,0:T(8,128)(2,1)}, u32[]{:S(2)}, u32[]{:S(2)}) async-start(bf16[64,192,64]{1,2,0:T(8,128)(2,1)} %copy.107), calls=%async_computation.9 | async-start | bytes 4194304 | tf_op jit(solution)/shard_map/all_to_all | solution.py:177
  689.6 112.1 %reduce-scatter.2.cloned.1.call-start = ((), (), s32[]{:S(2)}) async-start(), calls=%async_computation.10 | async-start | bytes 147456 | tf_op jit(solution)/shard_map/reduce_scatter | solution.py:118
  791.2 10.5 %copy-start.1 = (bf16[16,8,192]{2,1,0:T(8,128)(2,1)S(1)}, bf16[16,8,192]{2,1,0:T(8,128)(2,1)}, u32[]{:S(2)}) copy-start(bf16[16,8,192]{2,1,0:T(8,128)(2,1)} %param.14) | copy-start | bytes 147460
  (13 other events, 56.0 us)
Sparse Core Ops, SparseCore 0:
  693.8 39.6 reduce-scatter.1
where the time goes:
time: 819 us; the launch traced here: 809 us
  waiting for transfers between devices  506 us (62%)
  starting transfers between devices  95.4 us (12%)
  local copies, waits for them, and re-layouts  89.6 us (11%)
  other arithmetic  63 us (8%)
  blocking collectives  28.1 us (3%)
  between operations  15.8 us (2%)
  matrix products  11.6 us (1%)
    all_to_all x1, waiting for transfers between devices, on_device(): lax.all_to_all(grad_sent, 'expert', split_axis=0, concat_axis=0, tiled=True)  97.6 us
    all_to_all x1, waiting for transfers between devices, on_device(): lax.all_to_all(outgoing, 'expert', split_axis=0, concat_axis=2, tiled=True)  95.2 us
    all_to_all x1, waiting for transfers between devices, on_device(): lax.all_to_all(partial_value.astype(jnp.bfloat16).reshape(n_dev, capacity...  83.6 us
    all_to_all x1, waiting for transfers between devices, on_device(): lax.all_to_all(homeward, 'expert', split_axis=0, concat_axis=2, tiled=True)  77.6 us
    all_to_all x1, waiting for transfers between devices, on_device(): lax.all_to_all(copy_grad[None], 'expert', split_axis=2, concat_axis=0, ti...  70 us
    all_to_all x1, waiting for transfers between devices, on_device(): lax.all_to_all(local_w[None], 'expert', split_axis=2, concat_axis=0, tile...  68.4 us
    unnamed x2, other arithmetic  48.5 us
    unnamed x82, local copies, waits for them, and re-layouts  44.1 us
  transfers between devices with their start and end apart: 10, of which 8 were waited for; matrix products, arithmetic and copies ran while one was open for 8% of the time, Pallas kernels for 0%

commit v1 on v0

v1 whole, which is shorter than its diff:
```python
import jax
import jax.numpy as jnp
from jax import lax
from jax.experimental import pallas as pl
from jax.experimental.pallas import tpu as pltpu
from jax.sharding import PartitionSpec as P

CAP = 3
SLOTS = 2 * CAP
NY = 4
BF = jnp.bfloat16
F32 = jnp.float32
VM = pl.BlockSpec(memory_space=pltpu.VMEM)
SM = pl.BlockSpec(memory_space=pltpu.SMEM)


def call(kernel, outs, specs, flops=0, moved=1 << 20):
    return pl.pallas_call(
        kernel,
        out_shape=outs,
        in_specs=specs,
        out_specs=jax.tree.map(lambda _: VM, outs),
        compiler_params=pltpu.CompilerParams(vmem_limit_bytes=40 << 20),
        cost_estimate=pl.CostEstimate(flops=flops, bytes_accessed=moved, transcendentals=0),
    )


def dot(a, b, ca, cb):
    return lax.dot_general(a, b, (((ca,), (cb,)), ((), ())), preferred_element_type=F32)


def shape(dims, dtype=BF):
    return jax.ShapeDtypeStruct(dims, dtype)


def send(value, step, other):
    pairs = [(i, ((i // 2 + step) % NY) * 2 + ((i % 2) ^ other)) for i in range(2 * NY)]
    return lax.ppermute(value, "dp", pairs)


def peer_column(here, step, other, width):
    peer = lax.rem(here // 2 + step, NY) * 2 + (lax.rem(here, 2) + other) % 2
    return pl.multiple_of(peer * width, width)


def cut_weights(here_ref, w_ref, *outs):
    width = outs[0].shape[1]
    here = here_ref[0]
    for step in range(NY):
        for other in range(2):
            at = peer_column(here, step, other, width)
            outs[2 * step + other][...] = w_ref[:, pl.ds(at, width)]


def join_gradient(here_ref, *refs):
    parts, out_ref = refs[:-1], refs[-1]
    width = parts[0].shape[1]
    here = here_ref[0]
    for step in range(NY):
        for other in range(2):
            at = peer_column(here, (NY - step) % NY, other, width)
            out_ref[:, pl.ds(at, width)] = parts[2 * step + other][...]


def dispatch(
    id_row_ref, id_col_ref, pick_row_ref, pick_col_ref, place_ref, place_t_ref, cap_ref,
    act_ref, cot_ref, gate_ref, sent_ref, slot_ref,
):
    n_dev = cap_ref.shape[0]
    rows, hidden = act_ref.shape
    toks, feats = cot_ref.shape
    top = rows // toks
    id_row, id_col = id_row_ref[...], id_col_ref[...]
    match = (place_ref[:, 0:1] == id_row).astype(jnp.int32)
    has = jnp.sum(match, axis=0, keepdims=True)
    host = jnp.sum(match * place_ref[:, 1:2], axis=0, keepdims=True)
    copy_row = (has > 0) & (pick_row_ref[...] == 1)
    dest_row = jnp.where(copy_row, host, id_row)
    match_t = (place_t_ref[0:1, :] == id_col).astype(jnp.int32)
    has_t = jnp.sum(match_t, axis=1, keepdims=True)
    host_t = jnp.sum(match_t * place_t_ref[1:2, :], axis=1, keepdims=True)
    dest_col = jnp.where((has_t > 0) & (pick_col_ref[...] == 1), host_t, id_col)
    before = lax.broadcasted_iota(jnp.int32, (rows, rows), 0) < lax.broadcasted_iota(
        jnp.int32, (rows, rows), 1
    )
    same = (dest_col == dest_row) & before
    rank = jnp.sum(same.astype(jnp.int32), axis=0, keepdims=True)
    at_dest = lax.broadcasted_iota(jnp.int32, (n_dev, rows), 0) == dest_row
    limit = jnp.sum(jnp.where(at_dest, cap_ref[...], 0), axis=0, keepdims=True)
    place = (jnp.where(copy_row, CAP, 0) + rank) * n_dev + id_row
    slot = jnp.where(rank < limit, place, -1)
    slot_ref[...] = slot
    pick = lax.broadcasted_iota(jnp.int32, (SLOTS * n_dev, rows), 0) == slot
    pick = pick.astype(F32).astype(BF)
    act_s = dot(pick, act_ref[...], 1, 0)
    owner = lax.broadcasted_iota(jnp.int32, (rows, toks), 0) // top == lax.broadcasted_iota(
        jnp.int32, (rows, toks), 1
    )
    cot = dot(owner.astype(F32).astype(BF), cot_ref[...], 1, 0)
    grad = (gate_ref[...] * cot).astype(BF)
    grad_s = dot(pick, grad, 1, 0)
    base = SLOTS * feats
    for j in range(SLOTS):
        part = slice(j * n_dev, (j + 1) * n_dev)
        sent_ref[:, j * feats : (j + 1) * feats] = grad_s[part].astype(BF)
        sent_ref[:, base + j * hidden : base + (j + 1) * hidden] = act_s[part].astype(BF)


def backward(got_ref, *refs):
    w_refs = refs[: 2 * NY]
    act_ref, grad_ref, mine_ref, theirs_ref = refs[2 * NY :]
    n_dev = got_ref.shape[0]
    feats, hidden = grad_ref.shape[1], act_ref.shape[0]
    base = SLOTS * feats
    acts = []
    for j in range(SLOTS):
        part = slice(j * n_dev, (j + 1) * n_dev)
        grad_ref[part, :] = got_ref[:, j * feats : (j + 1) * feats]
        acts.append(got_ref[:, base + j * hidden : base + (j + 1) * hidden].astype(F32))
    act_ref[...] = jnp.concatenate(acts, axis=0).T.astype(BF)
    grad = grad_ref[...]
    for step in range(NY):
        mine_ref[step] = dot(w_refs[2 * step][...], grad, 1, 1).astype(BF)
        theirs_ref[step] = dot(w_refs[2 * step + 1][...], grad, 1, 1).astype(BF)


def add_cores(mine_ref, theirs_ref, *outs):
    for step in range(NY):
        outs[step][...] = (mine_ref[step].astype(F32) + theirs_ref[step].astype(F32)).astype(BF)


def forward(near_ref, far_ref, *refs):
    w_refs = refs[: 2 * NY]
    backs = refs[2 * NY : 3 * NY]
    sent_ref = refs[-1]
    n_dev = sent_ref.shape[0]
    feats = w_refs[0].shape[1]
    hidden = near_ref.shape[1]
    total = None
    for step in range(NY):
        for other, acts in enumerate((near_ref, far_ref)):
            part = dot(acts[step], w_refs[2 * step + other][...], 0, 0)
            total = part if total is None else total + part
    back = backs[0][...].astype(F32)
    for step in range(1, NY):
        back = back + backs[step][...].astype(F32)
    back = back.T.astype(BF)
    base = SLOTS * feats
    for j in range(SLOTS):
        part = slice(j * n_dev, (j + 1) * n_dev)
        sent_ref[:, j * feats : (j + 1) * feats] = total[part].astype(BF)
        sent_ref[:, base + j * hidden : base + (j + 1) * hidden] = back[part]


def weights_back(near_ref, far_ref, grad_ref, *outs):
    grad = grad_ref[...]
    for step in range(NY):
        outs[2 * step][...] = dot(near_ref[step], grad, 1, 0).astype(BF)
        outs[2 * step + 1][...] = dot(far_ref[step], grad, 1, 0).astype(BF)


def collect(got_ref, slot_ref, act_ref, gate_ref, mixed_ref, back_ref, gate_out_ref):
    n_dev = got_ref.shape[0]
    rows, hidden = act_ref.shape
    toks, feats = mixed_ref.shape
    base = SLOTS * feats
    pick = lax.broadcasted_iota(jnp.int32, (rows, SLOTS * n_dev), 1) == slot_ref[...]
    pick = pick.astype(F32).astype(BF)
    outs = jnp.concatenate(
        [got_ref[:, j * feats : (j + 1) * feats] for j in range(SLOTS)], axis=0
    )
    backs = jnp.concatenate(
        [got_ref[:, base + j * hidden : base + (j + 1) * hidden] for j in range(SLOTS)], axis=0
    )
    gate = gate_ref[...]
    row_out = dot(pick, outs, 1, 0) * gate
    mixed_ref[...] = jnp.sum(row_out.reshape(toks, rows // toks, feats), axis=1).astype(BF)
    back = dot(pick, backs, 1, 0)
    back_ref[...] = back.astype(BF)
    gate_out_ref[...] = jnp.sum(back * act_ref[...].astype(F32), axis=1, keepdims=True) / gate


def on_device(acts, w_down, gates, cotangent, expert_ids, replica_pick, placement, group_cap):
    n_dev = lax.axis_size("expert")
    toks, top, hidden = acts.shape
    feats = cotangent.shape[1]
    rows, slots = toks * top, SLOTS * n_dev
    here = lax.axis_index("dp").astype(jnp.int32).reshape(1)
    flat_act = acts.reshape(rows, hidden)
    gate_col = gates.reshape(rows, 1)
    ids, picks = expert_ids.astype(jnp.int32), replica_pick.astype(jnp.int32)

    cuts = call(cut_weights, [shape((hidden, feats))] * (2 * NY), [SM, VM], moved=3 << 20)(
        here, w_down[0]
    )
    weights = [None] * (2 * NY)
    for step in range(NY):
        for other in range(2):
            piece = cuts[2 * step + other]
            if step or other:
                piece = send(piece, step, other)
            weights[2 * ((NY - step) % NY) + other] = piece

    width = SLOTS * (feats + hidden)
    sent, slot_row = call(
        dispatch, [shape((n_dev, width)), shape((1, rows), jnp.int32)], [VM] * 10
    )(
        ids.reshape(1, rows), ids.reshape(rows, 1), picks.reshape(1, rows), picks.reshape(rows, 1),
        placement, placement.T, group_cap.reshape(n_dev, 1), flat_act, cotangent, gate_col,
    )
    got = lax.all_to_all(sent, "expert", 0, 0, tiled=True)

    block = shape((hidden, slots))
    flops = 2 * slots * feats * hidden * 2 * NY
    own_act, grad, mine, theirs = call(
        backward,
        [block, shape((slots, feats)), shape((NY, hidden, slots)), shape((NY, hidden, slots))],
        [VM] * (1 + 2 * NY),
        flops=flops,
    )(got, *weights)
    theirs = send(theirs, 0, 1)
    near = jnp.stack([own_act] + [send(own_act, NY - step, 0) for step in range(1, NY)])
    sums = call(add_cores, [block] * NY, [VM, VM])(mine, theirs)
    far = send(near, 0, 1)
    backs = [sums[0]] + [send(sums[step], step, 0) for step in range(1, NY)]
    returned = call(forward, shape((n_dev, width)), [VM] * (2 + 3 * NY), flops=flops)(
        near, far, *weights, *backs
    )
    home = lax.all_to_all(returned, "expert", 0, 0, tiled=True)

    pieces = call(weights_back, [shape((hidden, feats))] * (2 * NY), [VM] * 3, flops=flops)(
        near, far, grad
    )
    joined = []
    for step in range(NY):
        for other in range(2):
            piece = pieces[2 * step + other]
            joined.append(send(piece, step, other) if step or other else piece)
    weight_grad = call(
        join_gradient, shape((hidden, 2 * NY * feats)), [SM] + [VM] * (2 * NY), moved=3 << 20
    )(here, *joined)

    combined, back_rows, gate_part = call(
        collect,
        [shape((toks, feats)), shape((rows, hidden)), shape((rows, 1), F32)],
        [VM] * 4,
    )(home, slot_row.reshape(rows, 1), flat_act, gate_col)
    gate_grad = lax.psum(gate_part.reshape(toks, top), "dp")
    return combined, back_rows.reshape(toks, top, hidden), weight_grad[None], gate_grad


def solution(mesh):
    return jax.shard_map(
        on_device,
        mesh=mesh,
        in_specs=(
            P("expert", None, "dp"),
            P("expert", "dp", None),
            P("expert", None),
            P("expert", "dp"),
            P("expert", None),
            P("expert", None),
            P(),
            P(),
        ),
        out_specs=(
            P("expert", "dp"),
            P("expert", None, "dp"),
            P("expert", "dp", None),
            P("expert", None),
        ),
        check_vma=False,
    )
```

time: 819 us -> 170 us (0.21); the launches traced: 809 us -> 168 us
  waiting for transfers between devices: 506 us -> 26.3 us
  local copies, waits for them, and re-layouts: 89.6 us -> 18.1 us
  other arithmetic: 63 us -> 2.26 us
  between operations: 15.8 us -> 1.13 us
  blocking collectives: 28.1 us -> 15.3 us
  matrix products: 11.6 us -> 0 us
    all_to_all x9 -> x2, waiting for transfers between devices: 506 us -> 10.5 us  [the longest x1 10.5 us: on_device(): got = lax.all_to_all(sent, 'expert', 0, 0, tiled=True)]
    ppermute x0 -> x22, starting transfers between devices: none -> 68.1 us  [send(): return lax.ppermute(value, 'dp', pairs)]
    all_to_all x9 -> x2, starting transfers between devices: 95.3 us -> 30.2 us  [the longest x1 19 us: on_device(): got = lax.all_to_all(sent, 'expert', 0, 0, tiled=True)]
    unnamed x2 -> x0, other arithmetic: 48.5 us -> none
    unnamed x82 -> x25, local copies, waits for them, and re-layouts: 44.1 us -> 16.2 us
    ppermute x0 -> x22, waiting for transfers between devices: none -> 15.8 us  [send(): return lax.ppermute(value, 'dp', pairs)]
    all_gather x1 -> x0, blocking collectives: 13.3 us -> none  [on_device(): cotangent_full = lax.all_gather(cotangent, 'dp', axis=1, tiled=True)]
    dot_general x5 -> x0, matrix products: 11.6 us -> none  [the longest x1 5.12 us: on_device(): lax.dot_general(own_in, grad_in, (((0,), (0,)), ((), ())), preferred_elem...]
  transfers between devices with their start and end apart: 10 -> 24, of which waited for: 8 -> 7; matrix products, arithmetic and copies ran while one was open for 8% -> 2% of each run, Pallas kernels for 0% -> 2%
where the time goes in v1:
time: 170 us; the launch traced here: 168 us
  starting transfers between devices  98.3 us (58%)
  waiting for transfers between devices  26.3 us (15%)
  local copies, waits for them, and re-layouts  18.1 us (11%)
  blocking collectives  15.3 us (9%)
  Pallas kernels  7.03 us (4%)
  other arithmetic  2.26 us (1%)
    ppermute x22, starting transfers between devices, send(): return lax.ppermute(value, 'dp', pairs)  68.1 us
    all_to_all x1, starting transfers between devices, on_device(): got = lax.all_to_all(sent, 'expert', 0, 0, tiled=True)  19 us
    unnamed x25, local copies, waits for them, and re-layouts  16.2 us
    ppermute x22, waiting for transfers between devices, send(): return lax.ppermute(value, 'dp', pairs)  15.8 us
    psum x1, blocking collectives, on_device(): gate_grad = lax.psum(gate_part.reshape(toks, top), 'dp')  15.3 us
    all_to_all x1, starting transfers between devices, on_device(): home = lax.all_to_all(returned, 'expert', 0, 0, tiled=True)  11.3 us
    all_to_all x1, waiting for transfers between devices, on_device(): got = lax.all_to_all(sent, 'expert', 0, 0, tiled=True)  10.5 us
  transfers between devices with their start and end apart: 24, of which 7 were waited for; matrix products, arithmetic and copies ran while one was open for 2% of the time, Pallas kernels for 2%

profile of v1, /device:TPU:6, one launch (start us, length us, event | category | flops | bytes accessed | tf_op | source)
XLA Modules:
  0.0 168.4 jit_solution(8675650626662789722)
XLA Ops:
  10.5 19.0 %all-to-all-start = ((bf16[64,2,2112]{2,1,0:T(2,128)(2,1)}), bf16[64,2,2112]{2,1,0:T(2,128)(2,1)}, u32[]{:S(2)}, u32[]{:S(2)}) async-start(bf16[64,2,2112]{2,1,0:T(2,128)(2,1)} %reshape.60), calls=%async_computation | async-start | bytes 1114112 | tf_op jit(solution)/shard_map/all_to_all | solution.py:211
  30.4 1.9 %collective-permute-start = (bf16[192,512]{1,0:T(8,128)(2,1)S(1)}, bf16[192,512]{1,0:T(8,128)(2,1)S(1)}, u32[]{:S(2)}, u32[]{:S(2)}) collective-permute-start(bf16[192,512]{1,0:T(8,128)(2,1)S(1)} %get-tuple-element.35), channel_id=1, source_target_pairs={{0,64},{64,0},{128,192},{192,128},{256,320},{320,256},{384,448},{4... | collective-permute-start | bytes 589832 | tf_op jit(solution)/shard_map/ppermute | solution.py:38
  32.3 4.9 %collective-permute-start.1 = (bf16[192,512]{1,0:T(8,128)(2,1)S(1)}, bf16[192,512]{1,0:T(8,128)(2,1)S(1)}, u32[]{:S(2)}, u32[]{:S(2)}) collective-permute-start(bf16[192,512]{1,0:T(8,128)(2,1)S(1)} %get-tuple-element.36), channel_id=1, source_target_pairs={{0,384},{64,448},{128,0},{192,64},{256,128},{320,192},{384,256},{4... | collective-permute-start | bytes 589832 | tf_op jit(solution)/shard_map/ppermute | solution.py:38
  37.2 2.5 %collective-permute-start.2 = (bf16[192,512]{1,0:T(8,128)(2,1)}, bf16[192,512]{1,0:T(8,128)(2,1)S(1)}, u32[]{:S(2)}, u32[]{:S(2)}) collective-permute-start(bf16[192,512]{1,0:T(8,128)(2,1)} %get-tuple-element.37), channel_id=1, source_target_pairs={{0,448},{64,384},{128,64},{192,0},{256,192},{320,128},{384,320},{4... | collective-permute-start | bytes 589832 | tf_op jit(solution)/shard_map/ppermute | solution.py:38
  39.7 2.2 %collective-permute-start.3 = (bf16[192,512]{1,0:T(8,128)(2,1)}, bf16[192,512]{1,0:T(8,128)(2,1)S(1)}, u32[]{:S(2)}, u32[]{:S(2)}) collective-permute-start(bf16[192,512]{1,0:T(8,128)(2,1)} %get-tuple-element.38), channel_id=1, source_target_pairs={{0,256},{64,320},{128,384},{192,448},{256,0},{320,64},{384,128},{4... | collective-permute-start | bytes 589832 | tf_op jit(solution)/shard_map/ppermute | solution.py:38
  41.9 4.7 %collective-permute-start.4 = (bf16[192,512]{1,0:T(8,128)(2,1)S(1)}, bf16[192,512]{1,0:T(8,128)(2,1)S(1)}, u32[]{:S(2)}, u32[]{:S(2)}) collective-permute-start(bf16[192,512]{1,0:T(8,128)(2,1)S(1)} %get-tuple-element.39), channel_id=1, source_target_pairs={{0,320},{64,256},{128,448},{192,384},{256,64},{320,0},{384,192},{4... | collective-permute-start | bytes 589832 | tf_op jit(solution)/shard_map/ppermute | solution.py:38
  46.7 3.2 %collective-permute-start.5 = (bf16[192,512]{1,0:T(8,128)(2,1)S(1)}, bf16[192,512]{1,0:T(8,128)(2,1)S(1)}, u32[]{:S(2)}, u32[]{:S(2)}) collective-permute-start(bf16[192,512]{1,0:T(8,128)(2,1)S(1)} %get-tuple-element.40), channel_id=1, source_target_pairs={{0,128},{64,192},{128,256},{192,320},{256,384},{320,448},{384,0},{... | collective-permute-start | bytes 589832 | tf_op jit(solution)/shard_map/ppermute | solution.py:38
  49.9 2.0 %collective-permute-start.6 = (bf16[192,512]{1,0:T(8,128)(2,1)S(1)}, bf16[192,512]{1,0:T(8,128)(2,1)S(1)}, u32[]{:S(2)}, u32[]{:S(2)}) collective-permute-start(bf16[192,512]{1,0:T(8,128)(2,1)S(1)} %get-tuple-element.41), channel_id=1, source_target_pairs={{0,192},{64,128},{128,320},{192,256},{256,448},{320,384},{384,64},... | collective-permute-start | bytes 589832 | tf_op jit(solution)/shard_map/ppermute | solution.py:38
  51.9 10.5 %all-to-all-done = bf16[64,2,2112]{2,1,0:T(2,128)(2,1)} async-done(((bf16[64,2,2112]{2,1,0:T(2,128)(2,1)}), bf16[64,2,2112]{2,1,0:T(2,128)(2,1)}, u32[]{:S(2)}, u32[]{:S(2)}) %all-to-all-start) | async-done | bytes 540704 | tf_op jit(solution)/shard_map/all_to_all | solution.py:211
  62.4 3.9 %reshape.61 = bf16[64,1,4224]{2,1,0:T(2,128)(2,1)S(1)} reshape(bf16[64,2,2112]{2,1,0:T(2,128)(2,1)} %all-to-all-done) | data formatting | bytes 1081344
  67.6 3.5 %collective-permute-start.9 = (bf16[192,384]{1,0:T(8,128)(2,1)S(1)}, bf16[192,384]{1,0:T(8,128)(2,1)S(1)}, u32[]{:S(2)}, u32[]{:S(2)}) collective-permute-start(bf16[192,384]{1,0:T(8,128)(2,1)S(1)} %get-tuple-element.42), channel_id=1, source_target_pairs={{0,128},{64,192},{128,256},{192,320},{256,384},{320,448},{384,0},{... | collective-permute-start | bytes 442376 | tf_op jit(solution)/shard_map/ppermute | solution.py:38
  71.1 4.8 %collective-permute-start.8 = (bf16[192,384]{1,0:T(8,128)(2,1)S(1)}, bf16[192,384]{1,0:T(8,128)(2,1)S(1)}, u32[]{:S(2)}, u32[]{:S(2)}) collective-permute-start(bf16[192,384]{1,0:T(8,128)(2,1)S(1)} %get-tuple-element.42), channel_id=1, source_target_pairs={{0,256},{64,320},{128,384},{192,448},{256,0},{320,64},{384,128},{4... | collective-permute-start | bytes 442376 | tf_op jit(solution)/shard_map/ppermute | solution.py:38
  75.9 3.3 %collective-permute-start.7 = (bf16[192,384]{1,0:T(8,128)(2,1)S(1)}, bf16[192,384]{1,0:T(8,128)(2,1)S(1)}, u32[]{:S(2)}, u32[]{:S(2)}) collective-permute-start(bf16[192,384]{1,0:T(8,128)(2,1)S(1)} %get-tuple-element.42), channel_id=1, source_target_pairs={{0,384},{64,448},{128,0},{192,64},{256,128},{320,192},{384,256},{4... | collective-permute-start | bytes 442376 | tf_op jit(solution)/shard_map/ppermute | solution.py:38
  79.1 1.9 %collective-permute-start.11 = (bf16[4,192,384]{2,1,0:T(8,128)(2,1)S(1)}, bf16[4,192,384]{2,1,0:T(8,128)(2,1)S(1)}, u32[]{:S(2)}, u32[]{:S(2)}) collective-permute-start(bf16[4,192,384]{2,1,0:T(8,128)(2,1)S(1)} %get-tuple-element.44), channel_id=1, source_target_pairs={{0,64},{64,0},{128,192},{192,128},{256,320},{320,256},{384,448},{4... | collective-permute-start | bytes 1769480 | tf_op jit(solution)/shard_map/ppermute | solution.py:38
  83.0 1.9 %collective-permute-start.10 = (bf16[4,192,384]{2,1,0:T(8,128)(2,1)S(1)}, bf16[4,192,384]{2,1,0:T(8,128)(2,1)S(1)}, u32[]{:S(2)}, u32[]{:S(2)}) collective-permute-start(bf16[4,192,384]{2,1,0:T(8,128)(2,1)S(1)} %pad_maximum_fusion.near_ref), channel_id=1, source_target_pairs={{0,64},{64,0},{128,192},{192,128},{256,320},{320,256},{384,448},{4... | collective-permute-start | bytes 1769480 | tf_op jit(solution)/shard_map/ppermute | solution.py:38
  85.1 1.9 %collective-permute-start.12 = (bf16[192,384]{1,0:T(8,128)(2,1)S(1)}, bf16[192,384]{1,0:T(8,128)(2,1)S(1)}, u32[]{:S(2)}, u32[]{:S(2)}) collective-permute-start(bf16[192,384]{1,0:T(8,128)(2,1)S(1)} %get-tuple-element.46), channel_id=1, source_target_pairs={{0,128},{64,192},{128,256},{192,320},{256,384},{320,448},{384,0},{... | collective-permute-start | bytes 442376 | tf_op jit(solution)/shard_map/ppermute | solution.py:38
  87.0 5.9 %collective-permute-start.13 = (bf16[192,384]{1,0:T(8,128)(2,1)S(1)}, bf16[192,384]{1,0:T(8,128)(2,1)S(1)}, u32[]{:S(2)}, u32[]{:S(2)}) collective-permute-start(bf16[192,384]{1,0:T(8,128)(2,1)S(1)} %get-tuple-element.47), channel_id=1, source_target_pairs={{0,256},{64,320},{128,384},{192,448},{256,0},{320,64},{384,128},{4... | collective-permute-start | bytes 442376 | tf_op jit(solution)/shard_map/ppermute | solution.py:38
  93.0 1.9 %collective-permute-start.14 = (bf16[192,384]{1,0:T(8,128)(2,1)S(1)}, bf16[192,384]{1,0:T(8,128)(2,1)S(1)}, u32[]{:S(2)}, u32[]{:S(2)}) collective-permute-start(bf16[192,384]{1,0:T(8,128)(2,1)S(1)} %get-tuple-element.48), channel_id=1, source_target_pairs={{0,384},{64,448},{128,0},{192,64},{256,128},{320,192},{384,256},{4... | collective-permute-start | bytes 442376 | tf_op jit(solution)/shard_map/ppermute | solution.py:38
  94.9 3.5 %collective-permute-done.13.refs_10_ = bf16[192,384]{1,0:T(8,128)(2,1)S(1)} collective-permute-done((bf16[192,384]{1,0:T(8,128)(2,1)S(1)}, bf16[192,384]{1,0:T(8,128)(2,1)S(1)}, u32[]{:S(2)}, u32[]{:S(2)}) %collective-permute-start.13) | collective-permute-done | bytes 147488 | tf_op jit(solution)/shard_map/ppermute | solution.py:38
  98.4 2.1 %collective-permute-done.14.refs_11_ = bf16[192,384]{1,0:T(8,128)(2,1)S(1)} collective-permute-done((bf16[192,384]{1,0:T(8,128)(2,1)S(1)}, bf16[192,384]{1,0:T(8,128)(2,1)S(1)}, u32[]{:S(2)}, u32[]{:S(2)}) %collective-permute-start.14) | collective-permute-done | bytes 147488 | tf_op jit(solution)/shard_map/ppermute | solution.py:38
  103.8 11.3 %all-to-all-start.1 = ((bf16[64,2,2112]{2,1,0:T(2,128)(2,1)}), bf16[64,2,2112]{2,1,0:T(2,128)(2,1)}, u32[]{:S(2)}, u32[]{:S(2)}) async-start(bf16[64,2,2112]{2,1,0:T(2,128)(2,1)} %reshape.62), calls=%async_computation.1 | async-start | bytes 1114112 | tf_op jit(solution)/shard_map/all_to_all | solution.py:229
  116.1 1.9 %collective-permute-start.15 = (bf16[192,512]{1,0:T(8,128)(2,1)S(1)}, bf16[192,512]{1,0:T(8,128)(2,1)S(1)}, u32[]{:S(2)}, u32[]{:S(2)}) collective-permute-start(bf16[192,512]{1,0:T(8,128)(2,1)S(1)} %get-tuple-element.54), channel_id=1, source_target_pairs={{0,64},{64,0},{128,192},{192,128},{256,320},{320,256},{384,448},{4... | collective-permute-start | bytes 589832 | tf_op jit(solution)/shard_map/ppermute | solution.py:38
  118.0 2.1 %collective-permute-start.16 = (bf16[192,512]{1,0:T(8,128)(2,1)S(1)}, bf16[192,512]{1,0:T(8,128)(2,1)S(1)}, u32[]{:S(2)}, u32[]{:S(2)}) collective-permute-start(bf16[192,512]{1,0:T(8,128)(2,1)S(1)} %get-tuple-element.55), channel_id=1, source_target_pairs={{0,128},{64,192},{128,256},{192,320},{256,384},{320,448},{384,0},{... | collective-permute-start | bytes 589832 | tf_op jit(solution)/shard_map/ppermute | solution.py:38
  120.2 2.2 %collective-permute-start.17 = (bf16[192,512]{1,0:T(8,128)(2,1)S(1)}, bf16[192,512]{1,0:T(8,128)(2,1)S(1)}, u32[]{:S(2)}, u32[]{:S(2)}) collective-permute-start(bf16[192,512]{1,0:T(8,128)(2,1)S(1)} %get-tuple-element.56), channel_id=1, source_target_pairs={{0,192},{64,128},{128,320},{192,256},{256,448},{320,384},{384,64},... | collective-permute-start | bytes 589832 | tf_op jit(solution)/shard_map/ppermute | solution.py:38
  122.4 5.9 %collective-permute-start.18 = (bf16[192,512]{1,0:T(8,128)(2,1)S(1)}, bf16[192,512]{1,0:T(8,128)(2,1)S(1)}, u32[]{:S(2)}, u32[]{:S(2)}) collective-permute-start(bf16[192,512]{1,0:T(8,128)(2,1)S(1)} %get-tuple-element.57), channel_id=1, source_target_pairs={{0,256},{64,320},{128,384},{192,448},{256,0},{320,64},{384,128},{4... | collective-permute-start | bytes 589832 | tf_op jit(solution)/shard_map/ppermute | solution.py:38
  128.3 1.9 %collective-permute-start.19 = (bf16[192,512]{1,0:T(8,128)(2,1)S(1)}, bf16[192,512]{1,0:T(8,128)(2,1)S(1)}, u32[]{:S(2)}, u32[]{:S(2)}) collective-permute-start(bf16[192,512]{1,0:T(8,128)(2,1)S(1)} %get-tuple-element.58), channel_id=1, source_target_pairs={{0,320},{64,256},{128,448},{192,384},{256,64},{320,0},{384,192},{4... | collective-permute-start | bytes 589832 | tf_op jit(solution)/shard_map/ppermute | solution.py:38
  130.2 3.8 %collective-permute-start.20 = (bf16[192,512]{1,0:T(8,128)(2,1)S(1)}, bf16[192,512]{1,0:T(8,128)(2,1)S(1)}, u32[]{:S(2)}, u32[]{:S(2)}) collective-permute-start(bf16[192,512]{1,0:T(8,128)(2,1)S(1)} %get-tuple-element.59), channel_id=1, source_target_pairs={{0,384},{64,448},{128,0},{192,64},{256,128},{320,192},{384,256},{4... | collective-permute-start | bytes 589832 | tf_op jit(solution)/shard_map/ppermute | solution.py:38
  134.1 3.5 %collective-permute-start.21 = (bf16[192,512]{1,0:T(8,128)(2,1)S(1)}, bf16[192,512]{1,0:T(8,128)(2,1)S(1)}, u32[]{:S(2)}, u32[]{:S(2)}) collective-permute-start(bf16[192,512]{1,0:T(8,128)(2,1)S(1)} %get-tuple-element.60), channel_id=1, source_target_pairs={{0,448},{64,384},{128,64},{192,0},{256,192},{320,128},{384,320},{4... | collective-permute-start | bytes 589832 | tf_op jit(solution)/shard_map/ppermute | solution.py:38
  137.7 3.3 %collective-permute-done.19.refs_5_ = bf16[192,512]{1,0:T(8,128)(2,1)S(1)} collective-permute-done((bf16[192,512]{1,0:T(8,128)(2,1)S(1)}, bf16[192,512]{1,0:T(8,128)(2,1)S(1)}, u32[]{:S(2)}, u32[]{:S(2)}) %collective-permute-start.19) | collective-permute-done | bytes 196640 | tf_op jit(solution)/shard_map/ppermute | solution.py:38
  142.2 3.8 %collective-permute-done.21.refs_7_ = bf16[192,512]{1,0:T(8,128)(2,1)S(1)} collective-permute-done((bf16[192,512]{1,0:T(8,128)(2,1)S(1)}, bf16[192,512]{1,0:T(8,128)(2,1)S(1)}, u32[]{:S(2)}, u32[]{:S(2)}) %collective-permute-start.21) | collective-permute-done | bytes 196640 | tf_op jit(solution)/shard_map/ppermute | solution.py:38
  147.3 3.9 %reshape.63 = bf16[64,1,4224]{2,1,0:T(2,128)(2,1)S(1)} reshape(bf16[64,2,2112]{2,1,0:T(2,128)(2,1)} %all-to-all-done.1) | data formatting | bytes 1081344
  152.4 15.3 %psum.7 = f32[16,8]{1,0:T(8,128)S(1)} all-reduce(f32[16,8]{1,0:T(8,128)S(1)} %reshape.55), channel_id=1, replica_groups=mesh['dp'=8,'expert'=64] {'dp'}, use_global_device_ids=true, to_apply=%region_0.0 | all-reduce | flops 128 | bytes 1024 | tf_op jit(solution)/shard_map/psum | solution.py:248
  (63 shorter events, 22.6 us)
Async XLA Ops:
  4.8 0.8 copy-start.1
  5.7 0.7 copy-start.3
  6.4 0.7 copy-start.4
  8.2 21.3 %copy-start = (bf16[1,192,4096]{2,1,0:T(8,128)(2,1)S(1)}, bf16[1,192,4096]{2,1,0:T(8,128)(2,1)}, u32[]{:S(2)}) copy-start(bf16[1,192,4096]{2,1,0:T(8,128)(2,1)} %param.9) | copy-start | bytes 4718596
  10.5 51.9 %all-to-all-start = ((bf16[64,2,2112]{2,1,0:T(2,128)(2,1)}), bf16[64,2,2112]{2,1,0:T(2,128)(2,1)}, u32[]{:S(2)}, u32[]{:S(2)}) async-start(bf16[64,2,2112]{2,1,0:T(2,128)(2,1)} %reshape.60), calls=%async_computation | async-start | bytes 1114112 | tf_op jit(solution)/shard_map/all_to_all | solution.py:211
  30.4 16.3 %collective-permute-start = (bf16[192,512]{1,0:T(8,128)(2,1)S(1)}, bf16[192,512]{1,0:T(8,128)(2,1)S(1)}, u32[]{:S(2)}, u32[]{:S(2)}) collective-permute-start(bf16[192,512]{1,0:T(8,128)(2,1)S(1)} %get-tuple-element.35), channel_id=1, source_target_pairs={{0,64},{64,0},{128,192},{192,128},{256,320},{320,256},{384,448},{4... | collective-permute-start | bytes 589832 | tf_op jit(solution)/shard_map/ppermute | solution.py:38
  32.3 17.6 %collective-permute-start.1 = (bf16[192,512]{1,0:T(8,128)(2,1)S(1)}, bf16[192,512]{1,0:T(8,128)(2,1)S(1)}, u32[]{:S(2)}, u32[]{:S(2)}) collective-permute-start(bf16[192,512]{1,0:T(8,128)(2,1)S(1)} %get-tuple-element.36), channel_id=1, source_target_pairs={{0,384},{64,448},{128,0},{192,64},{256,128},{320,192},{384,256},{4... | collective-permute-start | bytes 589832 | tf_op jit(solution)/shard_map/ppermute | solution.py:38
  37.2 29.1 %collective-permute-start.2 = (bf16[192,512]{1,0:T(8,128)(2,1)}, bf16[192,512]{1,0:T(8,128)(2,1)S(1)}, u32[]{:S(2)}, u32[]{:S(2)}) collective-permute-start(bf16[192,512]{1,0:T(8,128)(2,1)} %get-tuple-element.37), channel_id=1, source_target_pairs={{0,448},{64,384},{128,64},{192,0},{256,192},{320,128},{384,320},{4... | collective-permute-start | bytes 589832 | tf_op jit(solution)/shard_map/ppermute | solution.py:38
  39.7 26.6 %collective-permute-start.3 = (bf16[192,512]{1,0:T(8,128)(2,1)}, bf16[192,512]{1,0:T(8,128)(2,1)S(1)}, u32[]{:S(2)}, u32[]{:S(2)}) collective-permute-start(bf16[192,512]{1,0:T(8,128)(2,1)} %get-tuple-element.38), channel_id=1, source_target_pairs={{0,256},{64,320},{128,384},{192,448},{256,0},{320,64},{384,128},{4... | collective-permute-start | bytes 589832 | tf_op jit(solution)/shard_map/ppermute | solution.py:38
  41.9 24.4 %collective-permute-start.4 = (bf16[192,512]{1,0:T(8,128)(2,1)S(1)}, bf16[192,512]{1,0:T(8,128)(2,1)S(1)}, u32[]{:S(2)}, u32[]{:S(2)}) collective-permute-start(bf16[192,512]{1,0:T(8,128)(2,1)S(1)} %get-tuple-element.39), channel_id=1, source_target_pairs={{0,320},{64,256},{128,448},{192,384},{256,64},{320,0},{384,192},{4... | collective-permute-start | bytes 589832 | tf_op jit(solution)/shard_map/ppermute | solution.py:38
  46.7 19.7 %collective-permute-start.5 = (bf16[192,512]{1,0:T(8,128)(2,1)S(1)}, bf16[192,512]{1,0:T(8,128)(2,1)S(1)}, u32[]{:S(2)}, u32[]{:S(2)}) collective-permute-start(bf16[192,512]{1,0:T(8,128)(2,1)S(1)} %get-tuple-element.40), channel_id=1, source_target_pairs={{0,128},{64,192},{128,256},{192,320},{256,384},{320,448},{384,0},{... | collective-permute-start | bytes 589832 | tf_op jit(solution)/shard_map/ppermute | solution.py:38
  49.9 16.5 %collective-permute-start.6 = (bf16[192,512]{1,0:T(8,128)(2,1)S(1)}, bf16[192,512]{1,0:T(8,128)(2,1)S(1)}, u32[]{:S(2)}, u32[]{:S(2)}) collective-permute-start(bf16[192,512]{1,0:T(8,128)(2,1)S(1)} %get-tuple-element.41), channel_id=1, source_target_pairs={{0,192},{64,128},{128,320},{192,256},{256,448},{320,384},{384,64},... | collective-permute-start | bytes 589832 | tf_op jit(solution)/shard_map/ppermute | solution.py:38
  67.6 17.4 %copy-start.5 = (bf16[384,512]{1,0:T(8,128)(2,1)}, bf16[384,512]{1,0:T(8,128)(2,1)S(1)}, u32[]{:S(2)}) copy-start(bf16[384,512]{1,0:T(8,128)(2,1)S(1)} %get-tuple-element.52.grad_ref) | copy-start | bytes 1179652
  67.6 13.5 %collective-permute-start.9 = (bf16[192,384]{1,0:T(8,128)(2,1)S(1)}, bf16[192,384]{1,0:T(8,128)(2,1)S(1)}, u32[]{:S(2)}, u32[]{:S(2)}) collective-permute-start(bf16[192,384]{1,0:T(8,128)(2,1)S(1)} %get-tuple-element.42), channel_id=1, source_target_pairs={{0,128},{64,192},{128,256},{192,320},{256,384},{320,448},{384,0},{... | collective-permute-start | bytes 442376 | tf_op jit(solution)/shard_map/ppermute | solution.py:38
  71.1 10.0 %collective-permute-start.8 = (bf16[192,384]{1,0:T(8,128)(2,1)S(1)}, bf16[192,384]{1,0:T(8,128)(2,1)S(1)}, u32[]{:S(2)}, u32[]{:S(2)}) collective-permute-start(bf16[192,384]{1,0:T(8,128)(2,1)S(1)} %get-tuple-element.42), channel_id=1, source_target_pairs={{0,256},{64,320},{128,384},{192,448},{256,0},{320,64},{384,128},{4... | collective-permute-start | bytes 442376 | tf_op jit(solution)/shard_map/ppermute | solution.py:38
  75.9 7.0 %collective-permute-start.7 = (bf16[192,384]{1,0:T(8,128)(2,1)S(1)}, bf16[192,384]{1,0:T(8,128)(2,1)S(1)}, u32[]{:S(2)}, u32[]{:S(2)}) collective-permute-start(bf16[192,384]{1,0:T(8,128)(2,1)S(1)} %get-tuple-element.42), channel_id=1, source_target_pairs={{0,384},{64,448},{128,0},{192,64},{256,128},{320,192},{384,256},{4... | collective-permute-start | bytes 442376 | tf_op jit(solution)/shard_map/ppermute | solution.py:38
  79.1 5.8 %collective-permute-start.11 = (bf16[4,192,384]{2,1,0:T(8,128)(2,1)S(1)}, bf16[4,192,384]{2,1,0:T(8,128)(2,1)S(1)}, u32[]{:S(2)}, u32[]{:S(2)}) collective-permute-start(bf16[4,192,384]{2,1,0:T(8,128)(2,1)S(1)} %get-tuple-element.44), channel_id=1, source_target_pairs={{0,64},{64,0},{128,192},{192,128},{256,320},{320,256},{384,448},{4... | collective-permute-start | bytes 1769480 | tf_op jit(solution)/shard_map/ppermute | solution.py:38
  83.0 11.9 %collective-permute-start.10 = (bf16[4,192,384]{2,1,0:T(8,128)(2,1)S(1)}, bf16[4,192,384]{2,1,0:T(8,128)(2,1)S(1)}, u32[]{:S(2)}, u32[]{:S(2)}) collective-permute-start(bf16[4,192,384]{2,1,0:T(8,128)(2,1)S(1)} %pad_maximum_fusion.near_ref), channel_id=1, source_target_pairs={{0,64},{64,0},{128,192},{192,128},{256,320},{320,256},{384,448},{4... | collective-permute-start | bytes 1769480 | tf_op jit(solution)/shard_map/ppermute | solution.py:38
  85.1 9.8 %collective-permute-start.12 = (bf16[192,384]{1,0:T(8,128)(2,1)S(1)}, bf16[192,384]{1,0:T(8,128)(2,1)S(1)}, u32[]{:S(2)}, u32[]{:S(2)}) collective-permute-start(bf16[192,384]{1,0:T(8,128)(2,1)S(1)} %get-tuple-element.46), channel_id=1, source_target_pairs={{0,128},{64,192},{128,256},{192,320},{256,384},{320,448},{384,0},{... | collective-permute-start | bytes 442376 | tf_op jit(solution)/shard_map/ppermute | solution.py:38
  87.0 11.4 %collective-permute-start.13 = (bf16[192,384]{1,0:T(8,128)(2,1)S(1)}, bf16[192,384]{1,0:T(8,128)(2,1)S(1)}, u32[]{:S(2)}, u32[]{:S(2)}) collective-permute-start(bf16[192,384]{1,0:T(8,128)(2,1)S(1)} %get-tuple-element.47), channel_id=1, source_target_pairs={{0,256},{64,320},{128,384},{192,448},{256,0},{320,64},{384,128},{4... | collective-permute-start | bytes 442376 | tf_op jit(solution)/shard_map/ppermute | solution.py:38
  93.0 7.6 %collective-permute-start.14 = (bf16[192,384]{1,0:T(8,128)(2,1)S(1)}, bf16[192,384]{1,0:T(8,128)(2,1)S(1)}, u32[]{:S(2)}, u32[]{:S(2)}) collective-permute-start(bf16[192,384]{1,0:T(8,128)(2,1)S(1)} %get-tuple-element.48), channel_id=1, source_target_pairs={{0,384},{64,448},{128,0},{192,64},{256,128},{320,192},{384,256},{4... | collective-permute-start | bytes 442376 | tf_op jit(solution)/shard_map/ppermute | solution.py:38
  102.6 12.5 %copy-start.6 = (bf16[384,512]{1,0:T(8,128)(2,1)S(1)}, bf16[384,512]{1,0:T(8,128)(2,1)}, u32[]{:S(2)}) copy-start(bf16[384,512]{1,0:T(8,128)(2,1)} %copy-done.5) | copy-start | bytes 1179652
  103.8 43.5 %all-to-all-start.1 = ((bf16[64,2,2112]{2,1,0:T(2,128)(2,1)}), bf16[64,2,2112]{2,1,0:T(2,128)(2,1)}, u32[]{:S(2)}, u32[]{:S(2)}) async-start(bf16[64,2,2112]{2,1,0:T(2,128)(2,1)} %reshape.62), calls=%async_computation.1 | async-start | bytes 1114112 | tf_op jit(solution)/shard_map/all_to_all | solution.py:229
  116.1 14.1 %collective-permute-start.15 = (bf16[192,512]{1,0:T(8,128)(2,1)S(1)}, bf16[192,512]{1,0:T(8,128)(2,1)S(1)}, u32[]{:S(2)}, u32[]{:S(2)}) collective-permute-start(bf16[192,512]{1,0:T(8,128)(2,1)S(1)} %get-tuple-element.54), channel_id=1, source_target_pairs={{0,64},{64,0},{128,192},{192,128},{256,320},{320,256},{384,448},{4... | collective-permute-start | bytes 589832 | tf_op jit(solution)/shard_map/ppermute | solution.py:38
  118.0 16.0 %collective-permute-start.16 = (bf16[192,512]{1,0:T(8,128)(2,1)S(1)}, bf16[192,512]{1,0:T(8,128)(2,1)S(1)}, u32[]{:S(2)}, u32[]{:S(2)}) collective-permute-start(bf16[192,512]{1,0:T(8,128)(2,1)S(1)} %get-tuple-element.55), channel_id=1, source_target_pairs={{0,128},{64,192},{128,256},{192,320},{256,384},{320,448},{384,0},{... | collective-permute-start | bytes 589832 | tf_op jit(solution)/shard_map/ppermute | solution.py:38
  120.2 17.5 %collective-permute-start.17 = (bf16[192,512]{1,0:T(8,128)(2,1)S(1)}, bf16[192,512]{1,0:T(8,128)(2,1)S(1)}, u32[]{:S(2)}, u32[]{:S(2)}) collective-permute-start(bf16[192,512]{1,0:T(8,128)(2,1)S(1)} %get-tuple-element.56), channel_id=1, source_target_pairs={{0,192},{64,128},{128,320},{192,256},{256,448},{320,384},{384,64},... | collective-permute-start | bytes 589832 | tf_op jit(solution)/shard_map/ppermute | solution.py:38
  122.4 15.3 %collective-permute-start.18 = (bf16[192,512]{1,0:T(8,128)(2,1)S(1)}, bf16[192,512]{1,0:T(8,128)(2,1)S(1)}, u32[]{:S(2)}, u32[]{:S(2)}) collective-permute-start(bf16[192,512]{1,0:T(8,128)(2,1)S(1)} %get-tuple-element.57), channel_id=1, source_target_pairs={{0,256},{64,320},{128,384},{192,448},{256,0},{320,64},{384,128},{4... | collective-permute-start | bytes 589832 | tf_op jit(solution)/shard_map/ppermute | solution.py:38
  128.3 12.7 %collective-permute-start.19 = (bf16[192,512]{1,0:T(8,128)(2,1)S(1)}, bf16[192,512]{1,0:T(8,128)(2,1)S(1)}, u32[]{:S(2)}, u32[]{:S(2)}) collective-permute-start(bf16[192,512]{1,0:T(8,128)(2,1)S(1)} %get-tuple-element.58), channel_id=1, source_target_pairs={{0,320},{64,256},{128,448},{192,384},{256,64},{320,0},{384,192},{4... | collective-permute-start | bytes 589832 | tf_op jit(solution)/shard_map/ppermute | solution.py:38
  130.2 11.9 %collective-permute-start.20 = (bf16[192,512]{1,0:T(8,128)(2,1)S(1)}, bf16[192,512]{1,0:T(8,128)(2,1)S(1)}, u32[]{:S(2)}, u32[]{:S(2)}) collective-permute-start(bf16[192,512]{1,0:T(8,128)(2,1)S(1)} %get-tuple-element.59), channel_id=1, source_target_pairs={{0,384},{64,448},{128,0},{192,64},{256,128},{320,192},{384,256},{4... | collective-permute-start | bytes 589832 | tf_op jit(solution)/shard_map/ppermute | solution.py:38
  134.1 11.9 %collective-permute-start.21 = (bf16[192,512]{1,0:T(8,128)(2,1)S(1)}, bf16[192,512]{1,0:T(8,128)(2,1)S(1)}, u32[]{:S(2)}, u32[]{:S(2)}) collective-permute-start(bf16[192,512]{1,0:T(8,128)(2,1)S(1)} %get-tuple-element.60), channel_id=1, source_target_pairs={{0,448},{64,384},{128,64},{192,0},{256,192},{320,128},{384,320},{4... | collective-permute-start | bytes 589832 | tf_op jit(solution)/shard_map/ppermute | solution.py:38
  147.3 4.0 %copy-start.2 = (bf16[16,8,192]{2,1,0:T(8,128)(2,1)S(1)}, bf16[16,8,192]{2,1,0:T(8,128)(2,1)}, u32[]{:S(2)}) copy-start(bf16[16,8,192]{2,1,0:T(8,128)(2,1)} %param.8) | copy-start | bytes 147460

commit v2 on v1

v2 whole, which is shorter than its diff:
```python
import jax
import jax.numpy as jnp
from jax import lax
from jax.experimental import pallas as pl
from jax.experimental.pallas import tpu as pltpu
from jax.sharding import PartitionSpec as P

CAP = 3
SLOTS = 2 * CAP
ROWS = 8
NY = 4
EXTRA = 16
BF = jnp.bfloat16
F32 = jnp.float32
VM = pl.BlockSpec(memory_space=pltpu.VMEM)
SM = pl.BlockSpec(memory_space=pltpu.SMEM)


def call(kernel, outs, specs, flops=0, moved=1 << 20, scratch=()):
    return pl.pallas_call(
        kernel,
        out_shape=outs,
        in_specs=specs,
        out_specs=jax.tree.map(lambda _: VM, outs),
        scratch_shapes=list(scratch),
        compiler_params=pltpu.CompilerParams(vmem_limit_bytes=40 << 20),
        cost_estimate=pl.CostEstimate(flops=flops, bytes_accessed=moved, transcendentals=0),
    )


def dot(a, b, ca, cb):
    return lax.dot_general(a, b, (((ca,), (cb,)), ((), ())), preferred_element_type=F32)


def shape(dims, dtype=BF):
    return jax.ShapeDtypeStruct(dims, dtype)


def ones(mask):
    return mask.astype(F32).astype(BF)


def iota(dims, axis):
    return lax.broadcasted_iota(jnp.int32, dims, axis)


def payload_width(feats, hidden):
    return (max(feats + EXTRA, CAP * hidden) + 127) // 128 * 128


def send(value, step, other):
    pairs = [(i, ((i // 2 + step) % NY) * 2 + ((i % 2) ^ other)) for i in range(2 * NY)]
    return lax.ppermute(value, "dp", pairs)


def exchange_y(value):
    groups = [[2 * y + core for y in range(NY)] for core in range(2)]
    return lax.all_to_all(value, "dp", 0, 0, axis_index_groups=groups, tiled=True)


def chip(here, step):
    return lax.rem(here // 2 + step, NY)


def peer_column(here, step, other, width):
    peer = chip(here, step) * 2 + lax.rem(lax.rem(here, 2) + other, 2)
    return pl.multiple_of(peer * width, width)


def cut_weights(here_ref, w_ref, *outs):
    width = outs[0].shape[1]
    here = here_ref[0]
    for step in range(NY):
        for other in range(2):
            at = peer_column(here, step, other, width)
            outs[2 * step + other][...] = w_ref[:, pl.ds(at, width)]


def join_gradient(here_ref, *refs):
    parts, out_ref = refs[:-1], refs[-1]
    width = parts[0].shape[1]
    here = here_ref[0]
    for step in range(NY):
        for other in range(2):
            at = peer_column(here, (NY - step) % NY, other, width)
            out_ref[:, pl.ds(at, width)] = parts[2 * step + other][...]


def column(stored):
    top, toks = stored.shape
    spread = jnp.broadcast_to(stored[None], (toks, top, toks)).reshape(toks * top, toks)
    mine = iota(spread.shape, 0) // top == iota(spread.shape, 1)
    return jnp.sum(jnp.where(mine, spread, jnp.zeros_like(spread)), axis=1, keepdims=True)


def as_row(col):
    n = col.shape[0]
    diagonal = iota((n, n), 0) == iota((n, n), 1)
    return jnp.sum(jnp.where(diagonal, col, jnp.zeros_like(col)), axis=0, keepdims=True)


def split_slot(slot):
    expert, j = slot >> 3, slot & 7
    kind = (j >= CAP).astype(jnp.int32)
    return j - CAP * kind, expert * ROWS + SLOTS + kind


def dispatch(
    ids_ref, picks_ref, place_ref, cap_ref, act_ref, cot_ref, gate_ref, sent_ref, slot_ref, right_ref
):
    n_dev = cap_ref.shape[1]
    rows, hidden = act_ref.shape
    toks, feats = cot_ref.shape
    top = rows // toks
    ids, picks = column(ids_ref[...]), column(picks_ref[...])
    match = (place_ref[0:1, :] == ids).astype(jnp.int32)
    has = jnp.sum(match, axis=1, keepdims=True)
    host = jnp.sum(match * place_ref[1:2, :], axis=1, keepdims=True)
    copied = (has > 0) & (picks == 1)
    dest = jnp.where(copied, host, ids)
    dest_row = as_row(dest)
    earlier = (dest == dest_row) & (iota((rows, rows), 1) < iota((rows, rows), 0))
    rank = jnp.sum(earlier.astype(jnp.int32), axis=1, keepdims=True)
    at_dest = iota((rows, n_dev), 1) == dest
    limit = jnp.sum(jnp.where(at_dest, cap_ref[...], 0), axis=1, keepdims=True)
    slot = jnp.where(rank < limit, ids * ROWS + jnp.where(copied, CAP, 0) + rank, -1)
    slot_ref[...] = slot

    slot_row = as_row(slot)
    rank_row, act_row = split_slot(slot_row)
    q = iota((ROWS * n_dev, rows), 0)
    left = [q == slot_row] + [(q == act_row) & (rank_row == r) for r in range(CAP)]
    owner = ones(iota((rows, toks), 0) // top == iota((rows, toks), 1))
    grad = column(gate_ref[...]) * dot(owner, cot_ref[...], 1, 0)
    right_ref[...] = jnp.zeros_like(right_ref)
    right_ref[:rows, :feats] = grad.astype(BF)
    for r in range(CAP):
        right_ref[(1 + r) * rows : (2 + r) * rows, r * hidden : (r + 1) * hidden] = act_ref[...]
    total = None
    for i, mask in enumerate(left):
        part = dot(ones(mask), right_ref[i * rows : (i + 1) * rows, :], 1, 0)
        total = part if total is None else total + part
    sent_ref[...] = total.astype(BF)


def slot_masks(n_dev, q_axis):
    dims = [SLOTS * n_dev, SLOTS * n_dev]
    dims[q_axis] = ROWS * n_dev
    q, s = iota(dims, q_axis), iota(dims, 1 - q_axis)
    j, source = s // n_dev, lax.rem(s, n_dev)
    kind = (j >= CAP).astype(jnp.int32)
    wide = q == source * ROWS + j
    narrow = q == source * ROWS + SLOTS + kind
    return wide, [narrow & (j - CAP * kind == r) for r in range(CAP)]


def unpack(got_ref, act_ref, grad_ref):
    n_dev = got_ref.shape[0] // ROWS
    feats, hidden = grad_ref.shape[1], act_ref.shape[1]
    wide, _ = slot_masks(n_dev, 1)
    _, narrow = slot_masks(n_dev, 0)
    total = None
    for r in range(CAP):
        part = dot(got_ref[:, r * hidden : (r + 1) * hidden], ones(narrow[r]), 0, 0)
        total = part if total is None else total + part
    for y in range(NY):
        act_ref[y] = total.astype(BF)
    grad_ref[...] = dot(ones(wide), got_ref[:, :feats], 1, 0).astype(BF)


def backward(here_ref, grad_ref, *refs):
    w_refs, (mine_ref, theirs_ref) = refs[:-2], refs[-2:]
    grad = grad_ref[...]
    for step in range(NY):
        at = chip(here_ref[0], step)
        mine_ref[at] = dot(w_refs[2 * step][...], grad, 1, 1).astype(BF)
        theirs_ref[at] = dot(w_refs[2 * step + 1][...], grad, 1, 1).astype(BF)


def add_cores(near_ref, mine_ref, theirs_ref, out_ref):
    hidden, slots = near_ref.shape[1:]
    gate = jnp.zeros((1, slots), F32)
    for y in range(NY):
        both = mine_ref[y].astype(F32) + theirs_ref[y].astype(F32)
        gate = gate + jnp.sum(near_ref[y].astype(F32) * both, axis=0, keepdims=True)
        out_ref[y, :hidden] = both.astype(BF)
    extra = two_parts(gate)
    for y in range(NY):
        out_ref[y, hidden:] = extra


def two_parts(row):
    high = row.astype(BF).astype(F32)
    at = iota((EXTRA, row.shape[1]), 0)
    return jnp.where(at == 0, high, jnp.where(at == 1, row - high, 0.0)).astype(BF)


def forward(here_ref, near_ref, far_ref, back_ref, *refs):
    w_refs, (sent_ref, sum_ref) = refs[:-2], refs[-2:]
    n_dev = sent_ref.shape[0] // ROWS
    feats, hidden = w_refs[0].shape[1], near_ref.shape[1]
    total = None
    for step in range(NY):
        at = chip(here_ref[0], step)
        for other, acts in enumerate((near_ref, far_ref)):
            part = dot(acts[at], w_refs[2 * step + other][...], 0, 0)
            total = part if total is None else total + part
    back = sum(back_ref[y].astype(F32) for y in range(NY))
    gate = jnp.sum(back[hidden:], axis=0, keepdims=True)
    back = back[:hidden].astype(BF)
    wide, narrow = slot_masks(n_dev, 0)
    wide = ones(wide)
    sum_ref[...] = jnp.zeros_like(sum_ref)
    sum_ref[:, :feats] = dot(wide, total.astype(BF), 1, 0)
    sum_ref[:, feats : feats + EXTRA] = dot(wide, two_parts(gate), 1, 1)
    for r in range(CAP):
        sum_ref[:, r * hidden : (r + 1) * hidden] += dot(ones(narrow[r]), back, 1, 1)
    sent_ref[...] = sum_ref[...].astype(BF)


def weights_back(here_ref, near_ref, far_ref, grad_ref, *outs):
    grad = grad_ref[...]
    for step in range(NY):
        at = chip(here_ref[0], step)
        outs[2 * step][...] = dot(near_ref[at], grad, 1, 0).astype(BF)
        outs[2 * step + 1][...] = dot(far_ref[at], grad, 1, 0).astype(BF)


def collect(got_ref, slot_ref, gate_ref, mixed_ref, back_ref, gate_out_ref):
    top, toks = gate_ref.shape
    rows, hidden = back_ref.shape
    feats = mixed_ref.shape[1]
    gate = column(gate_ref[...])
    slot = slot_ref[...]
    rank, act_row = split_slot(slot)
    q = iota((rows, got_ref.shape[0]), 1)
    wide = ones(q == slot)
    row_out = dot(wide, got_ref[:, :feats], 1, 0) * gate
    mixed_ref[...] = jnp.sum(row_out.reshape(toks, top, feats), axis=1).astype(BF)
    back = None
    for r in range(CAP):
        pick = ones((q == act_row) & (rank == r))
        part = dot(pick, got_ref[:, r * hidden : (r + 1) * hidden], 1, 0)
        back = part if back is None else back + part
    back_ref[...] = back.astype(BF)
    extra = dot(wide, got_ref[:, feats:], 1, 0)
    gate_back = jnp.sum(jnp.where(iota(extra.shape, 1) < 2, extra, 0.0), axis=1, keepdims=True) / gate
    at_tok = iota((rows, toks), 0) // top == iota((rows, toks), 1)
    spread = jnp.where(at_tok, gate_back, 0.0)
    gate_out_ref[...] = jnp.sum(spread.reshape(toks, top, toks), axis=0)


def on_device(acts, w_down, gates, cotangent, expert_ids, replica_pick, placement, group_cap):
    n_dev = lax.axis_size("expert")
    toks, top, hidden = acts.shape
    feats = cotangent.shape[1]
    rows, slots = toks * top, SLOTS * n_dev
    width = payload_width(feats, hidden)
    here = lax.axis_index("dp").astype(jnp.int32).reshape(1)
    gates_t = gates.T
    pieces_shape = [shape((hidden, feats))] * (2 * NY)

    cuts = call(cut_weights, pieces_shape, [SM, VM], moved=3 << 20)(here, w_down[0])
    weights = [None] * (2 * NY)
    for step in range(NY):
        for other in range(2):
            piece = cuts[2 * step + other]
            if step or other:
                piece = send(piece, step, other)
            weights[2 * ((NY - step) % NY) + other] = piece

    sent, slot = call(
        dispatch,
        [shape((ROWS * n_dev, width)), shape((rows, 1), jnp.int32)],
        [VM] * 7,
        scratch=[pltpu.VMEM(((1 + CAP) * rows, width), BF)],
    )(
        expert_ids.T, replica_pick.T, placement.T, group_cap.reshape(1, n_dev),
        acts.reshape(rows, hidden), cotangent, gates_t,
    )

    def exchange(value):
        value = value.reshape(n_dev, ROWS, width)
        return lax.all_to_all(value, "expert", 0, 0, tiled=True).reshape(ROWS * n_dev, width)

    got = exchange(sent)
    stack = shape((NY, hidden, slots))
    flops = 2 * slots * feats * hidden * 2 * NY
    near, grad = call(unpack, [stack, shape((slots, feats))], [VM])(got)
    near = exchange_y(near)
    mine, theirs = call(backward, [stack] * 2, [SM] + [VM] * (1 + 2 * NY), flops=flops)(
        here, grad, *weights
    )
    theirs = send(theirs, 0, 1)
    back = call(add_cores, shape((NY, hidden + EXTRA, slots)), [VM] * 3)(near, mine, theirs)
    far = send(near, 0, 1)
    back = exchange_y(back)
    returned = call(
        forward,
        shape((ROWS * n_dev, width)),
        [SM] + [VM] * (3 + 2 * NY),
        flops=flops,
        scratch=[pltpu.VMEM((ROWS * n_dev, width), F32)],
    )(here, near, far, back, *weights)
    home = exchange(returned)

    pieces = call(weights_back, pieces_shape, [SM] + [VM] * 3, flops=flops)(here, near, far, grad)
    joined = []
    for step in range(NY):
        for other in range(2):
            piece = pieces[2 * step + other]
            joined.append(send(piece, step, other) if step or other else piece)
    weight_grad = call(
        join_gradient, shape((hidden, 2 * NY * feats)), [SM] + [VM] * (2 * NY), moved=3 << 20
    )(here, *joined)

    combined, back_rows, gate_part = call(
        collect,
        [shape((toks, feats)), shape((rows, hidden)), shape((top, toks), F32)],
        [VM] * 3,
    )(home, slot, gates_t)
    gate_grad = (gate_part + send(gate_part, 0, 1)).T
    return combined, back_rows.reshape(toks, top, hidden), weight_grad[None], gate_grad


def solution(mesh):
    return jax.shard_map(
        on_device,
        mesh=mesh,
        in_specs=(
            P("expert", None, "dp"),
            P("expert", "dp", None),
            P("expert", None),
            P("expert", "dp"),
            P("expert", None),
            P("expert", None),
            P(),
            P(),
        ),
        out_specs=(
            P("expert", "dp"),
            P("expert", None, "dp"),
            P("expert", "dp", None),
            P("expert", None),
        ),
        check_vma=False,
    )
```

time: 170 us -> 158 us (0.929)
  starting transfers between devices: 98.3 us -> 79.6 us
  waiting for transfers between devices: 26.3 us -> 40.2 us
  local copies, waits for them, and re-layouts: 18.1 us -> 7.34 us
  Pallas kernels: 7.03 us -> 11.5 us
    all_to_all x2 -> x3, waiting for transfers between devices: 10.5 us -> 37.1 us  [the longest x2 25.5 us: exchange(): lax.all_to_all(value, 'expert', 0, 0, tiled=True)]
    ppermute x22 -> x17, starting transfers between devices: 68.1 us -> 47.9 us  [send(): return lax.ppermute(value, 'dp', pairs)]
    psum x1 -> x0, blocking collectives: 15.3 us -> none  [on_device(): gate_grad = lax.psum(gate_part.reshape(toks, top), 'dp')]
    all_to_all x0 -> x1, blocking collectives: none -> 15.1 us  [exchange_y(): lax.all_to_all(value, 'dp', 0, 0, axis_index_groups=groups, tiled=True)]
    ppermute x22 -> x17, waiting for transfers between devices: 15.8 us -> 3.03 us  [send(): return lax.ppermute(value, 'dp', pairs)]
    unnamed x25 -> x22, local copies, waits for them, and re-layouts: 16.2 us -> 7.34 us
    pallas_call x7 -> x8, Pallas kernels: 5.78 us -> 10.3 us  [the longest x1 2.87 us: on_device(): call(forward, shape((ROWS * n_dev, width)), [SM] + [VM] * (3 + 2 * NY), f...]
    all_to_all x2 -> x0, other arithmetic: 2.06 us -> none  [the longest x1 1.09 us: on_device(): got = lax.all_to_all(sent, 'expert', 0, 0, tiled=True)]
  transfers between devices with their start and end apart: 24 -> 20, of which waited for: 7 -> 4; matrix products, arithmetic and copies ran while one was open for 2% -> 0% of each run, Pallas kernels for 2% -> 3%
where the time goes in v2:
time: 158 us; the launch traced here: 155 us
  starting transfers between devices  79.6 us (50%)
  waiting for transfers between devices  40.2 us (25%)
  blocking collectives  15.1 us (10%)
  Pallas kernels  11.5 us (7%)
  local copies, waits for them, and re-layouts  7.34 us (5%)
    ppermute x17, starting transfers between devices, send(): return lax.ppermute(value, 'dp', pairs)  47.9 us
    all_to_all x2, starting transfers between devices, exchange(): lax.all_to_all(value, 'expert', 0, 0, tiled=True)  28.3 us
    all_to_all x2, waiting for transfers between devices, exchange(): lax.all_to_all(value, 'expert', 0, 0, tiled=True)  25.5 us
    all_to_all x1, blocking collectives, exchange_y(): lax.all_to_all(value, 'dp', 0, 0, axis_index_groups=groups, tiled=True)  15.1 us
    all_to_all x1, waiting for transfers between devices, exchange_y(): lax.all_to_all(value, 'dp', 0, 0, axis_index_groups=groups, tiled=True)  11.6 us
    unnamed x22, local copies, waits for them, and re-layouts  7.34 us
    all_to_all x1, starting transfers between devices, exchange_y(): lax.all_to_all(value, 'dp', 0, 0, axis_index_groups=groups, tiled=True)  3.48 us
  transfers between devices with their start and end apart: 20, of which 4 were waited for; matrix products, arithmetic and copies ran while one was open for 0% of the time, Pallas kernels for 3%

profile of v2, /device:TPU:6, one launch (start us, length us, event | category | flops | bytes accessed | tf_op | source)
XLA Modules:
  0.0 155.4 jit_solution(11259641617764889030)
XLA Ops:
  5.6 2.1 %shard_map.111 = (bf16[512,640]{1,0:T(8,128)(2,1)}, s32[128,1]{1,0:T(8,128)S(1)}) custom-call(s32[8,16]{1,0:T(8,128)S(1)} %bitcast.22, s32[8,16]{1,0:T(8,128)S(1)} %bitcast.23, s32[2,16]{1,0:T(2,128)S(1)} %bitcast.24, s32[1,64]{1,0:T(1,128)S(1)} %bitcast.25, bf16[128,192]{1,0:T(8,128)(2,1)S(1)} %bitcast.19, bf16[16,512]{1,0:T(8,128)(2,1)S(1)} %copy-done.4, ...), custom_call_target="tpu_custom_call" | custom-call | bytes 1048576 | tf_op jit(solution)/shard_map/pallas_call | solution.py:272
  7.7 18.8 %all-to-all-start = ((bf16[64,8,640]{2,1,0:T(8,128)(2,1)}), bf16[64,8,640]{2,1,0:T(8,128)(2,1)S(1)}, u32[]{:S(2)}, u32[]{:S(2)}) async-start(bf16[64,8,640]{2,1,0:T(8,128)(2,1)} %bitcast.7), calls=%async_computation | async-start | bytes 1310720 | tf_op jit(solution)/shard_map/all_to_all | solution.py:284
  26.5 1.4 copy-done
  28.0 1.9 %collective-permute-start.1 = (bf16[192,512]{1,0:T(8,128)(2,1)S(1)}, bf16[192,512]{1,0:T(8,128)(2,1)S(1)}, u32[]{:S(2)}, u32[]{:S(2)}) collective-permute-start(bf16[192,512]{1,0:T(8,128)(2,1)S(1)} %get-tuple-element.33), channel_id=1, source_target_pairs={{0,64},{64,0},{128,192},{192,128},{256,320},{320,256},{384,448},{4... | collective-permute-start | bytes 589832 | tf_op jit(solution)/shard_map/ppermute | solution.py:53
  29.9 4.9 %collective-permute-start.2 = (bf16[192,512]{1,0:T(8,128)(2,1)S(1)}, bf16[192,512]{1,0:T(8,128)(2,1)S(1)}, u32[]{:S(2)}, u32[]{:S(2)}) collective-permute-start(bf16[192,512]{1,0:T(8,128)(2,1)S(1)} %get-tuple-element.34), channel_id=1, source_target_pairs={{0,384},{64,448},{128,0},{192,64},{256,128},{320,192},{384,256},{4... | collective-permute-start | bytes 589832 | tf_op jit(solution)/shard_map/ppermute | solution.py:53
  34.9 2.5 %collective-permute-start.3 = (bf16[192,512]{1,0:T(8,128)(2,1)S(1)}, bf16[192,512]{1,0:T(8,128)(2,1)S(1)}, u32[]{:S(2)}, u32[]{:S(2)}) collective-permute-start(bf16[192,512]{1,0:T(8,128)(2,1)S(1)} %get-tuple-element.35), channel_id=1, source_target_pairs={{0,448},{64,384},{128,64},{192,0},{256,192},{320,128},{384,320},{4... | collective-permute-start | bytes 589832 | tf_op jit(solution)/shard_map/ppermute | solution.py:53
  37.3 2.2 %collective-permute-start.4 = (bf16[192,512]{1,0:T(8,128)(2,1)S(1)}, bf16[192,512]{1,0:T(8,128)(2,1)S(1)}, u32[]{:S(2)}, u32[]{:S(2)}) collective-permute-start(bf16[192,512]{1,0:T(8,128)(2,1)S(1)} %get-tuple-element.36), channel_id=1, source_target_pairs={{0,256},{64,320},{128,384},{192,448},{256,0},{320,64},{384,128},{4... | collective-permute-start | bytes 589832 | tf_op jit(solution)/shard_map/ppermute | solution.py:53
  39.6 4.7 %collective-permute-start.5 = (bf16[192,512]{1,0:T(8,128)(2,1)S(1)}, bf16[192,512]{1,0:T(8,128)(2,1)S(1)}, u32[]{:S(2)}, u32[]{:S(2)}) collective-permute-start(bf16[192,512]{1,0:T(8,128)(2,1)S(1)} %get-tuple-element.37), channel_id=1, source_target_pairs={{0,320},{64,256},{128,448},{192,384},{256,64},{320,0},{384,192},{4... | collective-permute-start | bytes 589832 | tf_op jit(solution)/shard_map/ppermute | solution.py:53
  44.3 3.2 %collective-permute-start.6 = (bf16[192,512]{1,0:T(8,128)(2,1)S(1)}, bf16[192,512]{1,0:T(8,128)(2,1)S(1)}, u32[]{:S(2)}, u32[]{:S(2)}) collective-permute-start(bf16[192,512]{1,0:T(8,128)(2,1)S(1)} %get-tuple-element.38), channel_id=1, source_target_pairs={{0,128},{64,192},{128,256},{192,320},{256,384},{320,448},{384,0},{... | collective-permute-start | bytes 589832 | tf_op jit(solution)/shard_map/ppermute | solution.py:53
  47.5 2.0 %collective-permute-start.7 = (bf16[192,512]{1,0:T(8,128)(2,1)S(1)}, bf16[192,512]{1,0:T(8,128)(2,1)S(1)}, u32[]{:S(2)}, u32[]{:S(2)}) collective-permute-start(bf16[192,512]{1,0:T(8,128)(2,1)S(1)} %get-tuple-element.39), channel_id=1, source_target_pairs={{0,192},{64,128},{128,320},{192,256},{256,448},{320,384},{384,64},... | collective-permute-start | bytes 589832 | tf_op jit(solution)/shard_map/ppermute | solution.py:53
  49.6 14.1 %all-to-all-done = bf16[64,8,640]{2,1,0:T(8,128)(2,1)S(1)} async-done(((bf16[64,8,640]{2,1,0:T(8,128)(2,1)}), bf16[64,8,640]{2,1,0:T(8,128)(2,1)S(1)}, u32[]{:S(2)}, u32[]{:S(2)}) %all-to-all-start) | async-done | bytes 655392 | tf_op jit(solution)/shard_map/all_to_all | solution.py:284
  64.6 1.2 shard_map.114
  65.8 1.9 %collective-permute-start.8 = (bf16[4,192,384]{2,1,0:T(8,128)(2,1)S(1)}, bf16[4,192,384]{2,1,0:T(8,128)(2,1)S(1)}, u32[]{:S(2)}, u32[]{:S(2)}) collective-permute-start(bf16[4,192,384]{2,1,0:T(8,128)(2,1)S(1)} %get-tuple-element.41), channel_id=1, source_target_pairs={{0,64},{64,0},{128,192},{192,128},{256,320},{320,256},{384,448},{4... | collective-permute-start | bytes 1769480 | tf_op jit(solution)/shard_map/ppermute | solution.py:53
  67.7 15.1 %all_to_all.20.near_ref = bf16[4,192,384]{2,1,0:T(8,128)(2,1)S(1)} all-to-all(bf16[4,192,384]{2,1,0:T(8,128)(2,1)S(1)} %get-tuple-element.30), channel_id=1, replica_groups={{0,128,256,384},{64,192,320,448},{1,129,257,385},{65,193,321,449},{2,13..., dimensions={0} | all-to-all | bytes 1179648 | tf_op jit(solution)/shard_map/all_to_all | solution.py:58
  82.8 1.9 %collective-permute-start = (bf16[4,192,384]{2,1,0:T(8,128)(2,1)S(1)}, bf16[4,192,384]{2,1,0:T(8,128)(2,1)S(1)}, u32[]{:S(2)}, u32[]{:S(2)}) collective-permute-start(bf16[4,192,384]{2,1,0:T(8,128)(2,1)S(1)} %all_to_all.20.near_ref), channel_id=1, source_target_pairs={{0,64},{64,0},{128,192},{192,128},{256,320},{320,256},{384,448},{4... | collective-permute-start | bytes 1769480 | tf_op jit(solution)/shard_map/ppermute | solution.py:53
  84.8 1.1 shard_map.115
  85.9 3.5 %all-to-all-start.2 = ((bf16[4,208,384]{2,1,0:T(8,128)(2,1)}), bf16[4,208,384]{2,1,0:T(8,128)(2,1)S(1)}, u32[]{:S(2)}, u32[]{:S(2)}) async-start(bf16[4,208,384]{2,1,0:T(8,128)(2,1)} %shard_map.115), calls=%async_computation.2 | async-start | bytes 1277952 | tf_op jit(solution)/shard_map/all_to_all | solution.py:58
  89.4 11.6 %all-to-all-done.2.back_ref = bf16[4,208,384]{2,1,0:T(8,128)(2,1)S(1)} async-done(((bf16[4,208,384]{2,1,0:T(8,128)(2,1)}), bf16[4,208,384]{2,1,0:T(8,128)(2,1)S(1)}, u32[]{:S(2)}, u32[]{:S(2)}) %all-to-all-start.2) | async-done | bytes 639008 | tf_op jit(solution)/shard_map/all_to_all | solution.py:58
  101.0 2.9 %shard_map.116 = bf16[512,640]{1,0:T(8,128)(2,1)} custom-call(s32[1]{0:T(128)} %bitcast.here_ref, bf16[4,192,384]{2,1,0:T(8,128)(2,1)S(1)} %all_to_all.20.near_ref, bf16[4,192,384]{2,1,0:T(8,128)(2,1)S(1)} %collective-permute-done.far_ref, bf16[4,208,384]{2,1,0:T(8,128)(2,1)S(1)} %all-to-all-done.2.back_ref, bf16[192,512]{1,0:T(8,128)(2,1)S(1)} %get-tuple-element.32.refs_0_, ...), custom_call_target="tpu_custom_call" | custom-call | flops 603979776 | bytes 1048576 | tf_op jit(solution)/shard_map/pallas_call | solution.py:298
  103.8 9.5 %all-to-all-start.3 = ((bf16[64,8,640]{2,1,0:T(8,128)(2,1)}), bf16[64,8,640]{2,1,0:T(8,128)(2,1)S(1)}, u32[]{:S(2)}, u32[]{:S(2)}) async-start(bf16[64,8,640]{2,1,0:T(8,128)(2,1)} %bitcast.10), calls=%async_computation.3 | async-start | bytes 1310720 | tf_op jit(solution)/shard_map/all_to_all | solution.py:284
  115.3 2.5 %collective-permute-start.10 = (bf16[192,512]{1,0:T(8,128)(2,1)S(1)}, bf16[192,512]{1,0:T(8,128)(2,1)S(1)}, u32[]{:S(2)}, u32[]{:S(2)}) collective-permute-start(bf16[192,512]{1,0:T(8,128)(2,1)S(1)} %get-tuple-element.47), channel_id=1, source_target_pairs={{0,128},{64,192},{128,256},{192,320},{256,384},{320,448},{384,0},{... | collective-permute-start | bytes 589832 | tf_op jit(solution)/shard_map/ppermute | solution.py:53
  117.8 1.9 %collective-permute-start.11 = (bf16[192,512]{1,0:T(8,128)(2,1)S(1)}, bf16[192,512]{1,0:T(8,128)(2,1)S(1)}, u32[]{:S(2)}, u32[]{:S(2)}) collective-permute-start(bf16[192,512]{1,0:T(8,128)(2,1)S(1)} %get-tuple-element.48), channel_id=1, source_target_pairs={{0,192},{64,128},{128,320},{192,256},{256,448},{320,384},{384,64},... | collective-permute-start | bytes 589832 | tf_op jit(solution)/shard_map/ppermute | solution.py:53
  119.7 4.5 %collective-permute-start.12 = (bf16[192,512]{1,0:T(8,128)(2,1)S(1)}, bf16[192,512]{1,0:T(8,128)(2,1)S(1)}, u32[]{:S(2)}, u32[]{:S(2)}) collective-permute-start(bf16[192,512]{1,0:T(8,128)(2,1)S(1)} %get-tuple-element.49), channel_id=1, source_target_pairs={{0,256},{64,320},{128,384},{192,448},{256,0},{320,64},{384,128},{4... | collective-permute-start | bytes 589832 | tf_op jit(solution)/shard_map/ppermute | solution.py:53
  124.2 3.2 %collective-permute-start.13 = (bf16[192,512]{1,0:T(8,128)(2,1)S(1)}, bf16[192,512]{1,0:T(8,128)(2,1)S(1)}, u32[]{:S(2)}, u32[]{:S(2)}) collective-permute-start(bf16[192,512]{1,0:T(8,128)(2,1)S(1)} %get-tuple-element.50), channel_id=1, source_target_pairs={{0,320},{64,256},{128,448},{192,384},{256,64},{320,0},{384,192},{4... | collective-permute-start | bytes 589832 | tf_op jit(solution)/shard_map/ppermute | solution.py:53
  127.4 4.3 %collective-permute-start.14 = (bf16[192,512]{1,0:T(8,128)(2,1)S(1)}, bf16[192,512]{1,0:T(8,128)(2,1)S(1)}, u32[]{:S(2)}, u32[]{:S(2)}) collective-permute-start(bf16[192,512]{1,0:T(8,128)(2,1)S(1)} %get-tuple-element.51), channel_id=1, source_target_pairs={{0,384},{64,448},{128,0},{192,64},{256,128},{320,192},{384,256},{4... | collective-permute-start | bytes 589832 | tf_op jit(solution)/shard_map/ppermute | solution.py:53
  131.7 1.9 %collective-permute-start.15 = (bf16[192,512]{1,0:T(8,128)(2,1)S(1)}, bf16[192,512]{1,0:T(8,128)(2,1)S(1)}, u32[]{:S(2)}, u32[]{:S(2)}) collective-permute-start(bf16[192,512]{1,0:T(8,128)(2,1)S(1)} %get-tuple-element.52), channel_id=1, source_target_pairs={{0,448},{64,384},{128,64},{192,0},{256,192},{320,128},{384,320},{4... | collective-permute-start | bytes 589832 | tf_op jit(solution)/shard_map/ppermute | solution.py:53
  133.6 3.0 %collective-permute-done.11.refs_3_ = bf16[192,512]{1,0:T(8,128)(2,1)S(1)} collective-permute-done((bf16[192,512]{1,0:T(8,128)(2,1)S(1)}, bf16[192,512]{1,0:T(8,128)(2,1)S(1)}, u32[]{:S(2)}, u32[]{:S(2)}) %collective-permute-start.11) | collective-permute-done | bytes 196640 | tf_op jit(solution)/shard_map/ppermute | solution.py:53
  136.6 2.4 %collective-permute-start.9 = (bf16[192,512]{1,0:T(8,128)(2,1)S(1)}, bf16[192,512]{1,0:T(8,128)(2,1)S(1)}, u32[]{:S(2)}, u32[]{:S(2)}) collective-permute-start(bf16[192,512]{1,0:T(8,128)(2,1)S(1)} %get-tuple-element.46), channel_id=1, source_target_pairs={{0,64},{64,0},{128,192},{192,128},{256,320},{320,256},{384,448},{4... | collective-permute-start | bytes 589832 | tf_op jit(solution)/shard_map/ppermute | solution.py:53
  139.0 11.4 %all-to-all-done.3 = bf16[64,8,640]{2,1,0:T(8,128)(2,1)S(1)} async-done(((bf16[64,8,640]{2,1,0:T(8,128)(2,1)}), bf16[64,8,640]{2,1,0:T(8,128)(2,1)S(1)}, u32[]{:S(2)}, u32[]{:S(2)}) %all-to-all-start.3) | async-done | bytes 655392 | tf_op jit(solution)/shard_map/all_to_all | solution.py:284
  150.4 1.1 shard_map.117
  151.6 1.9 %collective-permute-start.16 = (f32[8,16]{1,0:T(8,128)S(1)}, f32[8,16]{1,0:T(8,128)S(1)}, u32[]{:S(2)}, u32[]{:S(2)}) collective-permute-start(f32[8,16]{1,0:T(8,128)S(1)} %get-tuple-element.53), channel_id=1, source_target_pairs={{0,64},{64,0},{128,192},{192,128},{256,320},{320,256},{384,448},{4... | collective-permute-start | bytes 1544 | tf_op jit(solution)/shard_map/ppermute | solution.py:53
  153.5 1.3 shard_map.119
  (41 shorter events, 8.5 us)
Async XLA Ops:
  0.6 0.8 copy-start.1
  1.5 0.7 copy-start.2
  2.2 0.7 copy-start.4
  2.9 0.7 copy-start.5
  3.6 0.7 copy-start.6
  4.3 0.7 copy-start.7
  4.9 0.7 copy-start.8
  7.7 56.0 %all-to-all-start = ((bf16[64,8,640]{2,1,0:T(8,128)(2,1)}), bf16[64,8,640]{2,1,0:T(8,128)(2,1)S(1)}, u32[]{:S(2)}, u32[]{:S(2)}) async-start(bf16[64,8,640]{2,1,0:T(8,128)(2,1)} %bitcast.7), calls=%async_computation | async-start | bytes 1310720 | tf_op jit(solution)/shard_map/all_to_all | solution.py:284
  26.5 1.4 copy-start
  28.0 16.3 %collective-permute-start.1 = (bf16[192,512]{1,0:T(8,128)(2,1)S(1)}, bf16[192,512]{1,0:T(8,128)(2,1)S(1)}, u32[]{:S(2)}, u32[]{:S(2)}) collective-permute-start(bf16[192,512]{1,0:T(8,128)(2,1)S(1)} %get-tuple-element.33), channel_id=1, source_target_pairs={{0,64},{64,0},{128,192},{192,128},{256,320},{320,256},{384,448},{4... | collective-permute-start | bytes 589832 | tf_op jit(solution)/shard_map/ppermute | solution.py:53
  29.9 17.6 %collective-permute-start.2 = (bf16[192,512]{1,0:T(8,128)(2,1)S(1)}, bf16[192,512]{1,0:T(8,128)(2,1)S(1)}, u32[]{:S(2)}, u32[]{:S(2)}) collective-permute-start(bf16[192,512]{1,0:T(8,128)(2,1)S(1)} %get-tuple-element.34), channel_id=1, source_target_pairs={{0,384},{64,448},{128,0},{192,64},{256,128},{320,192},{384,256},{4... | collective-permute-start | bytes 589832 | tf_op jit(solution)/shard_map/ppermute | solution.py:53
  34.9 29.7 %collective-permute-start.3 = (bf16[192,512]{1,0:T(8,128)(2,1)S(1)}, bf16[192,512]{1,0:T(8,128)(2,1)S(1)}, u32[]{:S(2)}, u32[]{:S(2)}) collective-permute-start(bf16[192,512]{1,0:T(8,128)(2,1)S(1)} %get-tuple-element.35), channel_id=1, source_target_pairs={{0,448},{64,384},{128,64},{192,0},{256,192},{320,128},{384,320},{4... | collective-permute-start | bytes 589832 | tf_op jit(solution)/shard_map/ppermute | solution.py:53
  37.3 27.2 %collective-permute-start.4 = (bf16[192,512]{1,0:T(8,128)(2,1)S(1)}, bf16[192,512]{1,0:T(8,128)(2,1)S(1)}, u32[]{:S(2)}, u32[]{:S(2)}) collective-permute-start(bf16[192,512]{1,0:T(8,128)(2,1)S(1)} %get-tuple-element.36), channel_id=1, source_target_pairs={{0,256},{64,320},{128,384},{192,448},{256,0},{320,64},{384,128},{4... | collective-permute-start | bytes 589832 | tf_op jit(solution)/shard_map/ppermute | solution.py:53
  39.6 25.0 %collective-permute-start.5 = (bf16[192,512]{1,0:T(8,128)(2,1)S(1)}, bf16[192,512]{1,0:T(8,128)(2,1)S(1)}, u32[]{:S(2)}, u32[]{:S(2)}) collective-permute-start(bf16[192,512]{1,0:T(8,128)(2,1)S(1)} %get-tuple-element.37), channel_id=1, source_target_pairs={{0,320},{64,256},{128,448},{192,384},{256,64},{320,0},{384,192},{4... | collective-permute-start | bytes 589832 | tf_op jit(solution)/shard_map/ppermute | solution.py:53
  44.3 20.3 %collective-permute-start.6 = (bf16[192,512]{1,0:T(8,128)(2,1)S(1)}, bf16[192,512]{1,0:T(8,128)(2,1)S(1)}, u32[]{:S(2)}, u32[]{:S(2)}) collective-permute-start(bf16[192,512]{1,0:T(8,128)(2,1)S(1)} %get-tuple-element.38), channel_id=1, source_target_pairs={{0,128},{64,192},{128,256},{192,320},{256,384},{320,448},{384,0},{... | collective-permute-start | bytes 589832 | tf_op jit(solution)/shard_map/ppermute | solution.py:53
  47.5 17.1 %collective-permute-start.7 = (bf16[192,512]{1,0:T(8,128)(2,1)S(1)}, bf16[192,512]{1,0:T(8,128)(2,1)S(1)}, u32[]{:S(2)}, u32[]{:S(2)}) collective-permute-start(bf16[192,512]{1,0:T(8,128)(2,1)S(1)} %get-tuple-element.39), channel_id=1, source_target_pairs={{0,192},{64,128},{128,320},{192,256},{256,448},{320,384},{384,64},... | collective-permute-start | bytes 589832 | tf_op jit(solution)/shard_map/ppermute | solution.py:53
  64.6 18.3 %copy-start.9 = (bf16[384,512]{1,0:T(8,128)(2,1)}, bf16[384,512]{1,0:T(8,128)(2,1)S(1)}, u32[]{:S(2)}) copy-start(bf16[384,512]{1,0:T(8,128)(2,1)S(1)} %get-tuple-element.31.grad_ref) | copy-start | bytes 1179652
  65.8 19.0 %collective-permute-start.8 = (bf16[4,192,384]{2,1,0:T(8,128)(2,1)S(1)}, bf16[4,192,384]{2,1,0:T(8,128)(2,1)S(1)}, u32[]{:S(2)}, u32[]{:S(2)}) collective-permute-start(bf16[4,192,384]{2,1,0:T(8,128)(2,1)S(1)} %get-tuple-element.41), channel_id=1, source_target_pairs={{0,64},{64,0},{128,192},{192,128},{256,320},{320,256},{384,448},{4... | collective-permute-start | bytes 1769480 | tf_op jit(solution)/shard_map/ppermute | solution.py:53
  82.8 6.5 %collective-permute-start = (bf16[4,192,384]{2,1,0:T(8,128)(2,1)S(1)}, bf16[4,192,384]{2,1,0:T(8,128)(2,1)S(1)}, u32[]{:S(2)}, u32[]{:S(2)}) collective-permute-start(bf16[4,192,384]{2,1,0:T(8,128)(2,1)S(1)} %all_to_all.20.near_ref), channel_id=1, source_target_pairs={{0,64},{64,0},{128,192},{192,128},{256,320},{320,256},{384,448},{4... | collective-permute-start | bytes 1769480 | tf_op jit(solution)/shard_map/ppermute | solution.py:53
  85.9 15.1 %all-to-all-start.2 = ((bf16[4,208,384]{2,1,0:T(8,128)(2,1)}), bf16[4,208,384]{2,1,0:T(8,128)(2,1)S(1)}, u32[]{:S(2)}, u32[]{:S(2)}) async-start(bf16[4,208,384]{2,1,0:T(8,128)(2,1)} %shard_map.115), calls=%async_computation.2 | async-start | bytes 1277952 | tf_op jit(solution)/shard_map/all_to_all | solution.py:58
  103.8 46.6 %copy-start.3 = (f32[16,8]{0,1:T(8,128)S(1)}, f32[16,8]{0,1:T(8,128)}, u32[]{:S(2)}) copy-start(f32[16,8]{0,1:T(8,128)} %param.10) | copy-start | bytes 1540
  103.8 46.6 %all-to-all-start.3 = ((bf16[64,8,640]{2,1,0:T(8,128)(2,1)}), bf16[64,8,640]{2,1,0:T(8,128)(2,1)S(1)}, u32[]{:S(2)}, u32[]{:S(2)}) async-start(bf16[64,8,640]{2,1,0:T(8,128)(2,1)} %bitcast.10), calls=%async_computation.3 | async-start | bytes 1310720 | tf_op jit(solution)/shard_map/all_to_all | solution.py:284
  113.3 1.0 copy-start.10
  115.3 16.4 %collective-permute-start.10 = (bf16[192,512]{1,0:T(8,128)(2,1)S(1)}, bf16[192,512]{1,0:T(8,128)(2,1)S(1)}, u32[]{:S(2)}, u32[]{:S(2)}) collective-permute-start(bf16[192,512]{1,0:T(8,128)(2,1)S(1)} %get-tuple-element.47), channel_id=1, source_target_pairs={{0,128},{64,192},{128,256},{192,320},{256,384},{320,448},{384,0},{... | collective-permute-start | bytes 589832 | tf_op jit(solution)/shard_map/ppermute | solution.py:53
  117.8 18.8 %collective-permute-start.11 = (bf16[192,512]{1,0:T(8,128)(2,1)S(1)}, bf16[192,512]{1,0:T(8,128)(2,1)S(1)}, u32[]{:S(2)}, u32[]{:S(2)}) collective-permute-start(bf16[192,512]{1,0:T(8,128)(2,1)S(1)} %get-tuple-element.48), channel_id=1, source_target_pairs={{0,192},{64,128},{128,320},{192,256},{256,448},{320,384},{384,64},... | collective-permute-start | bytes 589832 | tf_op jit(solution)/shard_map/ppermute | solution.py:53
  119.7 31.9 %collective-permute-start.12 = (bf16[192,512]{1,0:T(8,128)(2,1)S(1)}, bf16[192,512]{1,0:T(8,128)(2,1)S(1)}, u32[]{:S(2)}, u32[]{:S(2)}) collective-permute-start(bf16[192,512]{1,0:T(8,128)(2,1)S(1)} %get-tuple-element.49), channel_id=1, source_target_pairs={{0,256},{64,320},{128,384},{192,448},{256,0},{320,64},{384,128},{4... | collective-permute-start | bytes 589832 | tf_op jit(solution)/shard_map/ppermute | solution.py:53
  124.2 29.3 %collective-permute-start.13 = (bf16[192,512]{1,0:T(8,128)(2,1)S(1)}, bf16[192,512]{1,0:T(8,128)(2,1)S(1)}, u32[]{:S(2)}, u32[]{:S(2)}) collective-permute-start(bf16[192,512]{1,0:T(8,128)(2,1)S(1)} %get-tuple-element.50), channel_id=1, source_target_pairs={{0,320},{64,256},{128,448},{192,384},{256,64},{320,0},{384,192},{4... | collective-permute-start | bytes 589832 | tf_op jit(solution)/shard_map/ppermute | solution.py:53
  127.4 26.1 %collective-permute-start.14 = (bf16[192,512]{1,0:T(8,128)(2,1)S(1)}, bf16[192,512]{1,0:T(8,128)(2,1)S(1)}, u32[]{:S(2)}, u32[]{:S(2)}) collective-permute-start(bf16[192,512]{1,0:T(8,128)(2,1)S(1)} %get-tuple-element.51), channel_id=1, source_target_pairs={{0,384},{64,448},{128,0},{192,64},{256,128},{320,192},{384,256},{4... | collective-permute-start | bytes 589832 | tf_op jit(solution)/shard_map/ppermute | solution.py:53
  131.7 21.8 %collective-permute-start.15 = (bf16[192,512]{1,0:T(8,128)(2,1)S(1)}, bf16[192,512]{1,0:T(8,128)(2,1)S(1)}, u32[]{:S(2)}, u32[]{:S(2)}) collective-permute-start(bf16[192,512]{1,0:T(8,128)(2,1)S(1)} %get-tuple-element.52), channel_id=1, source_target_pairs={{0,448},{64,384},{128,64},{192,0},{256,192},{320,128},{384,320},{4... | collective-permute-start | bytes 589832 | tf_op jit(solution)/shard_map/ppermute | solution.py:53
  136.6 16.9 %collective-permute-start.9 = (bf16[192,512]{1,0:T(8,128)(2,1)S(1)}, bf16[192,512]{1,0:T(8,128)(2,1)S(1)}, u32[]{:S(2)}, u32[]{:S(2)}) collective-permute-start(bf16[192,512]{1,0:T(8,128)(2,1)S(1)} %get-tuple-element.46), channel_id=1, source_target_pairs={{0,64},{64,0},{128,192},{192,128},{256,320},{320,256},{384,448},{4... | collective-permute-start | bytes 589832 | tf_op jit(solution)/shard_map/ppermute | solution.py:53
  151.6 3.2 %collective-permute-start.16 = (f32[8,16]{1,0:T(8,128)S(1)}, f32[8,16]{1,0:T(8,128)S(1)}, u32[]{:S(2)}, u32[]{:S(2)}) collective-permute-start(f32[8,16]{1,0:T(8,128)S(1)} %get-tuple-element.53), channel_id=1, source_target_pairs={{0,64},{64,0},{128,192},{192,128},{256,320},{320,256},{384,448},{4... | collective-permute-start | bytes 1544 | tf_op jit(solution)/shard_map/ppermute | solution.py:53

commit v3 on v2

v3 whole, which is shorter than its diff:
```python
import jax
import jax.numpy as jnp
from jax import lax
from jax.experimental import pallas as pl
from jax.experimental.pallas import tpu as pltpu
from jax.sharding import PartitionSpec as P

CAP = 3
SLOTS = 2 * CAP
LANES = 128
TILE = 4
NY = 4
BF = jnp.bfloat16
F32 = jnp.float32
VM = pl.BlockSpec(memory_space=pltpu.VMEM)
SM = pl.BlockSpec(memory_space=pltpu.SMEM)


def call(kernel, outs, specs, flops=0, moved=1 << 20, scratch=(), vmem=40 << 20):
    return pl.pallas_call(
        kernel,
        out_shape=outs,
        in_specs=specs,
        out_specs=jax.tree.map(lambda _: VM, outs),
        scratch_shapes=list(scratch),
        compiler_params=pltpu.CompilerParams(vmem_limit_bytes=vmem),
        cost_estimate=pl.CostEstimate(flops=flops, bytes_accessed=moved, transcendentals=0),
    )


def dot(a, b, ca, cb):
    return lax.dot_general(a, b, (((ca,), (cb,)), ((), ())), preferred_element_type=F32)


def shape(dims, dtype=BF):
    return jax.ShapeDtypeStruct(dims, dtype)


def ones(mask):
    return mask.astype(F32).astype(BF)


def iota(dims, axis):
    return lax.broadcasted_iota(jnp.int32, dims, axis)


def payload_rows(feats, hidden):
    wide = SLOTS * feats // LANES
    narrow = -(-SLOTS * hidden // LANES)
    return wide, narrow, -(-(wide + narrow) // TILE) * TILE


def send(value, step, other):
    pairs = [(i, ((i // 2 + step) % NY) * 2 + ((i % 2) ^ other)) for i in range(2 * NY)]
    return lax.ppermute(value, "dp", pairs)


def exchange_y(value):
    groups = [[2 * y + core for y in range(NY)] for core in range(2)]
    return lax.all_to_all(value, "dp", 0, 0, axis_index_groups=groups, tiled=True)


def chip(here, step):
    return lax.rem(here // 2 + step, NY)


def peer_column(here, step, other, width):
    peer = chip(here, step) * 2 + lax.rem(lax.rem(here, 2) + other, 2)
    return pl.multiple_of(peer * width, width)


def cut_weights(here_ref, w_ref, *outs):
    width = outs[0].shape[1]
    here = here_ref[0]
    for step in range(NY):
        for other in range(2):
            at = peer_column(here, step, other, width)
            outs[2 * step + other][...] = w_ref[:, pl.ds(at, width)]


def join_gradient(here_ref, *refs):
    parts, out_ref = refs[:-1], refs[-1]
    width = parts[0].shape[1]
    here = here_ref[0]
    for step in range(NY):
        for other in range(2):
            at = peer_column(here, (NY - step) % NY, other, width)
            out_ref[:, pl.ds(at, width)] = parts[2 * step + other][...]


def column(stored):
    top, toks = stored.shape
    spread = jnp.broadcast_to(stored[None], (toks, top, toks)).reshape(toks * top, toks)
    mine = iota(spread.shape, 0) // top == iota(spread.shape, 1)
    return jnp.sum(jnp.where(mine, spread, jnp.zeros_like(spread)), axis=1, keepdims=True)


def as_row(col):
    n = col.shape[0]
    diagonal = iota((n, n), 0) == iota((n, n), 1)
    return jnp.sum(jnp.where(diagonal, col, jnp.zeros_like(col)), axis=0, keepdims=True)


def pack(rows_ref, flat_ref, wide_vals, narrow_vals):
    n_dev = flat_ref.shape[0]
    feats, hidden = wide_vals.shape[1], narrow_vals.shape[1]
    wide, narrow, rows = payload_rows(feats, hidden)
    each = feats // LANES
    for j in range(SLOTS):
        part = slice(j * n_dev, (j + 1) * n_dev)
        for i in range(each):
            block = wide_vals[part, i * LANES : (i + 1) * LANES]
            rows_ref[pl.ds(j * each + i, n_dev, stride=rows), :] = block
        flat_ref[:, j * hidden : (j + 1) * hidden] = narrow_vals[part]
    for i in range(rows - wide):
        block = jnp.zeros((n_dev, LANES), F32)
        if i < narrow:
            block = flat_ref[:, i * LANES : (i + 1) * LANES]
        rows_ref[pl.ds(wide + i, n_dev, stride=rows), :] = block


def unpack(rows_ref, flat_ref, feats, hidden):
    n_dev = flat_ref.shape[0]
    wide, narrow, rows = payload_rows(feats, hidden)
    each = feats // LANES
    wide_vals = jnp.concatenate(
        [
            jnp.concatenate(
                [rows_ref[pl.ds(j * each + i, n_dev, stride=rows), :] for i in range(each)], axis=1
            )
            for j in range(SLOTS)
        ],
        axis=0,
    )
    for i in range(narrow):
        block = rows_ref[pl.ds(wide + i, n_dev, stride=rows), :]
        flat_ref[:, i * LANES : (i + 1) * LANES] = block
    narrow_vals = jnp.concatenate(
        [flat_ref[:, j * hidden : (j + 1) * hidden] for j in range(SLOTS)], axis=0
    )
    return wide_vals, narrow_vals


def dispatch(
    ids_hbm, picks_hbm, place_hbm, cap_hbm, act_hbm, cot_hbm, gate_hbm, sent_ref, slot_ref,
    ids_ref, picks_ref, place_ref, cap_ref, act_ref, cot_ref, gate_ref, rows_ref, flat_ref, sems,
):
    sources = (ids_hbm, picks_hbm, place_hbm, cap_hbm, act_hbm, cot_hbm, gate_hbm)
    targets = (ids_ref, picks_ref, place_ref, cap_ref, act_ref, cot_ref, gate_ref)
    copies = [
        pltpu.make_async_copy(source, target, sems.at[i])
        for i, (source, target) in enumerate(zip(sources, targets))
    ]
    for copy in copies:
        copy.start()
    for copy in copies:
        copy.wait()
    n_dev = cap_ref.shape[1]
    rows, hidden = act_ref.shape
    toks, feats = cot_ref.shape
    top = rows // toks
    ids, picks = column(ids_ref[...]), column(picks_ref[...])
    match = (place_ref[0:1, :] == ids).astype(jnp.int32)
    has = jnp.sum(match, axis=1, keepdims=True)
    host = jnp.sum(match * place_ref[1:2, :], axis=1, keepdims=True)
    copied = (has > 0) & (picks == 1)
    dest = jnp.where(copied, host, ids)
    dest_row = as_row(dest)
    earlier = (dest == dest_row) & (iota((rows, rows), 1) < iota((rows, rows), 0))
    rank = jnp.sum(earlier.astype(jnp.int32), axis=1, keepdims=True)
    at_dest = iota((rows, n_dev), 1) == dest
    limit = jnp.sum(jnp.where(at_dest, cap_ref[...], 0), axis=1, keepdims=True)
    slot = jnp.where(rank < limit, (jnp.where(copied, CAP, 0) + rank) * n_dev + ids, -1)
    slot_ref[...] = slot
    pick = ones(iota((SLOTS * n_dev, rows), 0) == as_row(slot))
    owner = ones(iota((rows, toks), 0) // top == iota((rows, toks), 1))
    grad = (column(gate_ref[...]) * dot(owner, cot_ref[...], 1, 0)).astype(BF)
    pack(rows_ref, flat_ref, dot(pick, grad, 1, 0), dot(pick, act_ref[...], 1, 0))
    sent_ref[...] = rows_ref[...].astype(BF)


def backward(here_ref, got_ref, *refs):
    w_refs, (mine_ref, theirs_ref, grad_ref, rows_ref, flat_ref) = refs[:-5], refs[-5:]
    feats, hidden = grad_ref.shape[1], mine_ref.shape[1]
    rows_ref[...] = got_ref[...].astype(F32)
    grad, acts = unpack(rows_ref, flat_ref, feats, hidden)
    acts = acts.T.astype(BF)
    mine_ref[NY] = acts
    theirs_ref[NY] = acts
    grad = grad.astype(BF)
    grad_ref[...] = grad
    for step in range(NY):
        at = chip(here_ref[0], step)
        mine_ref[at] = dot(w_refs[2 * step][...], grad, 1, 1).astype(BF)
        theirs_ref[at] = dot(w_refs[2 * step + 1][...], grad, 1, 1).astype(BF)


def add_cores(mine_ref, theirs_ref, out_ref):
    for y in range(NY):
        out_ref[y, 0] = mine_ref[NY]
        out_ref[y, 1] = theirs_ref[NY]
        out_ref[y, 2] = (mine_ref[y].astype(F32) + theirs_ref[y].astype(F32)).astype(BF)


def forward(here_ref, all_ref, *refs):
    w_refs, (sent_ref, rows_ref, flat_ref) = refs[:-3], refs[-3:]
    total = None
    for step in range(NY):
        at = chip(here_ref[0], step)
        for other in range(2):
            part = dot(all_ref[at, other], w_refs[2 * step + other][...], 0, 0)
            total = part if total is None else total + part
    back = sum(all_ref[y, 2].astype(F32) for y in range(NY))
    pack(rows_ref, flat_ref, total, back.T)
    sent_ref[...] = rows_ref[...].astype(BF)


def weights_back(here_ref, all_ref, grad_ref, *outs):
    grad = grad_ref[...]
    for step in range(NY):
        at = chip(here_ref[0], step)
        for other in range(2):
            outs[2 * step + other][...] = dot(all_ref[at, other], grad, 1, 0).astype(BF)


def collect(got_ref, slot_ref, gate_ref, act_ref, mixed_ref, back_ref, gate_out_ref, rows_ref, flat_ref):
    top, toks = gate_ref.shape
    rows, hidden = back_ref.shape
    feats = mixed_ref.shape[1]
    rows_ref[...] = got_ref[...].astype(F32)
    outs, backs = unpack(rows_ref, flat_ref, feats, hidden)
    gate = column(gate_ref[...])
    pick = ones(iota((rows, outs.shape[0]), 1) == slot_ref[...])
    row_out = dot(pick, outs.astype(BF), 1, 0) * gate
    mixed_ref[...] = jnp.sum(row_out.reshape(toks, top, feats), axis=1).astype(BF)
    back = dot(pick, backs.astype(BF), 1, 0)
    back_ref[...] = back.astype(BF)
    gate_back = jnp.sum(back * act_ref[...].astype(F32), axis=1, keepdims=True) / gate
    at_tok = iota((rows, toks), 0) // top == iota((rows, toks), 1)
    spread = jnp.where(at_tok, gate_back, 0.0)
    gate_out_ref[...] = jnp.zeros_like(gate_out_ref)
    part = jnp.sum(spread.reshape(toks, top, toks), axis=0)
    for i in range(2 * NY):
        gate_out_ref[i, :, :toks] = part


def on_device(acts, w_down, gates, cotangent, expert_ids, replica_pick, placement, group_cap):
    n_dev = lax.axis_size("expert")
    toks, top, hidden = acts.shape
    feats = cotangent.shape[1]
    rows, slots = toks * top, SLOTS * n_dev
    _, narrow, per_peer = payload_rows(feats, hidden)
    payload = shape((n_dev * per_peer, LANES))
    scratch = [
        pltpu.VMEM((n_dev * per_peer, LANES), F32),
        pltpu.VMEM((n_dev, narrow * LANES), F32),
    ]
    here = lax.axis_index("dp").astype(jnp.int32).reshape(1)
    gates_t = gates.T
    pieces_shape = [shape((hidden, feats))] * (2 * NY)

    cuts = call(cut_weights, pieces_shape, [SM, VM], moved=3 << 20)(here, w_down[0])
    weights = [None] * (2 * NY)
    for step in range(NY):
        for other in range(2):
            piece = cuts[2 * step + other]
            if step or other:
                piece = send(piece, step, other)
            weights[2 * ((NY - step) % NY) + other] = piece

    inputs = (
        expert_ids.T, replica_pick.T, placement.T, group_cap.reshape(1, n_dev),
        acts.reshape(rows, hidden), cotangent, gates_t,
    )
    sent, slot = call(
        dispatch,
        [payload, shape((rows, 1), jnp.int32)],
        [pl.BlockSpec(memory_space=pltpu.HBM)] * len(inputs),
        scratch=[pltpu.VMEM(x.shape, x.dtype) for x in inputs]
        + scratch
        + [pltpu.SemaphoreType.DMA((len(inputs),))],
        vmem=63 << 20,
    )(*inputs)

    def exchange(value):
        value = value.reshape(n_dev, per_peer // TILE, TILE, LANES)
        return lax.all_to_all(value, "expert", 0, 0, tiled=True).reshape(payload.shape)

    got = exchange(sent)
    stack = shape((NY + 1, hidden, slots))
    flops = 2 * slots * feats * hidden * 2 * NY
    mine, theirs, grad = call(
        backward,
        [stack, stack, shape((slots, feats))],
        [SM] + [VM] * (1 + 2 * NY),
        flops=flops,
        scratch=scratch,
    )(here, got, *weights)
    theirs = send(theirs, 0, 1)
    shared = call(add_cores, shape((NY, 3, hidden, slots)), [VM] * 2)(mine, theirs)
    shared = exchange_y(shared)
    returned = call(forward, payload, [SM] + [VM] * (1 + 2 * NY), flops=flops, scratch=scratch)(
        here, shared, *weights
    )
    home = exchange(returned)

    pieces = call(weights_back, pieces_shape, [SM] + [VM] * 2, flops=flops)(here, shared, grad)
    joined = []
    for step in range(NY):
        for other in range(2):
            piece = pieces[2 * step + other]
            joined.append(send(piece, step, other) if step or other else piece)
    weight_grad = call(
        join_gradient, shape((hidden, 2 * NY * feats)), [SM] + [VM] * (2 * NY), moved=3 << 20
    )(here, *joined)

    home, weight_grad = lax.optimization_barrier((home, weight_grad))
    combined, back_rows, gate_parts = call(
        collect,
        [shape((toks, feats)), shape((rows, hidden)), shape((2 * NY, top, LANES), F32)],
        [VM] * 4,
        scratch=scratch,
    )(home, slot, gates_t, inputs[4])
    gate_parts = lax.all_to_all(gate_parts, "dp", 0, 0, tiled=True)
    gate_grad = jnp.sum(gate_parts, axis=0)[:, :toks].T
    return combined, back_rows.reshape(toks, top, hidden), weight_grad[None], gate_grad


def solution(mesh):
    return jax.shard_map(
        on_device,
        mesh=mesh,
        in_specs=(
            P("expert", None, "dp"),
            P("expert", "dp", None),
            P("expert", None),
            P("expert", "dp"),
            P("expert", None),
            P("expert", None),
            P(),
            P(),
        ),
        out_specs=(
            P("expert", "dp"),
            P("expert", None, "dp"),
            P("expert", "dp", None),
            P("expert", None),
        ),
        check_vma=False,
    )
```

time: 158 us -> 151 us (0.956)
  blocking collectives: 15.1 us -> 36.8 us
  waiting for transfers between devices: 40.2 us -> 21.5 us
  local copies, waits for them, and re-layouts: 7.34 us -> 3.75 us
  starting transfers between devices: 79.6 us -> 76.9 us
  Pallas kernels: 11.5 us -> 9.45 us
    all_to_all x3 -> x2, waiting for transfers between devices: 37.1 us -> 0.78 us  [exchange(): lax.all_to_all(value, 'expert', 0, 0, tiled=True).reshape(payload.shape)]
    ppermute x17 -> x15, waiting for transfers between devices: 3.03 us -> 20.8 us  [send(): return lax.ppermute(value, 'dp', pairs)]
    all_to_all x1, blocking collectives: 15.1 us -> 27.4 us  [exchange_y(): lax.all_to_all(value, 'dp', 0, 0, axis_index_groups=groups, tiled=True)]
    all_to_all x0 -> x1, blocking collectives: none -> 9.42 us  [on_device(): gate_parts = lax.all_to_all(gate_parts, 'dp', 0, 0, tiled=True)]
    unnamed x22 -> x12, local copies, waits for them, and re-layouts: 7.34 us -> 3.15 us
    ppermute x17 -> x15, starting transfers between devices: 47.9 us -> 45 us  [send(): return lax.ppermute(value, 'dp', pairs)]
    pallas_call x7 -> x6, Pallas kernels: 10.2 us -> 8.09 us  [the longest x1 2.61 us: on_device(): call(dispatch, [payload, shape((rows, 1), jnp.int32)], [pl.BlockSpec(memo...]
    all_to_all x3 -> x2, starting transfers between devices: 31.7 us -> 32 us  [exchange(): lax.all_to_all(value, 'expert', 0, 0, tiled=True).reshape(payload.shape)]
  transfers between devices with their start and end apart: 20 -> 17, of which waited for: 4 -> 9; matrix products, arithmetic and copies ran while one was open for 0% -> 0% of each run, Pallas kernels for 3% -> 2%
where the time goes in v3:
time: 151 us; the launch traced here: 149 us
  starting transfers between devices  76.9 us (51%)
  blocking collectives  36.8 us (24%)
  waiting for transfers between devices  21.5 us (14%)
  Pallas kernels  9.45 us (6%)
  local copies, waits for them, and re-layouts  3.75 us (2%)
    ppermute x15, starting transfers between devices, send(): return lax.ppermute(value, 'dp', pairs)  45 us
    all_to_all x2, starting transfers between devices, exchange(): lax.all_to_all(value, 'expert', 0, 0, tiled=True).reshape(payload.shape)  32 us
    all_to_all x1, blocking collectives, exchange_y(): lax.all_to_all(value, 'dp', 0, 0, axis_index_groups=groups, tiled=True)  27.4 us
    ppermute x15, waiting for transfers between devices, send(): return lax.ppermute(value, 'dp', pairs)  20.8 us
    all_to_all x1, blocking collectives, on_device(): gate_parts = lax.all_to_all(gate_parts, 'dp', 0, 0, tiled=True)  9.42 us
    unnamed x12, local copies, waits for them, and re-layouts  3.15 us
  transfers between devices with their start and end apart: 17, of which 9 were waited for; matrix products, arithmetic and copies ran while one was open for 0% of the time, Pallas kernels for 2%

profile of v3, /device:TPU:6, one launch (start us, length us, event | category | flops | bytes accessed | tf_op | source)
XLA Modules:
  0.0 149.4 jit_solution(4684322911216606860)
XLA Ops:
  0.6 2.6 %shard_map.111 = (bf16[2304,128]{1,0:T(8,128)(2,1)}, s32[128,1]{1,0:T(8,128)}) custom-call(s32[8,16]{1,0:T(8,128)} %bitcast.25, s32[8,16]{1,0:T(8,128)} %bitcast.26, s32[2,16]{1,0:T(2,128)} %bitcast.27, s32[1,64]{1,0:T(1,128)} %bitcast.28, bf16[128,192]{1,0:T(8,128)(2,1)} %bitcast.19, bf16[16,512]{1,0:T(8,128)(2,1)} %cot_hbm.1, f32[8,16]{1,0:T(8,128)} %bitcast.21), custom_call_target="tpu_custom_call" | custom-call | bytes 1048576 | tf_op jit(solution)/shard_map/pallas_call | solution.py:275
  3.3 18.8 %all-to-all-start = ((bf16[64,9,4,128]{3,2,1,0:T(4,128)(2,1)}), bf16[64,9,4,128]{3,2,1,0:T(4,128)(2,1)S(1)}, u32[]{:S(2)}, u32[]{:S(2)}) async-start(bf16[64,9,4,128]{3,2,1,0:T(4,128)(2,1)} %bitcast.24), calls=%async_computation | async-start | bytes 1179648 | tf_op jit(solution)/shard_map/all_to_all | solution.py:287
  22.1 1.4 copy-done
  23.6 1.9 %collective-permute-start = (bf16[192,512]{1,0:T(8,128)(2,1)S(1)}, bf16[192,512]{1,0:T(8,128)(2,1)S(1)}, u32[]{:S(2)}, u32[]{:S(2)}) collective-permute-start(bf16[192,512]{1,0:T(8,128)(2,1)S(1)} %get-tuple-element.32), channel_id=1, source_target_pairs={{0,64},{64,0},{128,192},{192,128},{256,320},{320,256},{384,448},{4... | collective-permute-start | bytes 589832 | tf_op jit(solution)/shard_map/ppermute | solution.py:55
  25.5 4.9 %collective-permute-start.1 = (bf16[192,512]{1,0:T(8,128)(2,1)S(1)}, bf16[192,512]{1,0:T(8,128)(2,1)S(1)}, u32[]{:S(2)}, u32[]{:S(2)}) collective-permute-start(bf16[192,512]{1,0:T(8,128)(2,1)S(1)} %get-tuple-element.33), channel_id=1, source_target_pairs={{0,384},{64,448},{128,0},{192,64},{256,128},{320,192},{384,256},{4... | collective-permute-start | bytes 589832 | tf_op jit(solution)/shard_map/ppermute | solution.py:55
  30.5 2.5 %collective-permute-start.2 = (bf16[192,512]{1,0:T(8,128)(2,1)S(1)}, bf16[192,512]{1,0:T(8,128)(2,1)S(1)}, u32[]{:S(2)}, u32[]{:S(2)}) collective-permute-start(bf16[192,512]{1,0:T(8,128)(2,1)S(1)} %get-tuple-element.34), channel_id=1, source_target_pairs={{0,448},{64,384},{128,64},{192,0},{256,192},{320,128},{384,320},{4... | collective-permute-start | bytes 589832 | tf_op jit(solution)/shard_map/ppermute | solution.py:55
  32.9 2.2 %collective-permute-start.3 = (bf16[192,512]{1,0:T(8,128)(2,1)S(1)}, bf16[192,512]{1,0:T(8,128)(2,1)S(1)}, u32[]{:S(2)}, u32[]{:S(2)}) collective-permute-start(bf16[192,512]{1,0:T(8,128)(2,1)S(1)} %get-tuple-element.35), channel_id=1, source_target_pairs={{0,256},{64,320},{128,384},{192,448},{256,0},{320,64},{384,128},{4... | collective-permute-start | bytes 589832 | tf_op jit(solution)/shard_map/ppermute | solution.py:55
  35.2 4.7 %collective-permute-start.4 = (bf16[192,512]{1,0:T(8,128)(2,1)S(1)}, bf16[192,512]{1,0:T(8,128)(2,1)S(1)}, u32[]{:S(2)}, u32[]{:S(2)}) collective-permute-start(bf16[192,512]{1,0:T(8,128)(2,1)S(1)} %get-tuple-element.36), channel_id=1, source_target_pairs={{0,320},{64,256},{128,448},{192,384},{256,64},{320,0},{384,192},{4... | collective-permute-start | bytes 589832 | tf_op jit(solution)/shard_map/ppermute | solution.py:55
  39.9 3.2 %collective-permute-start.5 = (bf16[192,512]{1,0:T(8,128)(2,1)S(1)}, bf16[192,512]{1,0:T(8,128)(2,1)S(1)}, u32[]{:S(2)}, u32[]{:S(2)}) collective-permute-start(bf16[192,512]{1,0:T(8,128)(2,1)S(1)} %get-tuple-element.37), channel_id=1, source_target_pairs={{0,128},{64,192},{128,256},{192,320},{256,384},{320,448},{384,0},{... | collective-permute-start | bytes 589832 | tf_op jit(solution)/shard_map/ppermute | solution.py:55
  43.1 2.0 %collective-permute-start.6 = (bf16[192,512]{1,0:T(8,128)(2,1)S(1)}, bf16[192,512]{1,0:T(8,128)(2,1)S(1)}, u32[]{:S(2)}, u32[]{:S(2)}) collective-permute-start(bf16[192,512]{1,0:T(8,128)(2,1)S(1)} %get-tuple-element.38), channel_id=1, source_target_pairs={{0,192},{64,128},{128,320},{192,256},{256,448},{320,384},{384,64},... | collective-permute-start | bytes 589832 | tf_op jit(solution)/shard_map/ppermute | solution.py:55
  45.2 2.8 %collective-permute-done.2.refs_3_ = bf16[192,512]{1,0:T(8,128)(2,1)S(1)} collective-permute-done((bf16[192,512]{1,0:T(8,128)(2,1)S(1)}, bf16[192,512]{1,0:T(8,128)(2,1)S(1)}, u32[]{:S(2)}, u32[]{:S(2)}) %collective-permute-start.2) | collective-permute-done | bytes 196640 | tf_op jit(solution)/shard_map/ppermute | solution.py:55
  47.9 4.0 %collective-permute-done.5.refs_6_ = bf16[192,512]{1,0:T(8,128)(2,1)S(1)} collective-permute-done((bf16[192,512]{1,0:T(8,128)(2,1)S(1)}, bf16[192,512]{1,0:T(8,128)(2,1)S(1)}, u32[]{:S(2)}, u32[]{:S(2)}) %collective-permute-start.5) | collective-permute-done | bytes 196640 | tf_op jit(solution)/shard_map/ppermute | solution.py:55
  51.9 4.1 %collective-permute-done.6.refs_7_ = bf16[192,512]{1,0:T(8,128)(2,1)S(1)} collective-permute-done((bf16[192,512]{1,0:T(8,128)(2,1)S(1)}, bf16[192,512]{1,0:T(8,128)(2,1)S(1)}, u32[]{:S(2)}, u32[]{:S(2)}) %collective-permute-start.6) | collective-permute-done | bytes 196640 | tf_op jit(solution)/shard_map/ppermute | solution.py:55
  56.5 1.2 shard_map.113
  58.5 1.9 %collective-permute-start.7 = (bf16[5,192,384]{2,1,0:T(8,128)(2,1)S(1)}, bf16[5,192,384]{2,1,0:T(8,128)(2,1)S(1)}, u32[]{:S(2)}, u32[]{:S(2)}) collective-permute-start(bf16[5,192,384]{2,1,0:T(8,128)(2,1)S(1)} %get-tuple-element.40), channel_id=1, source_target_pairs={{0,64},{64,0},{128,192},{192,128},{256,320},{320,256},{384,448},{4... | collective-permute-start | bytes 2211848 | tf_op jit(solution)/shard_map/ppermute | solution.py:55
  60.4 2.2 %collective-permute-done.7.theirs_ref = bf16[5,192,384]{2,1,0:T(8,128)(2,1)S(1)} collective-permute-done((bf16[5,192,384]{2,1,0:T(8,128)(2,1)S(1)}, bf16[5,192,384]{2,1,0:T(8,128)(2,1)S(1)}, u32[]{:S(2)}, u32[]{:S(2)}) %collective-permute-start.7) | collective-permute-done | bytes 737312 | tf_op jit(solution)/shard_map/ppermute | solution.py:55
  62.8 27.4 %all_to_all.20.all_ref = bf16[4,3,192,384]{3,2,1,0:T(8,128)(2,1)S(1)} all-to-all(bf16[4,3,192,384]{3,2,1,0:T(8,128)(2,1)S(1)} %shard_map.114), channel_id=1, replica_groups={{0,128,256,384},{64,192,320,448},{1,129,257,385},{65,193,321,449},{2,13..., dimensions={0} | all-to-all | bytes 3538944 | tf_op jit(solution)/shard_map/all_to_all | solution.py:60
  90.2 2.0 %shard_map.115 = bf16[2304,128]{1,0:T(8,128)(2,1)} custom-call(s32[1]{0:T(128)} %bitcast.here_ref, bf16[4,3,192,384]{3,2,1,0:T(8,128)(2,1)S(1)} %all_to_all.20.all_ref, bf16[192,512]{1,0:T(8,128)(2,1)S(1)} %get-tuple-element.31.refs_0_, bf16[192,512]{1,0:T(8,128)(2,1)S(1)} %collective-permute-done.refs_1_, ...), custom_call_target="tpu_custom_call" | custom-call | flops 603979776 | bytes 1048576 | tf_op jit(solution)/shard_map/pallas_call | solution.py:302
  92.1 13.2 %all-to-all-start.2 = ((bf16[64,9,4,128]{3,2,1,0:T(4,128)(2,1)}), bf16[64,9,4,128]{3,2,1,0:T(4,128)(2,1)S(1)}, u32[]{:S(2)}, u32[]{:S(2)}) async-start(bf16[64,9,4,128]{3,2,1,0:T(4,128)(2,1)} %bitcast.10), calls=%async_computation.2 | async-start | bytes 1179648 | tf_op jit(solution)/shard_map/all_to_all | solution.py:287
  107.3 2.1 %collective-permute-start.8 = (bf16[192,512]{1,0:T(8,128)(2,1)S(1)}, bf16[192,512]{1,0:T(8,128)(2,1)S(1)}, u32[]{:S(2)}, u32[]{:S(2)}) collective-permute-start(bf16[192,512]{1,0:T(8,128)(2,1)S(1)} %get-tuple-element.43), channel_id=1, source_target_pairs={{0,64},{64,0},{128,192},{192,128},{256,320},{320,256},{384,448},{4... | collective-permute-start | bytes 589832 | tf_op jit(solution)/shard_map/ppermute | solution.py:55
  109.4 2.5 %collective-permute-start.9 = (bf16[192,512]{1,0:T(8,128)(2,1)S(1)}, bf16[192,512]{1,0:T(8,128)(2,1)S(1)}, u32[]{:S(2)}, u32[]{:S(2)}) collective-permute-start(bf16[192,512]{1,0:T(8,128)(2,1)S(1)} %get-tuple-element.44), channel_id=1, source_target_pairs={{0,128},{64,192},{128,256},{192,320},{256,384},{320,448},{384,0},{... | collective-permute-start | bytes 589832 | tf_op jit(solution)/shard_map/ppermute | solution.py:55
  111.9 2.1 %collective-permute-start.10 = (bf16[192,512]{1,0:T(8,128)(2,1)S(1)}, bf16[192,512]{1,0:T(8,128)(2,1)S(1)}, u32[]{:S(2)}, u32[]{:S(2)}) collective-permute-start(bf16[192,512]{1,0:T(8,128)(2,1)S(1)} %get-tuple-element.45), channel_id=1, source_target_pairs={{0,192},{64,128},{128,320},{192,256},{256,448},{320,384},{384,64},... | collective-permute-start | bytes 589832 | tf_op jit(solution)/shard_map/ppermute | solution.py:55
  114.0 5.6 %collective-permute-start.11 = (bf16[192,512]{1,0:T(8,128)(2,1)S(1)}, bf16[192,512]{1,0:T(8,128)(2,1)S(1)}, u32[]{:S(2)}, u32[]{:S(2)}) collective-permute-start(bf16[192,512]{1,0:T(8,128)(2,1)S(1)} %get-tuple-element.46), channel_id=1, source_target_pairs={{0,256},{64,320},{128,384},{192,448},{256,0},{320,64},{384,128},{4... | collective-permute-start | bytes 589832 | tf_op jit(solution)/shard_map/ppermute | solution.py:55
  119.7 1.9 %collective-permute-start.12 = (bf16[192,512]{1,0:T(8,128)(2,1)S(1)}, bf16[192,512]{1,0:T(8,128)(2,1)S(1)}, u32[]{:S(2)}, u32[]{:S(2)}) collective-permute-start(bf16[192,512]{1,0:T(8,128)(2,1)S(1)} %get-tuple-element.47), channel_id=1, source_target_pairs={{0,320},{64,256},{128,448},{192,384},{256,64},{320,0},{384,192},{4... | collective-permute-start | bytes 589832 | tf_op jit(solution)/shard_map/ppermute | solution.py:55
  121.6 4.1 %collective-permute-start.13 = (bf16[192,512]{1,0:T(8,128)(2,1)S(1)}, bf16[192,512]{1,0:T(8,128)(2,1)S(1)}, u32[]{:S(2)}, u32[]{:S(2)}) collective-permute-start(bf16[192,512]{1,0:T(8,128)(2,1)S(1)} %get-tuple-element.48), channel_id=1, source_target_pairs={{0,384},{64,448},{128,0},{192,64},{256,128},{320,192},{384,256},{4... | collective-permute-start | bytes 589832 | tf_op jit(solution)/shard_map/ppermute | solution.py:55
  125.8 3.2 %collective-permute-start.14 = (bf16[192,512]{1,0:T(8,128)(2,1)S(1)}, bf16[192,512]{1,0:T(8,128)(2,1)S(1)}, u32[]{:S(2)}, u32[]{:S(2)}) collective-permute-start(bf16[192,512]{1,0:T(8,128)(2,1)S(1)} %get-tuple-element.49), channel_id=1, source_target_pairs={{0,448},{64,384},{128,64},{192,0},{256,192},{320,128},{384,320},{4... | collective-permute-start | bytes 589832 | tf_op jit(solution)/shard_map/ppermute | solution.py:55
  129.0 3.1 %collective-permute-done.10.refs_3_ = bf16[192,512]{1,0:T(8,128)(2,1)S(1)} collective-permute-done((bf16[192,512]{1,0:T(8,128)(2,1)S(1)}, bf16[192,512]{1,0:T(8,128)(2,1)S(1)}, u32[]{:S(2)}, u32[]{:S(2)}) %collective-permute-start.10) | collective-permute-done | bytes 196640 | tf_op jit(solution)/shard_map/ppermute | solution.py:55
  132.0 1.7 %collective-permute-done.13.refs_6_ = bf16[192,512]{1,0:T(8,128)(2,1)S(1)} collective-permute-done((bf16[192,512]{1,0:T(8,128)(2,1)S(1)}, bf16[192,512]{1,0:T(8,128)(2,1)S(1)}, u32[]{:S(2)}, u32[]{:S(2)}) %collective-permute-start.13) | collective-permute-done | bytes 196640 | tf_op jit(solution)/shard_map/ppermute | solution.py:55
  133.7 3.0 %collective-permute-done.14.refs_7_ = bf16[192,512]{1,0:T(8,128)(2,1)S(1)} collective-permute-done((bf16[192,512]{1,0:T(8,128)(2,1)S(1)}, bf16[192,512]{1,0:T(8,128)(2,1)S(1)}, u32[]{:S(2)}, u32[]{:S(2)}) %collective-permute-start.14) | collective-permute-done | bytes 196640 | tf_op jit(solution)/shard_map/ppermute | solution.py:55
  136.7 1.3 shard_map.117
  138.3 1.0 shard_map.118
  139.4 9.4 %all_to_all.21 = f32[8,8,128]{2,1,0:T(8,128)S(1)} all-to-all(f32[8,8,128]{2,1,0:T(8,128)S(1)} %get-tuple-element.55), channel_id=1, replica_groups=mesh['dp'=8,'expert'=64] {'dp'}, dimensions={0} | all-to-all | bytes 65536 | tf_op jit(solution)/shard_map/all_to_all | solution.py:324
  (26 shorter events, 4.5 us)
Async XLA Ops:
  3.3 53.2 %all-to-all-start = ((bf16[64,9,4,128]{3,2,1,0:T(4,128)(2,1)}), bf16[64,9,4,128]{3,2,1,0:T(4,128)(2,1)S(1)}, u32[]{:S(2)}, u32[]{:S(2)}) async-start(bf16[64,9,4,128]{3,2,1,0:T(4,128)(2,1)} %bitcast.24), calls=%async_computation | async-start | bytes 1179648 | tf_op jit(solution)/shard_map/all_to_all | solution.py:287
  22.1 1.4 copy-start
  23.6 16.3 %collective-permute-start = (bf16[192,512]{1,0:T(8,128)(2,1)S(1)}, bf16[192,512]{1,0:T(8,128)(2,1)S(1)}, u32[]{:S(2)}, u32[]{:S(2)}) collective-permute-start(bf16[192,512]{1,0:T(8,128)(2,1)S(1)} %get-tuple-element.32), channel_id=1, source_target_pairs={{0,64},{64,0},{128,192},{192,128},{256,320},{320,256},{384,448},{4... | collective-permute-start | bytes 589832 | tf_op jit(solution)/shard_map/ppermute | solution.py:55
  25.5 17.6 %collective-permute-start.1 = (bf16[192,512]{1,0:T(8,128)(2,1)S(1)}, bf16[192,512]{1,0:T(8,128)(2,1)S(1)}, u32[]{:S(2)}, u32[]{:S(2)}) collective-permute-start(bf16[192,512]{1,0:T(8,128)(2,1)S(1)} %get-tuple-element.33), channel_id=1, source_target_pairs={{0,384},{64,448},{128,0},{192,64},{256,128},{320,192},{384,256},{4... | collective-permute-start | bytes 589832 | tf_op jit(solution)/shard_map/ppermute | solution.py:55
  30.5 17.5 %collective-permute-start.2 = (bf16[192,512]{1,0:T(8,128)(2,1)S(1)}, bf16[192,512]{1,0:T(8,128)(2,1)S(1)}, u32[]{:S(2)}, u32[]{:S(2)}) collective-permute-start(bf16[192,512]{1,0:T(8,128)(2,1)S(1)} %get-tuple-element.34), channel_id=1, source_target_pairs={{0,448},{64,384},{128,64},{192,0},{256,192},{320,128},{384,320},{4... | collective-permute-start | bytes 589832 | tf_op jit(solution)/shard_map/ppermute | solution.py:55
  32.9 15.0 %collective-permute-start.3 = (bf16[192,512]{1,0:T(8,128)(2,1)S(1)}, bf16[192,512]{1,0:T(8,128)(2,1)S(1)}, u32[]{:S(2)}, u32[]{:S(2)}) collective-permute-start(bf16[192,512]{1,0:T(8,128)(2,1)S(1)} %get-tuple-element.35), channel_id=1, source_target_pairs={{0,256},{64,320},{128,384},{192,448},{256,0},{320,64},{384,128},{4... | collective-permute-start | bytes 589832 | tf_op jit(solution)/shard_map/ppermute | solution.py:55
  35.2 12.7 %collective-permute-start.4 = (bf16[192,512]{1,0:T(8,128)(2,1)S(1)}, bf16[192,512]{1,0:T(8,128)(2,1)S(1)}, u32[]{:S(2)}, u32[]{:S(2)}) collective-permute-start(bf16[192,512]{1,0:T(8,128)(2,1)S(1)} %get-tuple-element.36), channel_id=1, source_target_pairs={{0,320},{64,256},{128,448},{192,384},{256,64},{320,0},{384,192},{4... | collective-permute-start | bytes 589832 | tf_op jit(solution)/shard_map/ppermute | solution.py:55
  39.9 12.0 %collective-permute-start.5 = (bf16[192,512]{1,0:T(8,128)(2,1)S(1)}, bf16[192,512]{1,0:T(8,128)(2,1)S(1)}, u32[]{:S(2)}, u32[]{:S(2)}) collective-permute-start(bf16[192,512]{1,0:T(8,128)(2,1)S(1)} %get-tuple-element.37), channel_id=1, source_target_pairs={{0,128},{64,192},{128,256},{192,320},{256,384},{320,448},{384,0},{... | collective-permute-start | bytes 589832 | tf_op jit(solution)/shard_map/ppermute | solution.py:55
  43.1 12.9 %collective-permute-start.6 = (bf16[192,512]{1,0:T(8,128)(2,1)S(1)}, bf16[192,512]{1,0:T(8,128)(2,1)S(1)}, u32[]{:S(2)}, u32[]{:S(2)}) collective-permute-start(bf16[192,512]{1,0:T(8,128)(2,1)S(1)} %get-tuple-element.38), channel_id=1, source_target_pairs={{0,192},{64,128},{128,320},{192,256},{256,448},{320,384},{384,64},... | collective-permute-start | bytes 589832 | tf_op jit(solution)/shard_map/ppermute | solution.py:55
  57.7 0.7 copy-start.4
  58.5 4.1 %collective-permute-start.7 = (bf16[5,192,384]{2,1,0:T(8,128)(2,1)S(1)}, bf16[5,192,384]{2,1,0:T(8,128)(2,1)S(1)}, u32[]{:S(2)}, u32[]{:S(2)}) collective-permute-start(bf16[5,192,384]{2,1,0:T(8,128)(2,1)S(1)} %get-tuple-element.40), channel_id=1, source_target_pairs={{0,64},{64,0},{128,192},{192,128},{256,320},{320,256},{384,448},{4... | collective-permute-start | bytes 2211848 | tf_op jit(solution)/shard_map/ppermute | solution.py:55
  92.1 46.2 %all-to-all-start.2 = ((bf16[64,9,4,128]{3,2,1,0:T(4,128)(2,1)}), bf16[64,9,4,128]{3,2,1,0:T(4,128)(2,1)S(1)}, u32[]{:S(2)}, u32[]{:S(2)}) async-start(bf16[64,9,4,128]{3,2,1,0:T(4,128)(2,1)} %bitcast.10), calls=%async_computation.2 | async-start | bytes 1179648 | tf_op jit(solution)/shard_map/all_to_all | solution.py:287
  105.3 1.0 copy-start.5
  107.3 31.0 %copy-start.1 = (bf16[16,8,192]{2,1,0:T(8,128)(2,1)S(1)}, bf16[16,8,192]{2,1,0:T(8,128)(2,1)}, u32[]{:S(2)}) copy-start(bf16[16,8,192]{2,1,0:T(8,128)(2,1)} %param.8) | copy-start | bytes 147460
  107.3 31.0 %copy-start.2 = (s32[128,1]{1,0:T(8,128)S(1)}, s32[128,1]{1,0:T(8,128)}, u32[]{:S(2)}) copy-start(s32[128,1]{1,0:T(8,128)} %get-tuple-element.51.slot_ref) | copy-start | bytes 1540
  107.3 31.0 %copy-start.3 = (f32[16,8]{0,1:T(8,128)S(1)}, f32[16,8]{0,1:T(8,128)}, u32[]{:S(2)}) copy-start(f32[16,8]{0,1:T(8,128)} %param.10) | copy-start | bytes 1540
  107.3 14.3 %collective-permute-start.8 = (bf16[192,512]{1,0:T(8,128)(2,1)S(1)}, bf16[192,512]{1,0:T(8,128)(2,1)S(1)}, u32[]{:S(2)}, u32[]{:S(2)}) collective-permute-start(bf16[192,512]{1,0:T(8,128)(2,1)S(1)} %get-tuple-element.43), channel_id=1, source_target_pairs={{0,64},{64,0},{128,192},{192,128},{256,320},{320,256},{384,448},{4... | collective-permute-start | bytes 589832 | tf_op jit(solution)/shard_map/ppermute | solution.py:55
  109.4 16.4 %collective-permute-start.9 = (bf16[192,512]{1,0:T(8,128)(2,1)S(1)}, bf16[192,512]{1,0:T(8,128)(2,1)S(1)}, u32[]{:S(2)}, u32[]{:S(2)}) collective-permute-start(bf16[192,512]{1,0:T(8,128)(2,1)S(1)} %get-tuple-element.44), channel_id=1, source_target_pairs={{0,128},{64,192},{128,256},{192,320},{256,384},{320,448},{384,0},{... | collective-permute-start | bytes 589832 | tf_op jit(solution)/shard_map/ppermute | solution.py:55
  111.9 20.2 %collective-permute-start.10 = (bf16[192,512]{1,0:T(8,128)(2,1)S(1)}, bf16[192,512]{1,0:T(8,128)(2,1)S(1)}, u32[]{:S(2)}, u32[]{:S(2)}) collective-permute-start(bf16[192,512]{1,0:T(8,128)(2,1)S(1)} %get-tuple-element.45), channel_id=1, source_target_pairs={{0,192},{64,128},{128,320},{192,256},{256,448},{320,384},{384,64},... | collective-permute-start | bytes 589832 | tf_op jit(solution)/shard_map/ppermute | solution.py:55
  114.0 18.0 %collective-permute-start.11 = (bf16[192,512]{1,0:T(8,128)(2,1)S(1)}, bf16[192,512]{1,0:T(8,128)(2,1)S(1)}, u32[]{:S(2)}, u32[]{:S(2)}) collective-permute-start(bf16[192,512]{1,0:T(8,128)(2,1)S(1)} %get-tuple-element.46), channel_id=1, source_target_pairs={{0,256},{64,320},{128,384},{192,448},{256,0},{320,64},{384,128},{4... | collective-permute-start | bytes 589832 | tf_op jit(solution)/shard_map/ppermute | solution.py:55
  119.7 12.4 %collective-permute-start.12 = (bf16[192,512]{1,0:T(8,128)(2,1)S(1)}, bf16[192,512]{1,0:T(8,128)(2,1)S(1)}, u32[]{:S(2)}, u32[]{:S(2)}) collective-permute-start(bf16[192,512]{1,0:T(8,128)(2,1)S(1)} %get-tuple-element.47), channel_id=1, source_target_pairs={{0,320},{64,256},{128,448},{192,384},{256,64},{320,0},{384,192},{4... | collective-permute-start | bytes 589832 | tf_op jit(solution)/shard_map/ppermute | solution.py:55
  121.6 12.1 %collective-permute-start.13 = (bf16[192,512]{1,0:T(8,128)(2,1)S(1)}, bf16[192,512]{1,0:T(8,128)(2,1)S(1)}, u32[]{:S(2)}, u32[]{:S(2)}) collective-permute-start(bf16[192,512]{1,0:T(8,128)(2,1)S(1)} %get-tuple-element.48), channel_id=1, source_target_pairs={{0,384},{64,448},{128,0},{192,64},{256,128},{320,192},{384,256},{4... | collective-permute-start | bytes 589832 | tf_op jit(solution)/shard_map/ppermute | solution.py:55
  125.8 10.9 %collective-permute-start.14 = (bf16[192,512]{1,0:T(8,128)(2,1)S(1)}, bf16[192,512]{1,0:T(8,128)(2,1)S(1)}, u32[]{:S(2)}, u32[]{:S(2)}) collective-permute-start(bf16[192,512]{1,0:T(8,128)(2,1)S(1)} %get-tuple-element.49), channel_id=1, source_target_pairs={{0,448},{64,384},{128,64},{192,0},{256,192},{320,128},{384,320},{4... | collective-permute-start | bytes 589832 | tf_op jit(solution)/shard_map/ppermute | solution.py:55

commit v4 on v3

--- a/solution.py
+++ b/solution.py
@@ -1,3 +1,5 @@
+import functools
+
 import jax
 import jax.numpy as jnp
 from jax import lax
@@ -64,28 +66,27 @@
     return lax.rem(here // 2 + step, NY)
 
 
-def peer_column(here, step, other, width):
-    peer = chip(here, step) * 2 + lax.rem(lax.rem(here, 2) + other, 2)
-    return pl.multiple_of(peer * width, width)
+def chip_columns(here, step, width):
+    return pl.ds(pl.multiple_of(chip(here, step) * width, width), width)
+
+
+def core_columns(here, other, width):
+    core = lax.rem(lax.rem(here, 2) + other, 2)
+    return pl.ds(pl.multiple_of(core * width, width), width)
 
 
 def cut_weights(here_ref, w_ref, *outs):
     width = outs[0].shape[1]
-    here = here_ref[0]
-    for step in range(NY):
-        for other in range(2):
-            at = peer_column(here, step, other, width)
-            outs[2 * step + other][...] = w_ref[:, pl.ds(at, width)]
+    for step in range(NY):
+        outs[step][...] = w_ref[:, chip_columns(here_ref[0], step, width)]
 
 
 def join_gradient(here_ref, *refs):
     parts, out_ref = refs[:-1], refs[-1]
     width = parts[0].shape[1]
-    here = here_ref[0]
-    for step in range(NY):
-        for other in range(2):
-            at = peer_column(here, (NY - step) % NY, other, width)
-            out_ref[:, pl.ds(at, width)] = parts[2 * step + other][...]
+    for step in range(NY):
+        columns = chip_columns(here_ref[0], (NY - step) % NY, width)
+        out_ref[:, columns] = parts[step][...]
 
 
 def column(stored):
@@ -179,48 +180,48 @@
     sent_ref[...] = rows_ref[...].astype(BF)
 
 
-def backward(here_ref, got_ref, *refs):
-    w_refs, (mine_ref, theirs_ref, grad_ref, rows_ref, flat_ref) = refs[:-5], refs[-5:]
-    feats, hidden = grad_ref.shape[1], mine_ref.shape[1]
+def arrive(got_ref, grad_ref, act_ref, rows_ref, flat_ref):
     rows_ref[...] = got_ref[...].astype(F32)
-    grad, acts = unpack(rows_ref, flat_ref, feats, hidden)
-    acts = acts.T.astype(BF)
-    mine_ref[NY] = acts
-    theirs_ref[NY] = acts
-    grad = grad.astype(BF)
-    grad_ref[...] = grad
-    for step in range(NY):
-        at = chip(here_ref[0], step)
-        mine_ref[at] = dot(w_refs[2 * step][...], grad, 1, 1).astype(BF)
-        theirs_ref[at] = dot(w_refs[2 * step + 1][...], grad, 1, 1).astype(BF)
-
-
-def add_cores(mine_ref, theirs_ref, out_ref):
-    for y in range(NY):
-        out_ref[y, 0] = mine_ref[NY]
-        out_ref[y, 1] = theirs_ref[NY]
-        out_ref[y, 2] = (mine_ref[y].astype(F32) + theirs_ref[y].astype(F32)).astype(BF)
-
-
-def forward(here_ref, all_ref, *refs):
-    w_refs, (sent_ref, rows_ref, flat_ref) = refs[:-3], refs[-3:]
+    grad, acts = unpack(rows_ref, flat_ref, grad_ref.shape[1], act_ref.shape[0])
+    grad_ref[...] = grad.astype(BF)
+    act_ref[...] = acts.T.astype(BF)
+
+
+def backward(here_ref, act_ref, near_ref, far_ref, *refs):
+    w_refs, out_ref = refs[:-1], refs[-1]
+    here, feats = here_ref[0], near_ref.shape[1]
+    near, far = core_columns(here, 0, feats), core_columns(here, 1, feats)
+    for step in range(NY):
+        at, w_ref = chip(here, step), w_refs[step]
+        part = dot(w_ref[:, near], near_ref[...], 1, 1) + dot(w_ref[:, far], far_ref[...], 1, 1)
+        out_ref[at, 0] = act_ref[...]
+        out_ref[at, 1] = part.astype(BF)
+
+
+def forward(other, here_ref, all_ref, *refs):
+    w_refs, out_ref = refs[:-1], refs[-1]
+    here = here_ref[0]
+    columns = core_columns(here, other, out_ref.shape[1])
     total = None
     for step in range(NY):
-        at = chip(here_ref[0], step)
-        for other in range(2):
-            part = dot(all_ref[at, other], w_refs[2 * step + other][...], 0, 0)
-            total = part if total is None else total + part
-    back = sum(all_ref[y, 2].astype(F32) for y in range(NY))
-    pack(rows_ref, flat_ref, total, back.T)
+        part = dot(all_ref[chip(here, step), 0], w_refs[step][:, columns], 0, 0)
+        total = part if total is None else total + part
+    out_ref[...] = total.astype(out_ref.dtype)
+
+
+def leave(all_ref, own_ref, swapped_ref, sent_ref, rows_ref, flat_ref):
+    back = sum(all_ref[y, 1].astype(F32) for y in range(NY))
+    pack(rows_ref, flat_ref, own_ref[...] + swapped_ref[...].astype(F32), back.T)
     sent_ref[...] = rows_ref[...].astype(BF)
 
 
-def weights_back(here_ref, all_ref, grad_ref, *outs):
-    grad = grad_ref[...]
-    for step in range(NY):
-        at = chip(here_ref[0], step)
-        for other in range(2):
-            outs[2 * step + other][...] = dot(all_ref[at, other], grad, 1, 0).astype(BF)
+def weights_back(here_ref, all_ref, near_ref, far_ref, *outs):
+    here, feats = here_ref[0], near_ref.shape[1]
+    near, far = core_columns(here, 0, feats), core_columns(here, 1, feats)
+    for step in range(NY):
+        acts = all_ref[chip(here, step), 0]
+        outs[step][:, near] = dot(acts, near_ref[...], 1, 0).astype(BF)
+        outs[step][:, far] = dot(acts, far_ref[...], 1, 0).astype(BF)
 
 
 def collect(got_ref, slot_ref, gate_ref, act_ref, mixed_ref, back_ref, gate_out_ref, rows_ref, flat_ref):
@@ -257,16 +258,10 @@
     ]
     here = lax.axis_index("dp").astype(jnp.int32).reshape(1)
     gates_t = gates.T
-    pieces_shape = [shape((hidden, feats))] * (2 * NY)
+    pieces_shape = [shape((hidden, 2 * feats))] * NY
 
     cuts = call(cut_weights, pieces_shape, [SM, VM], moved=3 << 20)(here, w_down[0])
-    weights = [None] * (2 * NY)
-    for step in range(NY):
-        for other in range(2):
-            piece = cuts[2 * step + other]
-            if step or other:
-                piece = send(piece, step, other)
-            weights[2 * ((NY - step) % NY) + other] = piece
+    weights = [cuts[0]] + [send(cuts[NY - step], NY - step, 0) for step in range(1, NY)]
 
     inputs = (
         expert_ids.T, replica_pick.T, placement.T, group_cap.reshape(1, n_dev),
@@ -287,31 +282,34 @@
         return lax.all_to_all(value, "expert", 0, 0, tiled=True).reshape(payload.shape)
 
     got = exchange(sent)
-    stack = shape((NY + 1, hidden, slots))
     flops = 2 * slots * feats * hidden * 2 * NY
-    mine, theirs, grad = call(
-        backward,
-        [stack, stack, shape((slots, feats))],
-        [SM] + [VM] * (1 + 2 * NY),
-        flops=flops,
-        scratch=scratch,
-    )(here, got, *weights)
-    theirs = send(theirs, 0, 1)
-    shared = call(add_cores, shape((NY, 3, hidden, slots)), [VM] * 2)(mine, theirs)
+    grad, own_act = call(
+        arrive, [shape((slots, feats)), shape((hidden, slots))], [VM], scratch=scratch
+    )(got)
+    far_grad = send(grad, 0, 1)
+    shared = call(
+        backward, shape((NY, 2, hidden, slots)), [SM] + [VM] * (3 + NY), flops=flops
+    )(here, own_act, grad, far_grad, *weights)
     shared = exchange_y(shared)
-    returned = call(forward, payload, [SM] + [VM] * (1 + 2 * NY), flops=flops, scratch=scratch)(
-        here, shared, *weights
-    )
+
+    def part(other, dtype):
+        return call(
+            functools.partial(forward, other),
+            shape((slots, feats), dtype),
+            [SM] + [VM] * (1 + NY),
+            flops=flops // 2,
+        )(here, shared, *weights)
+
+    swapped = send(part(1, BF), 0, 1)
+    returned = call(leave, payload, [VM] * 3, scratch=scratch)(shared, part(0, F32), swapped)
     home = exchange(returned)
 
-    pieces = call(weights_back, pieces_shape, [SM] + [VM] * 2, flops=flops)(here, shared, grad)
-    joined = []
-    for step in range(NY):
-        for other in range(2):
-            piece = pieces[2 * step + other]
-            joined.append(send(piece, step, other) if step or other else piece)
+    pieces = call(weights_back, pieces_shape, [SM] + [VM] * 3, flops=flops)(
+        here, shared, grad, far_grad
+    )
+    joined = [pieces[0]] + [send(pieces[step], step, 0) for step in range(1, NY)]
     weight_grad = call(
-        join_gradient, shape((hidden, 2 * NY * feats)), [SM] + [VM] * (2 * NY), moved=3 << 20
+        join_gradient, shape((hidden, 2 * NY * feats)), [SM] + [VM] * NY, moved=3 << 20
     )(here, *joined)
 
     home, weight_grad = lax.optimization_barrier((home, weight_grad))

time: 151 us -> 140 us (0.927)
  starting transfers between devices: 76.9 us -> 48.9 us
  waiting for transfers between devices: 21.5 us -> 47.8 us
  blocking collectives: 36.8 us -> 28.9 us
  local copies, waits for them, and re-layouts: 3.75 us -> 2.01 us
    all_to_all x2, waiting for transfers between devices: 0.78 us -> 29.6 us  [exchange(): lax.all_to_all(value, 'expert', 0, 0, tiled=True).reshape(payload.shape)]
    ppermute x15 -> x8, starting transfers between devices: 45 us -> 23.3 us  [send(): return lax.ppermute(value, 'dp', pairs)]
    all_to_all x2, starting transfers between devices: 32 us -> 25.6 us  [exchange(): lax.all_to_all(value, 'expert', 0, 0, tiled=True).reshape(payload.shape)]
    all_to_all x1, blocking collectives: 27.4 us -> 21.1 us  [exchange_y(): lax.all_to_all(value, 'dp', 0, 0, axis_index_groups=groups, tiled=True)]
    ppermute x15 -> x8, waiting for transfers between devices: 20.8 us -> 18.2 us  [send(): return lax.ppermute(value, 'dp', pairs)]
    unnamed x12 -> x8, local copies, waits for them, and re-layouts: 3.15 us -> 1.41 us
    all_to_all x1, blocking collectives: 9.42 us -> 7.8 us  [on_device(): gate_parts = lax.all_to_all(gate_parts, 'dp', 0, 0, tiled=True)]
    pallas_call x5 -> x7, Pallas kernels: 5.68 us -> 6.04 us  [the longest x1 1.26 us: on_device(): call(join_gradient, shape((hidden, 2 * NY * feats)), [SM] + [VM] * NY, mo...]
  transfers between devices with their start and end apart: 17 -> 10, of which waited for: 9 -> 6; matrix products, arithmetic and copies ran while one was open for 0% -> 0% of each run, Pallas kernels for 2% -> 3%
where the time goes in v4:
time: 140 us; the launch traced here: 139 us
  starting transfers between devices  48.9 us (35%)
  waiting for transfers between devices  47.8 us (34%)
  blocking collectives  28.9 us (21%)
  Pallas kernels  10.7 us (8%)
  local copies, waits for them, and re-layouts  2.01 us (1%)
    all_to_all x2, waiting for transfers between devices, exchange(): lax.all_to_all(value, 'expert', 0, 0, tiled=True).reshape(payload.shape)  29.6 us
    all_to_all x2, starting transfers between devices, exchange(): lax.all_to_all(value, 'expert', 0, 0, tiled=True).reshape(payload.shape)  25.6 us
    ppermute x8, starting transfers between devices, send(): return lax.ppermute(value, 'dp', pairs)  23.3 us
    all_to_all x1, blocking collectives, exchange_y(): lax.all_to_all(value, 'dp', 0, 0, axis_index_groups=groups, tiled=True)  21.1 us
    ppermute x8, waiting for transfers between devices, send(): return lax.ppermute(value, 'dp', pairs)  18.2 us
    all_to_all x1, blocking collectives, on_device(): gate_parts = lax.all_to_all(gate_parts, 'dp', 0, 0, tiled=True)  7.8 us
  transfers between devices with their start and end apart: 10, of which 6 were waited for; matrix products, arithmetic and copies ran while one was open for 0% of the time, Pallas kernels for 3%

profile of v4, /device:TPU:6, one launch (start us, length us, event | category | flops | bytes accessed | tf_op | source)
XLA Modules:
  0.0 139.1 jit_solution(4902950286895130487)
XLA Ops:
  0.6 2.6 %shard_map.111 = (bf16[2304,128]{1,0:T(8,128)(2,1)}, s32[128,1]{1,0:T(8,128)}) custom-call(s32[8,16]{1,0:T(8,128)} %bitcast.25, s32[8,16]{1,0:T(8,128)} %bitcast.26, s32[2,16]{1,0:T(2,128)} %bitcast.27, s32[1,64]{1,0:T(1,128)} %bitcast.28, bf16[128,192]{1,0:T(8,128)(2,1)} %bitcast.19, bf16[16,512]{1,0:T(8,128)(2,1)} %cot_hbm.1, f32[8,16]{1,0:T(8,128)} %bitcast.21), custom_call_target="tpu_custom_call" | custom-call | bytes 1048576 | tf_op jit(solution)/shard_map/pallas_call | solution.py:270
  3.3 18.8 %all-to-all-start = ((bf16[64,9,4,128]{3,2,1,0:T(4,128)(2,1)}), bf16[64,9,4,128]{3,2,1,0:T(4,128)(2,1)S(1)}, u32[]{:S(2)}, u32[]{:S(2)}) async-start(bf16[64,9,4,128]{3,2,1,0:T(4,128)(2,1)} %bitcast.24), calls=%async_computation | async-start | bytes 1179648 | tf_op jit(solution)/shard_map/all_to_all | solution.py:282
  22.1 0.0 copy-start
  22.1 1.4 %copy-done = bf16[1,192,4096]{2,1,0:T(8,128)(2,1)S(1)} copy-done((bf16[1,192,4096]{2,1,0:T(8,128)(2,1)S(1)}, bf16[1,192,4096]{2,1,0:T(8,128)(2,1)}, u32[]{:S(2)}) %copy-start) | copy-done | bytes 1572888
  23.5 1.0 shard_map.113
  24.5 4.9 %collective-permute-start.1 = (bf16[192,1024]{1,0:T(8,128)(2,1)}, bf16[192,1024]{1,0:T(8,128)(2,1)S(1)}, u32[]{:S(2)}, u32[]{:S(2)}) collective-permute-start(bf16[192,1024]{1,0:T(8,128)(2,1)} %get-tuple-element.25), channel_id=1, source_target_pairs={{0,384},{64,448},{128,0},{192,64},{256,128},{320,192},{384,256},{4... | collective-permute-start | bytes 1179656 | tf_op jit(solution)/shard_map/ppermute | solution.py:57
  29.4 2.5 %collective-permute-start.2 = (bf16[192,1024]{1,0:T(8,128)(2,1)}, bf16[192,1024]{1,0:T(8,128)(2,1)S(1)}, u32[]{:S(2)}, u32[]{:S(2)}) collective-permute-start(bf16[192,1024]{1,0:T(8,128)(2,1)} %get-tuple-element.26), channel_id=1, source_target_pairs={{0,256},{64,320},{128,384},{192,448},{256,0},{320,64},{384,128},{4... | collective-permute-start | bytes 1179656 | tf_op jit(solution)/shard_map/ppermute | solution.py:57
  31.9 2.9 %collective-permute-start.3 = (bf16[192,1024]{1,0:T(8,128)(2,1)S(1)}, bf16[192,1024]{1,0:T(8,128)(2,1)S(1)}, u32[]{:S(2)}, u32[]{:S(2)}) collective-permute-start(bf16[192,1024]{1,0:T(8,128)(2,1)S(1)} %get-tuple-element.27), channel_id=1, source_target_pairs={{0,128},{64,192},{128,256},{192,320},{256,384},{320,448},{384,0},{... | collective-permute-start | bytes 1179656 | tf_op jit(solution)/shard_map/ppermute | solution.py:57
  34.8 21.6 %all-to-all-done = bf16[64,9,4,128]{3,2,1,0:T(4,128)(2,1)S(1)} async-done(((bf16[64,9,4,128]{3,2,1,0:T(4,128)(2,1)}), bf16[64,9,4,128]{3,2,1,0:T(4,128)(2,1)S(1)}, u32[]{:S(2)}, u32[]{:S(2)}) %all-to-all-start) | async-done | bytes 589856 | tf_op jit(solution)/shard_map/all_to_all | solution.py:282
  56.5 0.3 shard_map.112
  56.7 1.9 %collective-permute-start = (bf16[384,512]{1,0:T(8,128)(2,1)S(1)}, bf16[384,512]{1,0:T(8,128)(2,1)S(1)}, u32[]{:S(2)}, u32[]{:S(2)}) collective-permute-start(bf16[384,512]{1,0:T(8,128)(2,1)S(1)} %get-tuple-element.23.near_ref), channel_id=1, source_target_pairs={{0,64},{64,0},{128,192},{192,128},{256,320},{320,256},{384,448},{4... | collective-permute-start | bytes 1179656 | tf_op jit(solution)/shard_map/ppermute | solution.py:57
  58.7 0.0 collective-permute-done.1.refs_1_
  58.7 1.7 %collective-permute-done.far_ref = bf16[384,512]{1,0:T(8,128)(2,1)S(1)} collective-permute-done((bf16[384,512]{1,0:T(8,128)(2,1)S(1)}, bf16[384,512]{1,0:T(8,128)(2,1)S(1)}, u32[]{:S(2)}, u32[]{:S(2)}) %collective-permute-start) | collective-permute-done | bytes 393248 | tf_op jit(solution)/shard_map/ppermute | solution.py:57
  60.4 1.2 shard_map.114
  61.5 21.1 %all_to_all.20.all_ref = bf16[4,2,192,384]{3,2,1,0:T(8,128)(2,1)S(1)} all-to-all(bf16[4,2,192,384]{3,2,1,0:T(8,128)(2,1)S(1)} %shard_map.114), channel_id=1, replica_groups={{0,128,256,384},{64,192,320,448},{1,129,257,385},{65,193,321,449},{2,13..., dimensions={0} | all-to-all | bytes 2359296 | tf_op jit(solution)/shard_map/all_to_all | solution.py:62
  82.6 0.6 shard_map.116
  83.2 1.9 %collective-permute-start.4 = (bf16[384,512]{1,0:T(8,128)(2,1)S(1)}, bf16[384,512]{1,0:T(8,128)(2,1)S(1)}, u32[]{:S(2)}, u32[]{:S(2)}) collective-permute-start(bf16[384,512]{1,0:T(8,128)(2,1)S(1)} %shard_map.116), channel_id=1, source_target_pairs={{0,64},{64,0},{128,192},{192,128},{256,320},{320,256},{384,448},{4... | collective-permute-start | bytes 1179656 | tf_op jit(solution)/shard_map/ppermute | solution.py:57
  85.1 0.6 shard_map.115.own_ref
  85.7 1.1 collective-permute-done.4.swapped_ref
  86.8 1.1 shard_map.117
  88.0 6.8 %all-to-all-start.2 = ((bf16[64,9,4,128]{3,2,1,0:T(4,128)(2,1)}), bf16[64,9,4,128]{3,2,1,0:T(4,128)(2,1)S(1)}, u32[]{:S(2)}, u32[]{:S(2)}) async-start(bf16[64,9,4,128]{3,2,1,0:T(4,128)(2,1)} %bitcast.10), calls=%async_computation.2 | async-start | bytes 1179648 | tf_op jit(solution)/shard_map/all_to_all | solution.py:282
  94.8 1.0 shard_map.118
  95.7 2.5 %collective-permute-start.5 = (bf16[192,1024]{1,0:T(8,128)(2,1)S(1)}, bf16[192,1024]{1,0:T(8,128)(2,1)S(1)}, u32[]{:S(2)}, u32[]{:S(2)}) collective-permute-start(bf16[192,1024]{1,0:T(8,128)(2,1)S(1)} %get-tuple-element.29), channel_id=1, source_target_pairs={{0,128},{64,192},{128,256},{192,320},{256,384},{320,448},{384,0},{... | collective-permute-start | bytes 1179656 | tf_op jit(solution)/shard_map/ppermute | solution.py:57
  98.2 4.0 %collective-permute-start.6 = (bf16[192,1024]{1,0:T(8,128)(2,1)S(1)}, bf16[192,1024]{1,0:T(8,128)(2,1)S(1)}, u32[]{:S(2)}, u32[]{:S(2)}) collective-permute-start(bf16[192,1024]{1,0:T(8,128)(2,1)S(1)} %get-tuple-element.30), channel_id=1, source_target_pairs={{0,256},{64,320},{128,384},{192,448},{256,0},{320,64},{384,128},{4... | collective-permute-start | bytes 1179656 | tf_op jit(solution)/shard_map/ppermute | solution.py:57
  102.2 2.7 %collective-permute-start.7 = (bf16[192,1024]{1,0:T(8,128)(2,1)S(1)}, bf16[192,1024]{1,0:T(8,128)(2,1)S(1)}, u32[]{:S(2)}, u32[]{:S(2)}) collective-permute-start(bf16[192,1024]{1,0:T(8,128)(2,1)S(1)} %get-tuple-element.31), channel_id=1, source_target_pairs={{0,384},{64,448},{128,0},{192,64},{256,128},{320,192},{384,256},{4... | collective-permute-start | bytes 1179656 | tf_op jit(solution)/shard_map/ppermute | solution.py:57
  104.9 12.9 %collective-permute-done.5.refs_1_ = bf16[192,1024]{1,0:T(8,128)(2,1)S(1)} collective-permute-done((bf16[192,1024]{1,0:T(8,128)(2,1)S(1)}, bf16[192,1024]{1,0:T(8,128)(2,1)S(1)}, u32[]{:S(2)}, u32[]{:S(2)}) %collective-permute-start.5) | collective-permute-done | bytes 393248 | tf_op jit(solution)/shard_map/ppermute | solution.py:57
  117.9 2.5 %collective-permute-done.7.refs_3_ = bf16[192,1024]{1,0:T(8,128)(2,1)S(1)} collective-permute-done((bf16[192,1024]{1,0:T(8,128)(2,1)S(1)}, bf16[192,1024]{1,0:T(8,128)(2,1)S(1)}, u32[]{:S(2)}, u32[]{:S(2)}) %collective-permute-start.7) | collective-permute-done | bytes 393248 | tf_op jit(solution)/shard_map/ppermute | solution.py:57
  120.4 1.3 shard_map.119
  121.7 7.9 %all-to-all-done.2 = bf16[64,9,4,128]{3,2,1,0:T(4,128)(2,1)S(1)} async-done(((bf16[64,9,4,128]{3,2,1,0:T(4,128)(2,1)}), bf16[64,9,4,128]{3,2,1,0:T(4,128)(2,1)S(1)}, u32[]{:S(2)}, u32[]{:S(2)}) %all-to-all-start.2) | async-done | bytes 589856 | tf_op jit(solution)/shard_map/all_to_all | solution.py:282
  129.6 1.0 shard_map.120
  130.7 7.8 %all_to_all.21 = f32[8,8,128]{2,1,0:T(8,128)S(1)} all-to-all(f32[8,8,128]{2,1,0:T(8,128)S(1)} %get-tuple-element.37), channel_id=1, replica_groups=mesh['dp'=8,'expert'=64] {'dp'}, dimensions={0} | all-to-all | bytes 65536 | tf_op jit(solution)/shard_map/all_to_all | solution.py:322
  138.5 0.6 slice_bitcast_fusion
  (10 shorter events, 0.0 us)
Async XLA Ops:
  3.3 53.2 %all-to-all-start = ((bf16[64,9,4,128]{3,2,1,0:T(4,128)(2,1)}), bf16[64,9,4,128]{3,2,1,0:T(4,128)(2,1)S(1)}, u32[]{:S(2)}, u32[]{:S(2)}) async-start(bf16[64,9,4,128]{3,2,1,0:T(4,128)(2,1)} %bitcast.24), calls=%async_computation | async-start | bytes 1179648 | tf_op jit(solution)/shard_map/all_to_all | solution.py:282
  22.1 1.4 %copy-start = (bf16[1,192,4096]{2,1,0:T(8,128)(2,1)S(1)}, bf16[1,192,4096]{2,1,0:T(8,128)(2,1)}, u32[]{:S(2)}) copy-start(bf16[1,192,4096]{2,1,0:T(8,128)(2,1)} %param.9) | copy-start | bytes 4718596
  24.5 34.2 %collective-permute-start.1 = (bf16[192,1024]{1,0:T(8,128)(2,1)}, bf16[192,1024]{1,0:T(8,128)(2,1)S(1)}, u32[]{:S(2)}, u32[]{:S(2)}) collective-permute-start(bf16[192,1024]{1,0:T(8,128)(2,1)} %get-tuple-element.25), channel_id=1, source_target_pairs={{0,384},{64,448},{128,0},{192,64},{256,128},{320,192},{384,256},{4... | collective-permute-start | bytes 1179656 | tf_op jit(solution)/shard_map/ppermute | solution.py:57
  29.4 29.3 %collective-permute-start.2 = (bf16[192,1024]{1,0:T(8,128)(2,1)}, bf16[192,1024]{1,0:T(8,128)(2,1)S(1)}, u32[]{:S(2)}, u32[]{:S(2)}) collective-permute-start(bf16[192,1024]{1,0:T(8,128)(2,1)} %get-tuple-element.26), channel_id=1, source_target_pairs={{0,256},{64,320},{128,384},{192,448},{256,0},{320,64},{384,128},{4... | collective-permute-start | bytes 1179656 | tf_op jit(solution)/shard_map/ppermute | solution.py:57
  31.9 26.8 %collective-permute-start.3 = (bf16[192,1024]{1,0:T(8,128)(2,1)S(1)}, bf16[192,1024]{1,0:T(8,128)(2,1)S(1)}, u32[]{:S(2)}, u32[]{:S(2)}) collective-permute-start(bf16[192,1024]{1,0:T(8,128)(2,1)S(1)} %get-tuple-element.27), channel_id=1, source_target_pairs={{0,128},{64,192},{128,256},{192,320},{256,384},{320,448},{384,0},{... | collective-permute-start | bytes 1179656 | tf_op jit(solution)/shard_map/ppermute | solution.py:57
  56.7 3.6 %collective-permute-start = (bf16[384,512]{1,0:T(8,128)(2,1)S(1)}, bf16[384,512]{1,0:T(8,128)(2,1)S(1)}, u32[]{:S(2)}, u32[]{:S(2)}) collective-permute-start(bf16[384,512]{1,0:T(8,128)(2,1)S(1)} %get-tuple-element.23.near_ref), channel_id=1, source_target_pairs={{0,64},{64,0},{128,192},{192,128},{256,320},{320,256},{384,448},{4... | collective-permute-start | bytes 1179656 | tf_op jit(solution)/shard_map/ppermute | solution.py:57
  83.2 3.6 %collective-permute-start.4 = (bf16[384,512]{1,0:T(8,128)(2,1)S(1)}, bf16[384,512]{1,0:T(8,128)(2,1)S(1)}, u32[]{:S(2)}, u32[]{:S(2)}) collective-permute-start(bf16[384,512]{1,0:T(8,128)(2,1)S(1)} %shard_map.116), channel_id=1, source_target_pairs={{0,64},{64,0},{128,192},{192,128},{256,320},{320,256},{384,448},{4... | collective-permute-start | bytes 1179656 | tf_op jit(solution)/shard_map/ppermute | solution.py:57
  88.0 41.6 %all-to-all-start.2 = ((bf16[64,9,4,128]{3,2,1,0:T(4,128)(2,1)}), bf16[64,9,4,128]{3,2,1,0:T(4,128)(2,1)S(1)}, u32[]{:S(2)}, u32[]{:S(2)}) async-start(bf16[64,9,4,128]{3,2,1,0:T(4,128)(2,1)} %bitcast.10), calls=%async_computation.2 | async-start | bytes 1179648 | tf_op jit(solution)/shard_map/all_to_all | solution.py:282
  95.7 22.1 %collective-permute-start.5 = (bf16[192,1024]{1,0:T(8,128)(2,1)S(1)}, bf16[192,1024]{1,0:T(8,128)(2,1)S(1)}, u32[]{:S(2)}, u32[]{:S(2)}) collective-permute-start(bf16[192,1024]{1,0:T(8,128)(2,1)S(1)} %get-tuple-element.29), channel_id=1, source_target_pairs={{0,128},{64,192},{128,256},{192,320},{256,384},{320,448},{384,0},{... | collective-permute-start | bytes 1179656 | tf_op jit(solution)/shard_map/ppermute | solution.py:57
  98.2 19.6 %collective-permute-start.6 = (bf16[192,1024]{1,0:T(8,128)(2,1)S(1)}, bf16[192,1024]{1,0:T(8,128)(2,1)S(1)}, u32[]{:S(2)}, u32[]{:S(2)}) collective-permute-start(bf16[192,1024]{1,0:T(8,128)(2,1)S(1)} %get-tuple-element.30), channel_id=1, source_target_pairs={{0,256},{64,320},{128,384},{192,448},{256,0},{320,64},{384,128},{4... | collective-permute-start | bytes 1179656 | tf_op jit(solution)/shard_map/ppermute | solution.py:57
  102.2 18.2 %collective-permute-start.7 = (bf16[192,1024]{1,0:T(8,128)(2,1)S(1)}, bf16[192,1024]{1,0:T(8,128)(2,1)S(1)}, u32[]{:S(2)}, u32[]{:S(2)}) collective-permute-start(bf16[192,1024]{1,0:T(8,128)(2,1)S(1)} %get-tuple-element.31), channel_id=1, source_target_pairs={{0,384},{64,448},{128,0},{192,64},{256,128},{320,192},{384,256},{4... | collective-permute-start | bytes 1179656 | tf_op jit(solution)/shard_map/ppermute | solution.py:57
  120.4 9.2 %copy-start.1 = (bf16[16,8,192]{2,1,0:T(8,128)(2,1)S(1)}, bf16[16,8,192]{2,1,0:T(8,128)(2,1)}, u32[]{:S(2)}) copy-start(bf16[16,8,192]{2,1,0:T(8,128)(2,1)} %param.8) | copy-start | bytes 147460
  120.4 9.2 %copy-start.2 = (s32[128,1]{1,0:T(8,128)S(1)}, s32[128,1]{1,0:T(8,128)}, u32[]{:S(2)}) copy-start(s32[128,1]{1,0:T(8,128)} %get-tuple-element.33.slot_ref) | copy-start | bytes 1540
  120.4 9.2 %copy-start.3 = (f32[16,8]{0,1:T(8,128)S(1)}, f32[16,8]{0,1:T(8,128)}, u32[]{:S(2)}) copy-start(f32[16,8]{0,1:T(8,128)} %param.10) | copy-start | bytes 1540

commit v5 on v4

--- a/solution.py
+++ b/solution.py
@@ -18,7 +18,7 @@
 SM = pl.BlockSpec(memory_space=pltpu.SMEM)
 
 
-def call(kernel, outs, specs, flops=0, moved=1 << 20, scratch=(), vmem=40 << 20):
+def call(kernel, outs, specs, flops=0, moved=1 << 20, scratch=(), vmem=16 << 20):
     return pl.pallas_call(
         kernel,
         out_shape=outs,
@@ -154,7 +154,7 @@
     ]
     for copy in copies:
         copy.start()
-    for copy in copies:
+    for copy in copies[:4]:
         copy.wait()
     n_dev = cap_ref.shape[1]
     rows, hidden = act_ref.shape
@@ -175,6 +175,8 @@
     slot_ref[...] = slot
     pick = ones(iota((SLOTS * n_dev, rows), 0) == as_row(slot))
     owner = ones(iota((rows, toks), 0) // top == iota((rows, toks), 1))
+    for copy in copies[4:]:
+        copy.wait()
     grad = (column(gate_ref[...]) * dot(owner, cot_ref[...], 1, 0)).astype(BF)
     pack(rows_ref, flat_ref, dot(pick, grad, 1, 0), dot(pick, act_ref[...], 1, 0))
     sent_ref[...] = rows_ref[...].astype(BF)
@@ -187,41 +189,39 @@
     act_ref[...] = acts.T.astype(BF)
 
 
-def backward(here_ref, act_ref, near_ref, far_ref, *refs):
+def backward(here_ref, near_ref, far_ref, *refs):
     w_refs, out_ref = refs[:-1], refs[-1]
     here, feats = here_ref[0], near_ref.shape[1]
     near, far = core_columns(here, 0, feats), core_columns(here, 1, feats)
     for step in range(NY):
-        at, w_ref = chip(here, step), w_refs[step]
+        w_ref = w_refs[step]
         part = dot(w_ref[:, near], near_ref[...], 1, 1) + dot(w_ref[:, far], far_ref[...], 1, 1)
-        out_ref[at, 0] = act_ref[...]
-        out_ref[at, 1] = part.astype(BF)
-
-
-def forward(other, here_ref, all_ref, *refs):
-    w_refs, out_ref = refs[:-1], refs[-1]
-    here = here_ref[0]
-    columns = core_columns(here, other, out_ref.shape[1])
+        out_ref[chip(here, step)] = part.astype(BF)
+
+
+def forward(other, here_ref, *refs):
+    act_refs, w_refs, out_ref = refs[:NY], refs[NY:-1], refs[-1]
+    columns = core_columns(here_ref[0], other, out_ref.shape[1])
     total = None
-    for step in range(NY):
-        part = dot(all_ref[chip(here, step), 0], w_refs[step][:, columns], 0, 0)
+    for act_ref, w_ref in zip(act_refs, w_refs):
+        part = dot(act_ref[...], w_ref[:, columns], 0, 0)
         total = part if total is None else total + part
     out_ref[...] = total.astype(out_ref.dtype)
 
 
-def leave(all_ref, own_ref, swapped_ref, sent_ref, rows_ref, flat_ref):
-    back = sum(all_ref[y, 1].astype(F32) for y in range(NY))
+def leave(back_ref, own_ref, swapped_ref, sent_ref, rows_ref, flat_ref):
+    back = sum(back_ref[y].astype(F32) for y in range(NY))
     pack(rows_ref, flat_ref, own_ref[...] + swapped_ref[...].astype(F32), back.T)
     sent_ref[...] = rows_ref[...].astype(BF)
 
 
-def weights_back(here_ref, all_ref, near_ref, far_ref, *outs):
+def weights_back(here_ref, near_ref, far_ref, *refs):
+    act_refs, outs = refs[:NY], refs[NY:]
     here, feats = here_ref[0], near_ref.shape[1]
     near, far = core_columns(here, 0, feats), core_columns(here, 1, feats)
-    for step in range(NY):
-        acts = all_ref[chip(here, step), 0]
-        outs[step][:, near] = dot(acts, near_ref[...], 1, 0).astype(BF)
-        outs[step][:, far] = dot(acts, far_ref[...], 1, 0).astype(BF)
+    for act_ref, out_ref in zip(act_refs, outs):
+        out_ref[:, near] = dot(act_ref[...], near_ref[...], 1, 0).astype(BF)
+        out_ref[:, far] = dot(act_ref[...], far_ref[...], 1, 0).astype(BF)
 
 
 def collect(got_ref, slot_ref, gate_ref, act_ref, mixed_ref, back_ref, gate_out_ref, rows_ref, flat_ref):
@@ -287,25 +287,26 @@
         arrive, [shape((slots, feats)), shape((hidden, slots))], [VM], scratch=scratch
     )(got)
     far_grad = send(grad, 0, 1)
-    shared = call(
-        backward, shape((NY, 2, hidden, slots)), [SM] + [VM] * (3 + NY), flops=flops
-    )(here, own_act, grad, far_grad, *weights)
-    shared = exchange_y(shared)
+    all_acts = [own_act] + [send(own_act, NY - step, 0) for step in range(1, NY)]
+    back = call(backward, shape((NY, hidden, slots)), [SM] + [VM] * (2 + NY), flops=flops)(
+        here, grad, far_grad, *weights
+    )
+    back = exchange_y(back)
 
     def part(other, dtype):
         return call(
             functools.partial(forward, other),
             shape((slots, feats), dtype),
-            [SM] + [VM] * (1 + NY),
+            [SM] + [VM] * (2 * NY),
             flops=flops // 2,
-        )(here, shared, *weights)
+        )(here, *all_acts, *weights)
 
     swapped = send(part(1, BF), 0, 1)
-    returned = call(leave, payload, [VM] * 3, scratch=scratch)(shared, part(0, F32), swapped)
+    returned = call(leave, payload, [VM] * 3, scratch=scratch)(back, part(0, F32), swapped)
     home = exchange(returned)
 
-    pieces = call(weights_back, pieces_shape, [SM] + [VM] * 3, flops=flops)(
-        here, shared, grad, far_grad
+    pieces = call(weights_back, pieces_shape, [SM] + [VM] * (2 + NY), flops=flops)(
+        here, grad, far_grad, *all_acts
     )
     joined = [pieces[0]] + [send(pieces[step], step, 0) for step in range(1, NY)]
     weight_grad = call(

time: 140 us -> 139 us (level)
  blocking collectives: 28.9 us -> 8.01 us
  starting transfers between devices: 48.9 us -> 62.7 us
  local copies, waits for them, and re-layouts: 2.01 us -> 5.27 us
  waiting for transfers between devices: 47.8 us -> 49.3 us
    all_to_all x1 -> x0, blocking collectives: 21.1 us -> none  [exchange_y(): lax.all_to_all(value, 'dp', 0, 0, axis_index_groups=groups, tiled=True)]
    ppermute x8 -> x11, starting transfers between devices: 23.3 us -> 33.6 us  [send(): return lax.ppermute(value, 'dp', pairs)]
    all_to_all x0 -> x1, waiting for transfers between devices: none -> 5.18 us  [exchange_y(): lax.all_to_all(value, 'dp', 0, 0, axis_index_groups=groups, tiled=True)]
    all_to_all x0 -> x1, starting transfers between devices: none -> 3.54 us  [exchange_y(): lax.all_to_all(value, 'dp', 0, 0, axis_index_groups=groups, tiled=True)]
    unnamed x8 -> x20, local copies, waits for them, and re-layouts: 1.41 us -> 4.67 us
    ppermute x8 -> x11, waiting for transfers between devices: 18.2 us -> 15.2 us  [send(): return lax.ppermute(value, 'dp', pairs)]
  transfers between devices with their start and end apart: 10 -> 14, of which waited for: 6 -> 6; matrix products, arithmetic and copies ran while one was open for 0% -> 0% of each run, Pallas kernels for 3% -> 5%
where the time goes in v5:
time: 139 us; the launch traced here: 137 us
  starting transfers between devices  62.7 us (45%)
  waiting for transfers between devices  49.3 us (35%)
  Pallas kernels  11.3 us (8%)
  blocking collectives  8.01 us (6%)
  local copies, waits for them, and re-layouts  5.27 us (4%)
    ppermute x11, starting transfers between devices, send(): return lax.ppermute(value, 'dp', pairs)  33.6 us
    all_to_all x2, waiting for transfers between devices, exchange(): lax.all_to_all(value, 'expert', 0, 0, tiled=True).reshape(payload.shape)  28.9 us
    all_to_all x2, starting transfers between devices, exchange(): lax.all_to_all(value, 'expert', 0, 0, tiled=True).reshape(payload.shape)  25.6 us
    ppermute x11, waiting for transfers between devices, send(): return lax.ppermute(value, 'dp', pairs)  15.2 us
    all_to_all x1, blocking collectives, on_device(): gate_parts = lax.all_to_all(gate_parts, 'dp', 0, 0, tiled=True)  8.01 us
    all_to_all x1, waiting for transfers between devices, exchange_y(): lax.all_to_all(value, 'dp', 0, 0, axis_index_groups=groups, tiled=True)  5.18 us
    unnamed x20, local copies, waits for them, and re-layouts  4.67 us
    all_to_all x1, starting transfers between devices, exchange_y(): lax.all_to_all(value, 'dp', 0, 0, axis_index_groups=groups, tiled=True)  3.54 us
  transfers between devices with their start and end apart: 14, of which 6 were waited for; matrix products, arithmetic and copies ran while one was open for 0% of the time, Pallas kernels for 5%

profile of v5, /device:TPU:6, one launch (start us, length us, event | category | flops | bytes accessed | tf_op | source)
XLA Modules:
  0.0 137.5 jit_solution(15189484015199832671)
XLA Ops:
  0.6 2.6 %shard_map.111 = (bf16[2304,128]{1,0:T(8,128)(2,1)}, s32[128,1]{1,0:T(8,128)}) custom-call(s32[8,16]{1,0:T(8,128)} %bitcast.25, s32[8,16]{1,0:T(8,128)} %bitcast.26, s32[2,16]{1,0:T(2,128)} %bitcast.27, s32[1,64]{1,0:T(1,128)} %bitcast.28, bf16[128,192]{1,0:T(8,128)(2,1)} %bitcast.19, bf16[16,512]{1,0:T(8,128)(2,1)} %cot_hbm.1, f32[8,16]{1,0:T(8,128)} %bitcast.21), custom_call_target="tpu_custom_call" | custom-call | bytes 1048576 | tf_op jit(solution)/shard_map/pallas_call | solution.py:270
  3.2 18.8 %all-to-all-start = ((bf16[64,9,4,128]{3,2,1,0:T(4,128)(2,1)}), bf16[64,9,4,128]{3,2,1,0:T(4,128)(2,1)S(1)}, u32[]{:S(2)}, u32[]{:S(2)}) async-start(bf16[64,9,4,128]{3,2,1,0:T(4,128)(2,1)} %bitcast.24), calls=%async_computation | async-start | bytes 1179648 | tf_op jit(solution)/shard_map/all_to_all | solution.py:282
  22.0 1.4 %copy-done = bf16[1,192,4096]{2,1,0:T(8,128)(2,1)S(1)} copy-done((bf16[1,192,4096]{2,1,0:T(8,128)(2,1)S(1)}, bf16[1,192,4096]{2,1,0:T(8,128)(2,1)}, u32[]{:S(2)}) %copy-start) | copy-done | bytes 1572888
  23.4 0.9 shard_map.113
  24.3 4.9 %collective-permute-start.1 = (bf16[192,1024]{1,0:T(8,128)(2,1)}, bf16[192,1024]{1,0:T(8,128)(2,1)S(1)}, u32[]{:S(2)}, u32[]{:S(2)}) collective-permute-start(bf16[192,1024]{1,0:T(8,128)(2,1)} %get-tuple-element.24), channel_id=1, source_target_pairs={{0,384},{64,448},{128,0},{192,64},{256,128},{320,192},{384,256},{4... | collective-permute-start | bytes 1179656 | tf_op jit(solution)/shard_map/ppermute | solution.py:57
  29.2 2.5 %collective-permute-start.2 = (bf16[192,1024]{1,0:T(8,128)(2,1)S(1)}, bf16[192,1024]{1,0:T(8,128)(2,1)S(1)}, u32[]{:S(2)}, u32[]{:S(2)}) collective-permute-start(bf16[192,1024]{1,0:T(8,128)(2,1)S(1)} %get-tuple-element.25), channel_id=1, source_target_pairs={{0,256},{64,320},{128,384},{192,448},{256,0},{320,64},{384,128},{4... | collective-permute-start | bytes 1179656 | tf_op jit(solution)/shard_map/ppermute | solution.py:57
  31.8 2.9 %collective-permute-start.3 = (bf16[192,1024]{1,0:T(8,128)(2,1)S(1)}, bf16[192,1024]{1,0:T(8,128)(2,1)S(1)}, u32[]{:S(2)}, u32[]{:S(2)}) collective-permute-start(bf16[192,1024]{1,0:T(8,128)(2,1)S(1)} %get-tuple-element.26), channel_id=1, source_target_pairs={{0,128},{64,192},{128,256},{192,320},{256,384},{320,448},{384,0},{... | collective-permute-start | bytes 1179656 | tf_op jit(solution)/shard_map/ppermute | solution.py:57
  34.7 21.8 %all-to-all-done = bf16[64,9,4,128]{3,2,1,0:T(4,128)(2,1)S(1)} async-done(((bf16[64,9,4,128]{3,2,1,0:T(4,128)(2,1)}), bf16[64,9,4,128]{3,2,1,0:T(4,128)(2,1)S(1)}, u32[]{:S(2)}, u32[]{:S(2)}) %all-to-all-start) | async-done | bytes 589856 | tf_op jit(solution)/shard_map/all_to_all | solution.py:282
  56.7 1.9 %collective-permute-start = (bf16[384,512]{1,0:T(8,128)(2,1)S(1)}, bf16[384,512]{1,0:T(8,128)(2,1)S(1)}, u32[]{:S(2)}, u32[]{:S(2)}) collective-permute-start(bf16[384,512]{1,0:T(8,128)(2,1)S(1)} %get-tuple-element.22.near_ref), channel_id=1, source_target_pairs={{0,64},{64,0},{128,192},{192,128},{256,320},{320,256},{384,448},{4... | collective-permute-start | bytes 1179656 | tf_op jit(solution)/shard_map/ppermute | solution.py:57
  58.6 4.9 %collective-permute-start.4 = (bf16[192,384]{1,0:T(8,128)(2,1)S(1)}, bf16[192,384]{1,0:T(8,128)(2,1)S(1)}, u32[]{:S(2)}, u32[]{:S(2)}) collective-permute-start(bf16[192,384]{1,0:T(8,128)(2,1)S(1)} %get-tuple-element.27.refs_0_), channel_id=1, source_target_pairs={{0,384},{64,448},{128,0},{192,64},{256,128},{320,192},{384,256},{4... | collective-permute-start | bytes 442376 | tf_op jit(solution)/shard_map/ppermute | solution.py:57
  63.6 2.5 %collective-permute-start.5 = (bf16[192,384]{1,0:T(8,128)(2,1)S(1)}, bf16[192,384]{1,0:T(8,128)(2,1)S(1)}, u32[]{:S(2)}, u32[]{:S(2)}) collective-permute-start(bf16[192,384]{1,0:T(8,128)(2,1)S(1)} %get-tuple-element.27.refs_0_), channel_id=1, source_target_pairs={{0,256},{64,320},{128,384},{192,448},{256,0},{320,64},{384,128},{4... | collective-permute-start | bytes 442376 | tf_op jit(solution)/shard_map/ppermute | solution.py:57
  66.1 2.9 %collective-permute-start.6 = (bf16[192,384]{1,0:T(8,128)(2,1)S(1)}, bf16[192,384]{1,0:T(8,128)(2,1)S(1)}, u32[]{:S(2)}, u32[]{:S(2)}) collective-permute-start(bf16[192,384]{1,0:T(8,128)(2,1)S(1)} %get-tuple-element.27.refs_0_), channel_id=1, source_target_pairs={{0,128},{64,192},{128,256},{192,320},{256,384},{320,448},{384,0},{... | collective-permute-start | bytes 442376 | tf_op jit(solution)/shard_map/ppermute | solution.py:57
  69.0 2.0 %shard_map.114 = bf16[4,192,384]{2,1,0:T(8,128)(2,1)} custom-call(s32[1]{0:T(128)} %bitcast.here_ref, bf16[384,512]{1,0:T(8,128)(2,1)S(1)} %get-tuple-element.22.near_ref, bf16[384,512]{1,0:T(8,128)(2,1)S(1)} %collective-permute-done.far_ref, bf16[192,1024]{1,0:T(8,128)(2,1)S(1)} %get-tuple-element.23.refs_0_.refs_4_, ...), custom_call_target="tpu_custom_call" | custom-call | flops 603979776 | bytes 1048576 | tf_op jit(solution)/shard_map/pallas_call | solution.py:291
  71.0 0.8 copy-done.1
  72.5 3.5 %all-to-all-start.1 = ((bf16[4,192,384]{2,1,0:T(8,128)(2,1)}), bf16[4,192,384]{2,1,0:T(8,128)(2,1)S(1)}, u32[]{:S(2)}, u32[]{:S(2)}) async-start(bf16[4,192,384]{2,1,0:T(8,128)(2,1)} %shard_map.114), calls=%async_computation.1 | async-start | bytes 1179648 | tf_op jit(solution)/shard_map/all_to_all | solution.py:62
  76.7 1.9 %collective-permute-start.7 = (bf16[384,512]{1,0:T(8,128)(2,1)S(1)}, bf16[384,512]{1,0:T(8,128)(2,1)S(1)}, u32[]{:S(2)}, u32[]{:S(2)}) collective-permute-start(bf16[384,512]{1,0:T(8,128)(2,1)S(1)} %shard_map.116), channel_id=1, source_target_pairs={{0,64},{64,0},{128,192},{192,128},{256,320},{320,256},{384,448},{4... | collective-permute-start | bytes 1179656 | tf_op jit(solution)/shard_map/ppermute | solution.py:57
  79.3 1.1 collective-permute-done.7.swapped_ref
  80.3 0.8 copy-done.5
  81.1 5.2 %all-to-all-done.1.back_ref = bf16[4,192,384]{2,1,0:T(8,128)(2,1)S(1)} async-done(((bf16[4,192,384]{2,1,0:T(8,128)(2,1)}), bf16[4,192,384]{2,1,0:T(8,128)(2,1)S(1)}, u32[]{:S(2)}, u32[]{:S(2)}) %all-to-all-start.1) | async-done | bytes 589856 | tf_op jit(solution)/shard_map/all_to_all | solution.py:62
  86.3 1.0 copy-done.6
  87.3 1.1 shard_map.117
  88.4 6.8 %all-to-all-start.2 = ((bf16[64,9,4,128]{3,2,1,0:T(4,128)(2,1)}), bf16[64,9,4,128]{3,2,1,0:T(4,128)(2,1)S(1)}, u32[]{:S(2)}, u32[]{:S(2)}) async-start(bf16[64,9,4,128]{3,2,1,0:T(4,128)(2,1)} %bitcast.10), calls=%async_computation.2 | async-start | bytes 1179648 | tf_op jit(solution)/shard_map/all_to_all | solution.py:282
  95.2 1.0 shard_map.118
  96.2 2.5 %collective-permute-start.8 = (bf16[192,1024]{1,0:T(8,128)(2,1)S(1)}, bf16[192,1024]{1,0:T(8,128)(2,1)S(1)}, u32[]{:S(2)}, u32[]{:S(2)}) collective-permute-start(bf16[192,1024]{1,0:T(8,128)(2,1)S(1)} %get-tuple-element.29), channel_id=1, source_target_pairs={{0,128},{64,192},{128,256},{192,320},{256,384},{320,448},{384,0},{... | collective-permute-start | bytes 1179656 | tf_op jit(solution)/shard_map/ppermute | solution.py:57
  98.7 4.1 %collective-permute-start.9 = (bf16[192,1024]{1,0:T(8,128)(2,1)S(1)}, bf16[192,1024]{1,0:T(8,128)(2,1)S(1)}, u32[]{:S(2)}, u32[]{:S(2)}) collective-permute-start(bf16[192,1024]{1,0:T(8,128)(2,1)S(1)} %get-tuple-element.30), channel_id=1, source_target_pairs={{0,256},{64,320},{128,384},{192,448},{256,0},{320,64},{384,128},{4... | collective-permute-start | bytes 1179656 | tf_op jit(solution)/shard_map/ppermute | solution.py:57
  102.8 2.5 %collective-permute-start.10 = (bf16[192,1024]{1,0:T(8,128)(2,1)S(1)}, bf16[192,1024]{1,0:T(8,128)(2,1)S(1)}, u32[]{:S(2)}, u32[]{:S(2)}) collective-permute-start(bf16[192,1024]{1,0:T(8,128)(2,1)S(1)} %get-tuple-element.31), channel_id=1, source_target_pairs={{0,384},{64,448},{128,0},{192,64},{256,128},{320,192},{384,256},{4... | collective-permute-start | bytes 1179656 | tf_op jit(solution)/shard_map/ppermute | solution.py:57
  105.3 11.5 %collective-permute-done.8.refs_1_ = bf16[192,1024]{1,0:T(8,128)(2,1)S(1)} collective-permute-done((bf16[192,1024]{1,0:T(8,128)(2,1)S(1)}, bf16[192,1024]{1,0:T(8,128)(2,1)S(1)}, u32[]{:S(2)}, u32[]{:S(2)}) %collective-permute-start.8) | collective-permute-done | bytes 393248 | tf_op jit(solution)/shard_map/ppermute | solution.py:57
  116.9 2.5 %collective-permute-done.10.refs_3_ = bf16[192,1024]{1,0:T(8,128)(2,1)S(1)} collective-permute-done((bf16[192,1024]{1,0:T(8,128)(2,1)S(1)}, bf16[192,1024]{1,0:T(8,128)(2,1)S(1)}, u32[]{:S(2)}, u32[]{:S(2)}) %collective-permute-start.10) | collective-permute-done | bytes 393248 | tf_op jit(solution)/shard_map/ppermute | solution.py:57
  119.4 1.3 shard_map.119
  120.7 7.1 %all-to-all-done.2 = bf16[64,9,4,128]{3,2,1,0:T(4,128)(2,1)S(1)} async-done(((bf16[64,9,4,128]{3,2,1,0:T(4,128)(2,1)}), bf16[64,9,4,128]{3,2,1,0:T(4,128)(2,1)S(1)}, u32[]{:S(2)}, u32[]{:S(2)}) %all-to-all-start.2) | async-done | bytes 589856 | tf_op jit(solution)/shard_map/all_to_all | solution.py:282
  127.8 1.0 shard_map.120
  128.9 8.0 %all_to_all.20 = f32[8,8,128]{2,1,0:T(8,128)S(1)} all-to-all(f32[8,8,128]{2,1,0:T(8,128)S(1)} %get-tuple-element.37), channel_id=1, replica_groups=mesh['dp'=8,'expert'=64] {'dp'}, dimensions={0} | all-to-all | bytes 65536 | tf_op jit(solution)/shard_map/all_to_all | solution.py:323
  (29 shorter events, 2.9 us)
Async XLA Ops:
  3.2 53.2 %all-to-all-start = ((bf16[64,9,4,128]{3,2,1,0:T(4,128)(2,1)}), bf16[64,9,4,128]{3,2,1,0:T(4,128)(2,1)S(1)}, u32[]{:S(2)}, u32[]{:S(2)}) async-start(bf16[64,9,4,128]{3,2,1,0:T(4,128)(2,1)} %bitcast.24), calls=%async_computation | async-start | bytes 1179648 | tf_op jit(solution)/shard_map/all_to_all | solution.py:282
  22.0 1.4 %copy-start = (bf16[1,192,4096]{2,1,0:T(8,128)(2,1)S(1)}, bf16[1,192,4096]{2,1,0:T(8,128)(2,1)}, u32[]{:S(2)}) copy-start(bf16[1,192,4096]{2,1,0:T(8,128)(2,1)} %param.9) | copy-start | bytes 4718596
  24.3 39.3 %collective-permute-start.1 = (bf16[192,1024]{1,0:T(8,128)(2,1)}, bf16[192,1024]{1,0:T(8,128)(2,1)S(1)}, u32[]{:S(2)}, u32[]{:S(2)}) collective-permute-start(bf16[192,1024]{1,0:T(8,128)(2,1)} %get-tuple-element.24), channel_id=1, source_target_pairs={{0,384},{64,448},{128,0},{192,64},{256,128},{320,192},{384,256},{4... | collective-permute-start | bytes 1179656 | tf_op jit(solution)/shard_map/ppermute | solution.py:57
  29.2 36.9 %collective-permute-start.2 = (bf16[192,1024]{1,0:T(8,128)(2,1)S(1)}, bf16[192,1024]{1,0:T(8,128)(2,1)S(1)}, u32[]{:S(2)}, u32[]{:S(2)}) collective-permute-start(bf16[192,1024]{1,0:T(8,128)(2,1)S(1)} %get-tuple-element.25), channel_id=1, source_target_pairs={{0,256},{64,320},{128,384},{192,448},{256,0},{320,64},{384,128},{4... | collective-permute-start | bytes 1179656 | tf_op jit(solution)/shard_map/ppermute | solution.py:57
  31.8 37.3 %collective-permute-start.3 = (bf16[192,1024]{1,0:T(8,128)(2,1)S(1)}, bf16[192,1024]{1,0:T(8,128)(2,1)S(1)}, u32[]{:S(2)}, u32[]{:S(2)}) collective-permute-start(bf16[192,1024]{1,0:T(8,128)(2,1)S(1)} %get-tuple-element.26), channel_id=1, source_target_pairs={{0,128},{64,192},{128,256},{192,320},{256,384},{320,448},{384,0},{... | collective-permute-start | bytes 1179656 | tf_op jit(solution)/shard_map/ppermute | solution.py:57
  56.7 12.3 %collective-permute-start = (bf16[384,512]{1,0:T(8,128)(2,1)S(1)}, bf16[384,512]{1,0:T(8,128)(2,1)S(1)}, u32[]{:S(2)}, u32[]{:S(2)}) collective-permute-start(bf16[384,512]{1,0:T(8,128)(2,1)S(1)} %get-tuple-element.22.near_ref), channel_id=1, source_target_pairs={{0,64},{64,0},{128,192},{192,128},{256,320},{320,256},{384,448},{4... | collective-permute-start | bytes 1179656 | tf_op jit(solution)/shard_map/ppermute | solution.py:57
  58.6 17.4 %collective-permute-start.4 = (bf16[192,384]{1,0:T(8,128)(2,1)S(1)}, bf16[192,384]{1,0:T(8,128)(2,1)S(1)}, u32[]{:S(2)}, u32[]{:S(2)}) collective-permute-start(bf16[192,384]{1,0:T(8,128)(2,1)S(1)} %get-tuple-element.27.refs_0_), channel_id=1, source_target_pairs={{0,384},{64,448},{128,0},{192,64},{256,128},{320,192},{384,256},{4... | collective-permute-start | bytes 442376 | tf_op jit(solution)/shard_map/ppermute | solution.py:57
  63.6 12.5 %collective-permute-start.5 = (bf16[192,384]{1,0:T(8,128)(2,1)S(1)}, bf16[192,384]{1,0:T(8,128)(2,1)S(1)}, u32[]{:S(2)}, u32[]{:S(2)}) collective-permute-start(bf16[192,384]{1,0:T(8,128)(2,1)S(1)} %get-tuple-element.27.refs_0_), channel_id=1, source_target_pairs={{0,256},{64,320},{128,384},{192,448},{256,0},{320,64},{384,128},{4... | collective-permute-start | bytes 442376 | tf_op jit(solution)/shard_map/ppermute | solution.py:57
  66.1 10.0 %collective-permute-start.6 = (bf16[192,384]{1,0:T(8,128)(2,1)S(1)}, bf16[192,384]{1,0:T(8,128)(2,1)S(1)}, u32[]{:S(2)}, u32[]{:S(2)}) collective-permute-start(bf16[192,384]{1,0:T(8,128)(2,1)S(1)} %get-tuple-element.27.refs_0_), channel_id=1, source_target_pairs={{0,128},{64,192},{128,256},{192,320},{256,384},{320,448},{384,0},{... | collective-permute-start | bytes 442376 | tf_op jit(solution)/shard_map/ppermute | solution.py:57
  71.0 0.8 copy-start.1
  71.8 0.7 copy-start.3
  72.5 13.7 %all-to-all-start.1 = ((bf16[4,192,384]{2,1,0:T(8,128)(2,1)}), bf16[4,192,384]{2,1,0:T(8,128)(2,1)S(1)}, u32[]{:S(2)}, u32[]{:S(2)}) async-start(bf16[4,192,384]{2,1,0:T(8,128)(2,1)} %shard_map.114), calls=%async_computation.1 | async-start | bytes 1179648 | tf_op jit(solution)/shard_map/all_to_all | solution.py:62
  76.7 3.6 %collective-permute-start.7 = (bf16[384,512]{1,0:T(8,128)(2,1)S(1)}, bf16[384,512]{1,0:T(8,128)(2,1)S(1)}, u32[]{:S(2)}, u32[]{:S(2)}) collective-permute-start(bf16[384,512]{1,0:T(8,128)(2,1)S(1)} %shard_map.116), channel_id=1, source_target_pairs={{0,64},{64,0},{128,192},{192,128},{256,320},{320,256},{384,448},{4... | collective-permute-start | bytes 1179656 | tf_op jit(solution)/shard_map/ppermute | solution.py:57
  79.3 16.0 %copy-start.2 = (bf16[384,512]{1,0:T(8,128)(2,1)S(1)}, bf16[384,512]{1,0:T(8,128)(2,1)}, u32[]{:S(2)}) copy-start(bf16[384,512]{1,0:T(8,128)(2,1)} %copy-done.1) | copy-start | bytes 1179652
  79.3 16.0 %copy-start.4 = (bf16[384,512]{1,0:T(8,128)(2,1)S(1)}, bf16[384,512]{1,0:T(8,128)(2,1)}, u32[]{:S(2)}) copy-start(bf16[384,512]{1,0:T(8,128)(2,1)} %copy-done.3) | copy-start | bytes 1179652
  80.3 0.8 copy-start.5
  86.3 1.0 copy-start.6
  88.4 39.4 %all-to-all-start.2 = ((bf16[64,9,4,128]{3,2,1,0:T(4,128)(2,1)}), bf16[64,9,4,128]{3,2,1,0:T(4,128)(2,1)S(1)}, u32[]{:S(2)}, u32[]{:S(2)}) async-start(bf16[64,9,4,128]{3,2,1,0:T(4,128)(2,1)} %bitcast.10), calls=%async_computation.2 | async-start | bytes 1179648 | tf_op jit(solution)/shard_map/all_to_all | solution.py:282
  96.2 20.6 %collective-permute-start.8 = (bf16[192,1024]{1,0:T(8,128)(2,1)S(1)}, bf16[192,1024]{1,0:T(8,128)(2,1)S(1)}, u32[]{:S(2)}, u32[]{:S(2)}) collective-permute-start(bf16[192,1024]{1,0:T(8,128)(2,1)S(1)} %get-tuple-element.29), channel_id=1, source_target_pairs={{0,128},{64,192},{128,256},{192,320},{256,384},{320,448},{384,0},{... | collective-permute-start | bytes 1179656 | tf_op jit(solution)/shard_map/ppermute | solution.py:57
  98.7 18.2 %collective-permute-start.9 = (bf16[192,1024]{1,0:T(8,128)(2,1)S(1)}, bf16[192,1024]{1,0:T(8,128)(2,1)S(1)}, u32[]{:S(2)}, u32[]{:S(2)}) collective-permute-start(bf16[192,1024]{1,0:T(8,128)(2,1)S(1)} %get-tuple-element.30), channel_id=1, source_target_pairs={{0,256},{64,320},{128,384},{192,448},{256,0},{320,64},{384,128},{4... | collective-permute-start | bytes 1179656 | tf_op jit(solution)/shard_map/ppermute | solution.py:57
  102.8 16.6 %collective-permute-start.10 = (bf16[192,1024]{1,0:T(8,128)(2,1)S(1)}, bf16[192,1024]{1,0:T(8,128)(2,1)S(1)}, u32[]{:S(2)}, u32[]{:S(2)}) collective-permute-start(bf16[192,1024]{1,0:T(8,128)(2,1)S(1)} %get-tuple-element.31), channel_id=1, source_target_pairs={{0,384},{64,448},{128,0},{192,64},{256,128},{320,192},{384,256},{4... | collective-permute-start | bytes 1179656 | tf_op jit(solution)/shard_map/ppermute | solution.py:57
  119.4 8.4 %copy-start.7 = (bf16[16,8,192]{2,1,0:T(8,128)(2,1)S(1)}, bf16[16,8,192]{2,1,0:T(8,128)(2,1)}, u32[]{:S(2)}) copy-start(bf16[16,8,192]{2,1,0:T(8,128)(2,1)} %param.8) | copy-start | bytes 147460
  119.4 8.4 %copy-start.8 = (s32[128,1]{1,0:T(8,128)S(1)}, s32[128,1]{1,0:T(8,128)}, u32[]{:S(2)}) copy-start(s32[128,1]{1,0:T(8,128)} %get-tuple-element.33.slot_ref) | copy-start | bytes 1540
  119.4 8.4 %copy-start.9 = (f32[16,8]{0,1:T(8,128)S(1)}, f32[16,8]{0,1:T(8,128)}, u32[]{:S(2)}) copy-start(f32[16,8]{0,1:T(8,128)} %param.10) | copy-start | bytes 1540

commit v6 on v5

--- a/solution.py
+++ b/solution.py
@@ -12,6 +12,7 @@
 LANES = 128
 TILE = 4
 NY = 4
+EXTRA = 16
 BF = jnp.bfloat16
 F32 = jnp.float32
 VM = pl.BlockSpec(memory_space=pltpu.VMEM)
@@ -49,7 +50,7 @@
 def payload_rows(feats, hidden):
     wide = SLOTS * feats // LANES
     narrow = -(-SLOTS * hidden // LANES)
-    return wide, narrow, -(-(wide + narrow) // TILE) * TILE
+    return wide, narrow, -(-(wide + narrow + 1) // TILE) * TILE
 
 
 def send(value, step, other):
@@ -102,7 +103,7 @@
     return jnp.sum(jnp.where(diagonal, col, jnp.zeros_like(col)), axis=0, keepdims=True)
 
 
-def pack(rows_ref, flat_ref, wide_vals, narrow_vals):
+def pack(rows_ref, flat_ref, wide_vals, narrow_vals, scalars=None):
     n_dev = flat_ref.shape[0]
     feats, hidden = wide_vals.shape[1], narrow_vals.shape[1]
     wide, narrow, rows = payload_rows(feats, hidden)
@@ -118,6 +119,24 @@
         if i < narrow:
             block = flat_ref[:, i * LANES : (i + 1) * LANES]
         rows_ref[pl.ds(wide + i, n_dev, stride=rows), :] = block
+    if scalars is not None:
+        for j in range(SLOTS):
+            part = scalars[j * n_dev : (j + 1) * n_dev]
+            flat_ref[:, j * EXTRA : (j + 1) * EXTRA] = part
+        flat_ref[:, SLOTS * EXTRA : LANES] = jnp.zeros((n_dev, LANES - SLOTS * EXTRA), F32)
+        rows_ref[pl.ds(wide + narrow, n_dev, stride=rows), :] = flat_ref[:, :LANES]
+
+
+def unpack_scalars(rows_ref, n_dev, feats, hidden):
+    wide, narrow, rows = payload_rows(feats, hidden)
+    block = rows_ref[pl.ds(wide + narrow, n_dev, stride=rows), :]
+    return jnp.concatenate([block[:, j * EXTRA : (j + 1) * EXTRA] for j in range(SLOTS)], axis=0)
+
+
+def two_parts(row):
+    high = row.astype(BF).astype(F32)
+    at = iota((EXTRA, row.shape[1]), 0)
+    return jnp.where(at == 0, high, jnp.where(at == 1, row - high, 0.0))
 
 
 def unpack(rows_ref, flat_ref, feats, hidden):
@@ -184,9 +203,24 @@
 
 def arrive(got_ref, grad_ref, act_ref, rows_ref, flat_ref):
     rows_ref[...] = got_ref[...].astype(F32)
-    grad, acts = unpack(rows_ref, flat_ref, grad_ref.shape[1], act_ref.shape[0])
+    grad, acts = unpack(rows_ref, flat_ref, grad_ref.shape[1], act_ref.shape[1])
     grad_ref[...] = grad.astype(BF)
-    act_ref[...] = acts.T.astype(BF)
+    acts = acts.T.astype(BF)
+    for y in range(NY):
+        act_ref[y] = acts
+
+
+def seal(part_ref, act_ref, out_ref):
+    hidden, slots = act_ref.shape[1:]
+    gate = jnp.zeros((1, slots), F32)
+    for y in range(NY):
+        part = part_ref[y]
+        products = act_ref[y].astype(F32) * part.astype(F32)
+        gate = gate + jnp.sum(products, axis=0, keepdims=True)
+        out_ref[y, :hidden] = part
+    extra = two_parts(gate).astype(BF)
+    for y in range(NY):
+        out_ref[y, hidden:] = extra
 
 
 def backward(here_ref, near_ref, far_ref, *refs):
@@ -199,32 +233,35 @@
         out_ref[chip(here, step)] = part.astype(BF)
 
 
-def forward(other, here_ref, *refs):
-    act_refs, w_refs, out_ref = refs[:NY], refs[NY:-1], refs[-1]
-    columns = core_columns(here_ref[0], other, out_ref.shape[1])
-    total = None
-    for act_ref, w_ref in zip(act_refs, w_refs):
-        part = dot(act_ref[...], w_ref[:, columns], 0, 0)
+def forward(other, here_ref, act_ref, *refs):
+    w_refs, more, out_ref = refs[:NY], refs[NY:-1], refs[-1]
+    here = here_ref[0]
+    columns = core_columns(here, other, out_ref.shape[1])
+    total = more[0][...].astype(F32) if more else None
+    for step in range(NY):
+        part = dot(act_ref[chip(here, step)], w_refs[step][:, columns], 0, 0)
         total = part if total is None else total + part
     out_ref[...] = total.astype(out_ref.dtype)
 
 
-def leave(back_ref, own_ref, swapped_ref, sent_ref, rows_ref, flat_ref):
+def leave(back_ref, wide_ref, sent_ref, rows_ref, flat_ref):
     back = sum(back_ref[y].astype(F32) for y in range(NY))
-    pack(rows_ref, flat_ref, own_ref[...] + swapped_ref[...].astype(F32), back.T)
+    hidden = back.shape[0] - EXTRA
+    gate = jnp.sum(back[hidden:], axis=0, keepdims=True)
+    pack(rows_ref, flat_ref, wide_ref[...], back[:hidden].T, two_parts(gate).T)
     sent_ref[...] = rows_ref[...].astype(BF)
 
 
-def weights_back(here_ref, near_ref, far_ref, *refs):
-    act_refs, outs = refs[:NY], refs[NY:]
+def weights_back(here_ref, near_ref, far_ref, act_ref, *outs):
     here, feats = here_ref[0], near_ref.shape[1]
     near, far = core_columns(here, 0, feats), core_columns(here, 1, feats)
-    for act_ref, out_ref in zip(act_refs, outs):
-        out_ref[:, near] = dot(act_ref[...], near_ref[...], 1, 0).astype(BF)
-        out_ref[:, far] = dot(act_ref[...], far_ref[...], 1, 0).astype(BF)
-
-
-def collect(got_ref, slot_ref, gate_ref, act_ref, mixed_ref, back_ref, gate_out_ref, rows_ref, flat_ref):
+    for step in range(NY):
+        acts = act_ref[chip(here, step)]
+        outs[step][:, near] = dot(acts, near_ref[...], 1, 0).astype(BF)
+        outs[step][:, far] = dot(acts, far_ref[...], 1, 0).astype(BF)
+
+
+def collect(got_ref, slot_ref, gate_ref, mixed_ref, back_ref, gate_out_ref, rows_ref, flat_ref):
     top, toks = gate_ref.shape
     rows, hidden = back_ref.shape
     feats = mixed_ref.shape[1]
@@ -236,13 +273,11 @@
     mixed_ref[...] = jnp.sum(row_out.reshape(toks, top, feats), axis=1).astype(BF)
     back = dot(pick, backs.astype(BF), 1, 0)
     back_ref[...] = back.astype(BF)
-    gate_back = jnp.sum(back * act_ref[...].astype(F32), axis=1, keepdims=True) / gate
+    scalars = unpack_scalars(rows_ref, flat_ref.shape[0], feats, hidden)
+    gate_back = jnp.sum(dot(pick, scalars.astype(BF), 1, 0), axis=1, keepdims=True) / gate
     at_tok = iota((rows, toks), 0) // top == iota((rows, toks), 1)
     spread = jnp.where(at_tok, gate_back, 0.0)
-    gate_out_ref[...] = jnp.zeros_like(gate_out_ref)
-    part = jnp.sum(spread.reshape(toks, top, toks), axis=0)
-    for i in range(2 * NY):
-        gate_out_ref[i, :, :toks] = part
+    gate_out_ref[...] = jnp.sum(spread.reshape(toks, top, toks), axis=0)
 
 
 def on_device(acts, w_down, gates, cotangent, expert_ids, replica_pick, placement, group_cap):
@@ -283,30 +318,30 @@
 
     got = exchange(sent)
     flops = 2 * slots * feats * hidden * 2 * NY
-    grad, own_act = call(
-        arrive, [shape((slots, feats)), shape((hidden, slots))], [VM], scratch=scratch
-    )(got)
+    stack = shape((NY, hidden, slots))
+    grad, own_act = call(arrive, [shape((slots, feats)), stack], [VM], scratch=scratch)(got)
+    near_act = exchange_y(own_act)
     far_grad = send(grad, 0, 1)
-    all_acts = [own_act] + [send(own_act, NY - step, 0) for step in range(1, NY)]
-    back = call(backward, shape((NY, hidden, slots)), [SM] + [VM] * (2 + NY), flops=flops)(
+    back = call(backward, stack, [SM] + [VM] * (2 + NY), flops=flops)(
         here, grad, far_grad, *weights
     )
+    back = call(seal, shape((NY, hidden + EXTRA, slots)), [VM] * 2)(back, near_act)
     back = exchange_y(back)
 
-    def part(other, dtype):
+    def part(other, dtype, *more):
         return call(
             functools.partial(forward, other),
             shape((slots, feats), dtype),
-            [SM] + [VM] * (2 * NY),
+            [SM] + [VM] * (1 + NY + len(more)),
             flops=flops // 2,
-        )(here, *all_acts, *weights)
-
-    swapped = send(part(1, BF), 0, 1)
-    returned = call(leave, payload, [VM] * 3, scratch=scratch)(back, part(0, F32), swapped)
+        )(here, near_act, *weights, *more)
+
+    wide = part(0, F32, send(part(1, BF), 0, 1))
+    returned = call(leave, payload, [VM] * 2, scratch=scratch)(back, wide)
     home = exchange(returned)
 
-    pieces = call(weights_back, pieces_shape, [SM] + [VM] * (2 + NY), flops=flops)(
-        here, grad, far_grad, *all_acts
+    pieces = call(weights_back, pieces_shape, [SM] + [VM] * 3, flops=flops)(
+        here, grad, far_grad, near_act
     )
     joined = [pieces[0]] + [send(pieces[step], step, 0) for step in range(1, NY)]
     weight_grad = call(
@@ -314,14 +349,13 @@
     )(here, *joined)
 
     home, weight_grad = lax.optimization_barrier((home, weight_grad))
-    combined, back_rows, gate_parts = call(
+    combined, back_rows, gate_part = call(
         collect,
-        [shape((toks, feats)), shape((rows, hidden)), shape((2 * NY, top, LANES), F32)],
-        [VM] * 4,
+        [shape((toks, feats)), shape((rows, hidden)), shape((top, toks), F32)],
+        [VM] * 3,
         scratch=scratch,
-    )(home, slot, gates_t, inputs[4])
-    gate_parts = lax.all_to_all(gate_parts, "dp", 0, 0, tiled=True)
-    gate_grad = jnp.sum(gate_parts, axis=0)[:, :toks].T
+    )(home, slot, gates_t)
+    gate_grad = (gate_part + send(gate_part, 0, 1)).T
     return combined, back_rows.reshape(toks, top, hidden), weight_grad[None], gate_grad
 
 

time: 139 us -> 139 us (level)
  waiting for transfers between devices: 49.3 us -> 59.2 us
  blocking collectives: 8.01 us -> 0 us
  starting transfers between devices: 62.7 us -> 59.3 us
  Pallas kernels: 11.3 us -> 13.6 us
  local copies, waits for them, and re-layouts: 5.27 us -> 3.17 us
    ppermute x11 -> x9, starting transfers between devices: 33.6 us -> 25 us  [send(): return lax.ppermute(value, 'dp', pairs)]
    all_to_all x1 -> x2, waiting for transfers between devices: 5.18 us -> 13.6 us  [exchange_y(): lax.all_to_all(value, 'dp', 0, 0, axis_index_groups=groups, tiled=True)]
    all_to_all x1 -> x0, blocking collectives: 8.01 us -> none  [on_device(): gate_parts = lax.all_to_all(gate_parts, 'dp', 0, 0, tiled=True)]
    all_to_all x1 -> x2, starting transfers between devices: 3.54 us -> 8.64 us  [exchange_y(): lax.all_to_all(value, 'dp', 0, 0, axis_index_groups=groups, tiled=True)]
    pallas_call x5 -> x6, Pallas kernels: 5.45 us -> 7.6 us  [the longest x1 2.31 us: on_device(): returned = call(leave, payload, [VM] * 2, scratch=scratch)(back, wide)]
    ppermute x11 -> x9, waiting for transfers between devices: 15.2 us -> 16.8 us  [send(): return lax.ppermute(value, 'dp', pairs)]
    unnamed x20 -> x12, local copies, waits for them, and re-layouts: 4.67 us -> 3.17 us
  transfers between devices with their start and end apart: 14 -> 13, of which waited for: 6 -> 8; matrix products, arithmetic and copies ran while one was open for 0% -> 0% of each run, Pallas kernels for 5% -> 5%
where the time goes in v6:
time: 139 us; the launch traced here: 137 us
  starting transfers between devices  59.3 us (43%)
  waiting for transfers between devices  59.2 us (43%)
  Pallas kernels  13.6 us (10%)
  local copies, waits for them, and re-layouts  3.17 us (2%)
    all_to_all x2, waiting for transfers between devices, exchange(): lax.all_to_all(value, 'expert', 0, 0, tiled=True).reshape(payload.shape)  28.7 us
    all_to_all x2, starting transfers between devices, exchange(): lax.all_to_all(value, 'expert', 0, 0, tiled=True).reshape(payload.shape)  25.6 us
    ppermute x9, starting transfers between devices, send(): return lax.ppermute(value, 'dp', pairs)  25 us
    ppermute x9, waiting for transfers between devices, send(): return lax.ppermute(value, 'dp', pairs)  16.8 us
    all_to_all x2, waiting for transfers between devices, exchange_y(): lax.all_to_all(value, 'dp', 0, 0, axis_index_groups=groups, tiled=True)  13.6 us
    all_to_all x2, starting transfers between devices, exchange_y(): lax.all_to_all(value, 'dp', 0, 0, axis_index_groups=groups, tiled=True)  8.64 us
    unnamed x12, local copies, waits for them, and re-layouts  3.17 us
  transfers between devices with their start and end apart: 13, of which 8 were waited for; matrix products, arithmetic and copies ran while one was open for 0% of the time, Pallas kernels for 5%

profile of v6, /device:TPU:6, one launch (start us, length us, event | category | flops | bytes accessed | tf_op | source)
XLA Modules:
  0.0 136.7 jit_solution(3450370083468237205)
XLA Ops:
  0.6 2.6 %shard_map.111 = (bf16[2304,128]{1,0:T(8,128)(2,1)}, s32[128,1]{1,0:T(8,128)}) custom-call(s32[8,16]{1,0:T(8,128)} %bitcast.24, s32[8,16]{1,0:T(8,128)} %bitcast.25, s32[2,16]{1,0:T(2,128)} %bitcast.26, s32[1,64]{1,0:T(1,128)} %bitcast.27, bf16[128,192]{1,0:T(8,128)(2,1)} %bitcast.23, bf16[16,512]{1,0:T(8,128)(2,1)} %cot_hbm.1, f32[8,16]{1,0:T(8,128)} %bitcast.19), custom_call_target="tpu_custom_call" | custom-call | bytes 1048576 | tf_op jit(solution)/shard_map/pallas_call | solution.py:305
  3.2 18.8 %all-to-all-start = ((bf16[64,9,4,128]{3,2,1,0:T(4,128)(2,1)}), bf16[64,9,4,128]{3,2,1,0:T(4,128)(2,1)S(1)}, u32[]{:S(2)}, u32[]{:S(2)}) async-start(bf16[64,9,4,128]{3,2,1,0:T(4,128)(2,1)} %bitcast.22), calls=%async_computation | async-start | bytes 1179648 | tf_op jit(solution)/shard_map/all_to_all | solution.py:317
  22.0 1.4 %copy-done = bf16[1,192,4096]{2,1,0:T(8,128)(2,1)S(1)} copy-done((bf16[1,192,4096]{2,1,0:T(8,128)(2,1)S(1)}, bf16[1,192,4096]{2,1,0:T(8,128)(2,1)}, u32[]{:S(2)}) %copy-start) | copy-done | bytes 1572888
  23.4 1.0 shard_map.113
  24.4 4.9 %collective-permute-start.1 = (bf16[192,1024]{1,0:T(8,128)(2,1)}, bf16[192,1024]{1,0:T(8,128)(2,1)S(1)}, u32[]{:S(2)}, u32[]{:S(2)}) collective-permute-start(bf16[192,1024]{1,0:T(8,128)(2,1)} %get-tuple-element.24), channel_id=1, source_target_pairs={{0,384},{64,448},{128,0},{192,64},{256,128},{320,192},{384,256},{4... | collective-permute-start | bytes 1179656 | tf_op jit(solution)/shard_map/ppermute | solution.py:58
  29.3 2.5 %collective-permute-start.2 = (bf16[192,1024]{1,0:T(8,128)(2,1)}, bf16[192,1024]{1,0:T(8,128)(2,1)S(1)}, u32[]{:S(2)}, u32[]{:S(2)}) collective-permute-start(bf16[192,1024]{1,0:T(8,128)(2,1)} %get-tuple-element.25), channel_id=1, source_target_pairs={{0,256},{64,320},{128,384},{192,448},{256,0},{320,64},{384,128},{4... | collective-permute-start | bytes 1179656 | tf_op jit(solution)/shard_map/ppermute | solution.py:58
  31.9 2.9 %collective-permute-start.3 = (bf16[192,1024]{1,0:T(8,128)(2,1)S(1)}, bf16[192,1024]{1,0:T(8,128)(2,1)S(1)}, u32[]{:S(2)}, u32[]{:S(2)}) collective-permute-start(bf16[192,1024]{1,0:T(8,128)(2,1)S(1)} %get-tuple-element.26), channel_id=1, source_target_pairs={{0,128},{64,192},{128,256},{192,320},{256,384},{320,448},{384,0},{... | collective-permute-start | bytes 1179656 | tf_op jit(solution)/shard_map/ppermute | solution.py:58
  34.8 21.6 %all-to-all-done = bf16[64,9,4,128]{3,2,1,0:T(4,128)(2,1)S(1)} async-done(((bf16[64,9,4,128]{3,2,1,0:T(4,128)(2,1)}), bf16[64,9,4,128]{3,2,1,0:T(4,128)(2,1)S(1)}, u32[]{:S(2)}, u32[]{:S(2)}) %all-to-all-start) | async-done | bytes 589856 | tf_op jit(solution)/shard_map/all_to_all | solution.py:317
  56.4 1.1 shard_map.112
  57.5 1.9 %collective-permute-start = (bf16[384,512]{1,0:T(8,128)(2,1)S(1)}, bf16[384,512]{1,0:T(8,128)(2,1)S(1)}, u32[]{:S(2)}, u32[]{:S(2)}) collective-permute-start(bf16[384,512]{1,0:T(8,128)(2,1)S(1)} %get-tuple-element.22.near_ref), channel_id=1, source_target_pairs={{0,64},{64,0},{128,192},{192,128},{256,320},{320,256},{384,448},{4... | collective-permute-start | bytes 1179656 | tf_op jit(solution)/shard_map/ppermute | solution.py:58
  59.4 4.5 %all-to-all-start.1 = ((bf16[4,192,384]{2,1,0:T(8,128)(2,1)}), bf16[4,192,384]{2,1,0:T(8,128)(2,1)S(1)}, u32[]{:S(2)}, u32[]{:S(2)}) async-start(bf16[4,192,384]{2,1,0:T(8,128)(2,1)} %get-tuple-element.27), calls=%async_computation.1 | async-start | bytes 1179648 | tf_op jit(solution)/shard_map/all_to_all | solution.py:63
  64.7 1.0 copy-done.2
  65.7 1.1 shard_map.114.part_ref
  66.8 7.9 %all-to-all-done.1.act_ref = bf16[4,192,384]{2,1,0:T(8,128)(2,1)S(1)} async-done(((bf16[4,192,384]{2,1,0:T(8,128)(2,1)}), bf16[4,192,384]{2,1,0:T(8,128)(2,1)S(1)}, u32[]{:S(2)}, u32[]{:S(2)}) %all-to-all-start.1) | async-done | bytes 589856 | tf_op jit(solution)/shard_map/all_to_all | solution.py:63
  74.8 1.0 shard_map.115
  75.7 4.2 %all-to-all-start.2 = ((bf16[4,208,384]{2,1,0:T(8,128)(2,1)}), bf16[4,208,384]{2,1,0:T(8,128)(2,1)}, u32[]{:S(2)}, u32[]{:S(2)}) async-start(bf16[4,208,384]{2,1,0:T(8,128)(2,1)} %shard_map.115), calls=%async_computation.2 | async-start | bytes 1277952 | tf_op jit(solution)/shard_map/all_to_all | solution.py:63
  80.5 1.9 %collective-permute-start.4 = (bf16[384,512]{1,0:T(8,128)(2,1)S(1)}, bf16[384,512]{1,0:T(8,128)(2,1)S(1)}, u32[]{:S(2)}, u32[]{:S(2)}) collective-permute-start(bf16[384,512]{1,0:T(8,128)(2,1)S(1)} %shard_map.116), channel_id=1, source_target_pairs={{0,64},{64,0},{128,192},{192,128},{256,320},{320,256},{384,448},{4... | collective-permute-start | bytes 1179656 | tf_op jit(solution)/shard_map/ppermute | solution.py:58
  82.5 1.7 %collective-permute-done.4.refs_4_ = bf16[384,512]{1,0:T(8,128)(2,1)S(1)} collective-permute-done((bf16[384,512]{1,0:T(8,128)(2,1)S(1)}, bf16[384,512]{1,0:T(8,128)(2,1)S(1)}, u32[]{:S(2)}, u32[]{:S(2)}) %collective-permute-start.4) | collective-permute-done | bytes 393248 | tf_op jit(solution)/shard_map/ppermute | solution.py:58
  84.8 5.7 %all-to-all-done.2.back_ref = bf16[4,208,384]{2,1,0:T(8,128)(2,1)} async-done(((bf16[4,208,384]{2,1,0:T(8,128)(2,1)}), bf16[4,208,384]{2,1,0:T(8,128)(2,1)}, u32[]{:S(2)}, u32[]{:S(2)}) %all-to-all-start.2) | async-done | bytes 639008 | tf_op jit(solution)/shard_map/all_to_all | solution.py:63
  90.5 2.3 %shard_map.118 = bf16[2304,128]{1,0:T(8,128)(2,1)} custom-call(bf16[4,208,384]{2,1,0:T(8,128)(2,1)} %all-to-all-done.2.back_ref, f32[384,512]{1,0:T(8,128)S(1)} %shard_map.117.wide_ref), custom_call_target="tpu_custom_call" | custom-call | bytes 1048576 | tf_op jit(solution)/shard_map/pallas_call | solution.py:340
  92.8 6.8 %all-to-all-start.3 = ((bf16[64,9,4,128]{3,2,1,0:T(4,128)(2,1)}), bf16[64,9,4,128]{3,2,1,0:T(4,128)(2,1)S(1)}, u32[]{:S(2)}, u32[]{:S(2)}) async-start(bf16[64,9,4,128]{3,2,1,0:T(4,128)(2,1)} %bitcast.10), calls=%async_computation.3 | async-start | bytes 1179648 | tf_op jit(solution)/shard_map/all_to_all | solution.py:317
  99.6 1.0 shard_map.119
  100.6 2.5 %collective-permute-start.5 = (bf16[192,1024]{1,0:T(8,128)(2,1)S(1)}, bf16[192,1024]{1,0:T(8,128)(2,1)S(1)}, u32[]{:S(2)}, u32[]{:S(2)}) collective-permute-start(bf16[192,1024]{1,0:T(8,128)(2,1)S(1)} %get-tuple-element.29), channel_id=1, source_target_pairs={{0,128},{64,192},{128,256},{192,320},{256,384},{320,448},{384,0},{... | collective-permute-start | bytes 1179656 | tf_op jit(solution)/shard_map/ppermute | solution.py:58
  103.1 4.0 %collective-permute-start.6 = (bf16[192,1024]{1,0:T(8,128)(2,1)S(1)}, bf16[192,1024]{1,0:T(8,128)(2,1)S(1)}, u32[]{:S(2)}, u32[]{:S(2)}) collective-permute-start(bf16[192,1024]{1,0:T(8,128)(2,1)S(1)} %get-tuple-element.30), channel_id=1, source_target_pairs={{0,256},{64,320},{128,384},{192,448},{256,0},{320,64},{384,128},{4... | collective-permute-start | bytes 1179656 | tf_op jit(solution)/shard_map/ppermute | solution.py:58
  107.1 2.5 %collective-permute-start.7 = (bf16[192,1024]{1,0:T(8,128)(2,1)S(1)}, bf16[192,1024]{1,0:T(8,128)(2,1)S(1)}, u32[]{:S(2)}, u32[]{:S(2)}) collective-permute-start(bf16[192,1024]{1,0:T(8,128)(2,1)S(1)} %get-tuple-element.31), channel_id=1, source_target_pairs={{0,384},{64,448},{128,0},{192,64},{256,128},{320,192},{384,256},{4... | collective-permute-start | bytes 1179656 | tf_op jit(solution)/shard_map/ppermute | solution.py:58
  109.6 11.5 %collective-permute-done.5.refs_1_ = bf16[192,1024]{1,0:T(8,128)(2,1)S(1)} collective-permute-done((bf16[192,1024]{1,0:T(8,128)(2,1)S(1)}, bf16[192,1024]{1,0:T(8,128)(2,1)S(1)}, u32[]{:S(2)}, u32[]{:S(2)}) %collective-permute-start.5) | collective-permute-done | bytes 393248 | tf_op jit(solution)/shard_map/ppermute | solution.py:58
  121.1 2.5 %collective-permute-done.7.refs_3_ = bf16[192,1024]{1,0:T(8,128)(2,1)S(1)} collective-permute-done((bf16[192,1024]{1,0:T(8,128)(2,1)S(1)}, bf16[192,1024]{1,0:T(8,128)(2,1)S(1)}, u32[]{:S(2)}, u32[]{:S(2)}) %collective-permute-start.7) | collective-permute-done | bytes 393248 | tf_op jit(solution)/shard_map/ppermute | solution.py:58
  123.6 1.3 shard_map.120
  124.9 7.1 %all-to-all-done.3 = bf16[64,9,4,128]{3,2,1,0:T(4,128)(2,1)S(1)} async-done(((bf16[64,9,4,128]{3,2,1,0:T(4,128)(2,1)}), bf16[64,9,4,128]{3,2,1,0:T(4,128)(2,1)S(1)}, u32[]{:S(2)}, u32[]{:S(2)}) %all-to-all-start.3) | async-done | bytes 589856 | tf_op jit(solution)/shard_map/all_to_all | solution.py:317
  132.0 1.1 shard_map.121
  133.1 1.9 %collective-permute-start.8 = (f32[8,16]{1,0:T(8,128)S(1)}, f32[8,16]{1,0:T(8,128)S(1)}, u32[]{:S(2)}, u32[]{:S(2)}) collective-permute-start(f32[8,16]{1,0:T(8,128)S(1)} %get-tuple-element.37), channel_id=1, source_target_pairs={{0,64},{64,0},{128,192},{192,128},{256,320},{320,256},{384,448},{4... | collective-permute-start | bytes 1544 | tf_op jit(solution)/shard_map/ppermute | solution.py:58
  135.0 1.1 collective-permute-done.8
  (18 shorter events, 2.6 us)
Async XLA Ops:
  3.2 53.2 %all-to-all-start = ((bf16[64,9,4,128]{3,2,1,0:T(4,128)(2,1)}), bf16[64,9,4,128]{3,2,1,0:T(4,128)(2,1)S(1)}, u32[]{:S(2)}, u32[]{:S(2)}) async-start(bf16[64,9,4,128]{3,2,1,0:T(4,128)(2,1)} %bitcast.22), calls=%async_computation | async-start | bytes 1179648 | tf_op jit(solution)/shard_map/all_to_all | solution.py:317
  22.0 1.4 %copy-start = (bf16[1,192,4096]{2,1,0:T(8,128)(2,1)S(1)}, bf16[1,192,4096]{2,1,0:T(8,128)(2,1)}, u32[]{:S(2)}) copy-start(bf16[1,192,4096]{2,1,0:T(8,128)(2,1)} %param.9) | copy-start | bytes 4718596
  24.4 39.5 %collective-permute-start.1 = (bf16[192,1024]{1,0:T(8,128)(2,1)}, bf16[192,1024]{1,0:T(8,128)(2,1)S(1)}, u32[]{:S(2)}, u32[]{:S(2)}) collective-permute-start(bf16[192,1024]{1,0:T(8,128)(2,1)} %get-tuple-element.24), channel_id=1, source_target_pairs={{0,384},{64,448},{128,0},{192,64},{256,128},{320,192},{384,256},{4... | collective-permute-start | bytes 1179656 | tf_op jit(solution)/shard_map/ppermute | solution.py:58
  29.3 34.6 %collective-permute-start.2 = (bf16[192,1024]{1,0:T(8,128)(2,1)}, bf16[192,1024]{1,0:T(8,128)(2,1)S(1)}, u32[]{:S(2)}, u32[]{:S(2)}) collective-permute-start(bf16[192,1024]{1,0:T(8,128)(2,1)} %get-tuple-element.25), channel_id=1, source_target_pairs={{0,256},{64,320},{128,384},{192,448},{256,0},{320,64},{384,128},{4... | collective-permute-start | bytes 1179656 | tf_op jit(solution)/shard_map/ppermute | solution.py:58
  31.9 32.0 %collective-permute-start.3 = (bf16[192,1024]{1,0:T(8,128)(2,1)S(1)}, bf16[192,1024]{1,0:T(8,128)(2,1)S(1)}, u32[]{:S(2)}, u32[]{:S(2)}) collective-permute-start(bf16[192,1024]{1,0:T(8,128)(2,1)S(1)} %get-tuple-element.26), channel_id=1, source_target_pairs={{0,128},{64,192},{128,256},{192,320},{256,384},{320,448},{384,0},{... | collective-permute-start | bytes 1179656 | tf_op jit(solution)/shard_map/ppermute | solution.py:58
  57.5 6.4 %collective-permute-start = (bf16[384,512]{1,0:T(8,128)(2,1)S(1)}, bf16[384,512]{1,0:T(8,128)(2,1)S(1)}, u32[]{:S(2)}, u32[]{:S(2)}) collective-permute-start(bf16[384,512]{1,0:T(8,128)(2,1)S(1)} %get-tuple-element.22.near_ref), channel_id=1, source_target_pairs={{0,64},{64,0},{128,192},{192,128},{256,320},{320,256},{384,448},{4... | collective-permute-start | bytes 1179656 | tf_op jit(solution)/shard_map/ppermute | solution.py:58
  59.4 15.3 %all-to-all-start.1 = ((bf16[4,192,384]{2,1,0:T(8,128)(2,1)}), bf16[4,192,384]{2,1,0:T(8,128)(2,1)S(1)}, u32[]{:S(2)}, u32[]{:S(2)}) async-start(bf16[4,192,384]{2,1,0:T(8,128)(2,1)} %get-tuple-element.27), calls=%async_computation.1 | async-start | bytes 1179648 | tf_op jit(solution)/shard_map/all_to_all | solution.py:63
  63.9 0.8 copy-start.1
  64.7 1.0 copy-start.2
  75.7 14.8 %all-to-all-start.2 = ((bf16[4,208,384]{2,1,0:T(8,128)(2,1)}), bf16[4,208,384]{2,1,0:T(8,128)(2,1)}, u32[]{:S(2)}, u32[]{:S(2)}) async-start(bf16[4,208,384]{2,1,0:T(8,128)(2,1)} %shard_map.115), calls=%async_computation.2 | async-start | bytes 1277952 | tf_op jit(solution)/shard_map/all_to_all | solution.py:63
  80.5 3.6 %collective-permute-start.4 = (bf16[384,512]{1,0:T(8,128)(2,1)S(1)}, bf16[384,512]{1,0:T(8,128)(2,1)S(1)}, u32[]{:S(2)}, u32[]{:S(2)}) collective-permute-start(bf16[384,512]{1,0:T(8,128)(2,1)S(1)} %shard_map.116), channel_id=1, source_target_pairs={{0,64},{64,0},{128,192},{192,128},{256,320},{320,256},{384,448},{4... | collective-permute-start | bytes 1179656 | tf_op jit(solution)/shard_map/ppermute | solution.py:58
  84.8 14.9 %copy-start.3 = (bf16[384,512]{1,0:T(8,128)(2,1)S(1)}, bf16[384,512]{1,0:T(8,128)(2,1)}, u32[]{:S(2)}) copy-start(bf16[384,512]{1,0:T(8,128)(2,1)} %copy-done.1) | copy-start | bytes 1179652
  92.8 39.2 %all-to-all-start.3 = ((bf16[64,9,4,128]{3,2,1,0:T(4,128)(2,1)}), bf16[64,9,4,128]{3,2,1,0:T(4,128)(2,1)S(1)}, u32[]{:S(2)}, u32[]{:S(2)}) async-start(bf16[64,9,4,128]{3,2,1,0:T(4,128)(2,1)} %bitcast.10), calls=%async_computation.3 | async-start | bytes 1179648 | tf_op jit(solution)/shard_map/all_to_all | solution.py:317
  100.6 20.5 %collective-permute-start.5 = (bf16[192,1024]{1,0:T(8,128)(2,1)S(1)}, bf16[192,1024]{1,0:T(8,128)(2,1)S(1)}, u32[]{:S(2)}, u32[]{:S(2)}) collective-permute-start(bf16[192,1024]{1,0:T(8,128)(2,1)S(1)} %get-tuple-element.29), channel_id=1, source_target_pairs={{0,128},{64,192},{128,256},{192,320},{256,384},{320,448},{384,0},{... | collective-permute-start | bytes 1179656 | tf_op jit(solution)/shard_map/ppermute | solution.py:58
  103.1 18.0 %collective-permute-start.6 = (bf16[192,1024]{1,0:T(8,128)(2,1)S(1)}, bf16[192,1024]{1,0:T(8,128)(2,1)S(1)}, u32[]{:S(2)}, u32[]{:S(2)}) collective-permute-start(bf16[192,1024]{1,0:T(8,128)(2,1)S(1)} %get-tuple-element.30), channel_id=1, source_target_pairs={{0,256},{64,320},{128,384},{192,448},{256,0},{320,64},{384,128},{4... | collective-permute-start | bytes 1179656 | tf_op jit(solution)/shard_map/ppermute | solution.py:58
  107.1 16.5 %collective-permute-start.7 = (bf16[192,1024]{1,0:T(8,128)(2,1)S(1)}, bf16[192,1024]{1,0:T(8,128)(2,1)S(1)}, u32[]{:S(2)}, u32[]{:S(2)}) collective-permute-start(bf16[192,1024]{1,0:T(8,128)(2,1)S(1)} %get-tuple-element.31), channel_id=1, source_target_pairs={{0,384},{64,448},{128,0},{192,64},{256,128},{320,192},{384,256},{4... | collective-permute-start | bytes 1179656 | tf_op jit(solution)/shard_map/ppermute | solution.py:58
  123.6 8.4 %copy-start.4 = (s32[128,1]{1,0:T(8,128)S(1)}, s32[128,1]{1,0:T(8,128)}, u32[]{:S(2)}) copy-start(s32[128,1]{1,0:T(8,128)} %get-tuple-element.33.slot_ref) | copy-start | bytes 1540
  123.6 8.4 %copy-start.5 = (f32[16,8]{0,1:T(8,128)S(1)}, f32[16,8]{0,1:T(8,128)}, u32[]{:S(2)}) copy-start(f32[16,8]{0,1:T(8,128)} %param.10) | copy-start | bytes 1540
  133.1 3.0 %collective-permute-start.8 = (f32[8,16]{1,0:T(8,128)S(1)}, f32[8,16]{1,0:T(8,128)S(1)}, u32[]{:S(2)}, u32[]{:S(2)}) collective-permute-start(f32[8,16]{1,0:T(8,128)S(1)} %get-tuple-element.37), channel_id=1, source_target_pairs={{0,64},{64,0},{128,192},{192,128},{256,320},{320,256},{384,448},{4... | collective-permute-start | bytes 1544 | tf_op jit(solution)/shard_map/ppermute | solution.py:58

commit v7 on v6

--- a/solution.py
+++ b/solution.py
@@ -203,43 +203,45 @@
 
 def arrive(got_ref, grad_ref, act_ref, rows_ref, flat_ref):
     rows_ref[...] = got_ref[...].astype(F32)
-    grad, acts = unpack(rows_ref, flat_ref, grad_ref.shape[1], act_ref.shape[1])
+    grad, acts = unpack(rows_ref, flat_ref, grad_ref.shape[1], act_ref.shape[0])
     grad_ref[...] = grad.astype(BF)
-    acts = acts.T.astype(BF)
-    for y in range(NY):
-        act_ref[y] = acts
-
-
-def seal(part_ref, act_ref, out_ref):
-    hidden, slots = act_ref.shape[1:]
-    gate = jnp.zeros((1, slots), F32)
-    for y in range(NY):
-        part = part_ref[y]
-        products = act_ref[y].astype(F32) * part.astype(F32)
-        gate = gate + jnp.sum(products, axis=0, keepdims=True)
-        out_ref[y, :hidden] = part
-    extra = two_parts(gate).astype(BF)
-    for y in range(NY):
-        out_ref[y, hidden:] = extra
+    act_ref[...] = acts.T.astype(BF)
 
 
 def backward(here_ref, near_ref, far_ref, *refs):
-    w_refs, out_ref = refs[:-1], refs[-1]
+    w_refs, (out_ref, both_ref) = refs[:-2], refs[-2:]
     here, feats = here_ref[0], near_ref.shape[1]
     near, far = core_columns(here, 0, feats), core_columns(here, 1, feats)
     for step in range(NY):
         w_ref = w_refs[step]
         part = dot(w_ref[:, near], near_ref[...], 1, 1) + dot(w_ref[:, far], far_ref[...], 1, 1)
         out_ref[chip(here, step)] = part.astype(BF)
-
-
-def forward(other, here_ref, act_ref, *refs):
-    w_refs, more, out_ref = refs[:NY], refs[NY:-1], refs[-1]
-    here = here_ref[0]
-    columns = core_columns(here, other, out_ref.shape[1])
+    core = lax.rem(here, 2)
+    both_ref[core] = near_ref[...]
+    both_ref[1 - core] = far_ref[...]
+
+
+def seal(here_ref, part_ref, *refs):
+    act_refs, out_ref = refs[:-1], refs[-1]
+    hidden, slots = act_refs[0].shape
+    gate = jnp.zeros((1, slots), F32)
+    for step in range(NY):
+        at = chip(here_ref[0], step)
+        part = part_ref[at]
+        products = act_refs[step][...].astype(F32) * part.astype(F32)
+        gate = gate + jnp.sum(products, axis=0, keepdims=True)
+        out_ref[at, :hidden] = part
+    extra = two_parts(gate).astype(BF)
+    for y in range(NY):
+        out_ref[y, hidden:] = extra
+
+
+def forward(other, here_ref, *refs):
+    act_refs, w_refs, more, out_ref = refs[:NY], refs[NY : 2 * NY], refs[2 * NY : -1], refs[-1]
+    columns = core_columns(here_ref[0], other, out_ref.shape[1])
     total = more[0][...].astype(F32) if more else None
-    for step in range(NY):
-        part = dot(act_ref[chip(here, step)], w_refs[step][:, columns], 0, 0)
+    for act_ref, w_ref in zip(act_refs, w_refs):
+        part = dot(act_ref[...], w_ref[:, columns], 0, 0)
         total = part if total is None else total + part
     out_ref[...] = total.astype(out_ref.dtype)
 
@@ -252,13 +254,12 @@
     sent_ref[...] = rows_ref[...].astype(BF)
 
 
-def weights_back(here_ref, near_ref, far_ref, act_ref, *outs):
-    here, feats = here_ref[0], near_ref.shape[1]
-    near, far = core_columns(here, 0, feats), core_columns(here, 1, feats)
-    for step in range(NY):
-        acts = act_ref[chip(here, step)]
-        outs[step][:, near] = dot(acts, near_ref[...], 1, 0).astype(BF)
-        outs[step][:, far] = dot(acts, far_ref[...], 1, 0).astype(BF)
+def weights_back(both_ref, *refs):
+    feats = both_ref.shape[2]
+    for act_ref, out_ref in zip(refs[:NY], refs[NY:]):
+        for core in range(2):
+            part = dot(act_ref[...], both_ref[core], 1, 0)
+            out_ref[:, core * feats : (core + 1) * feats] = part.astype(BF)
 
 
 def collect(got_ref, slot_ref, gate_ref, mixed_ref, back_ref, gate_out_ref, rows_ref, flat_ref):
@@ -318,31 +319,35 @@
 
     got = exchange(sent)
     flops = 2 * slots * feats * hidden * 2 * NY
-    stack = shape((NY, hidden, slots))
-    grad, own_act = call(arrive, [shape((slots, feats)), stack], [VM], scratch=scratch)(got)
-    near_act = exchange_y(own_act)
+    grad, own_act = call(
+        arrive, [shape((slots, feats)), shape((hidden, slots))], [VM], scratch=scratch
+    )(got)
     far_grad = send(grad, 0, 1)
-    back = call(backward, stack, [SM] + [VM] * (2 + NY), flops=flops)(
-        here, grad, far_grad, *weights
-    )
-    back = call(seal, shape((NY, hidden + EXTRA, slots)), [VM] * 2)(back, near_act)
+    all_acts = [own_act] + [send(own_act, NY - step, 0) for step in range(1, NY)]
+    parts, both = call(
+        backward,
+        [shape((NY, hidden, slots)), shape((2, slots, feats))],
+        [SM] + [VM] * (2 + NY),
+        flops=flops,
+    )(here, grad, far_grad, *weights)
+    back = call(seal, shape((NY, hidden + EXTRA, slots)), [SM] + [VM] * (1 + NY))(
+        here, parts, *all_acts
+    )
     back = exchange_y(back)
 
     def part(other, dtype, *more):
         return call(
             functools.partial(forward, other),
             shape((slots, feats), dtype),
-            [SM] + [VM] * (1 + NY + len(more)),
+            [SM] + [VM] * (2 * NY + len(more)),
             flops=flops // 2,
-        )(here, near_act, *weights, *more)
+        )(here, *all_acts, *weights, *more)
 
     wide = part(0, F32, send(part(1, BF), 0, 1))
     returned = call(leave, payload, [VM] * 2, scratch=scratch)(back, wide)
     home = exchange(returned)
 
-    pieces = call(weights_back, pieces_shape, [SM] + [VM] * 3, flops=flops)(
-        here, grad, far_grad, near_act
-    )
+    pieces = call(weights_back, pieces_shape, [VM] * (1 + NY), flops=flops)(both, *all_acts)
     joined = [pieces[0]] + [send(pieces[step], step, 0) for step in range(1, NY)]
     weight_grad = call(
         join_gradient, shape((hidden, 2 * NY * feats)), [SM] + [VM] * NY, moved=3 << 20

time: 139 us -> 139 us (level)
  starting transfers between devices: 59.3 us -> 64.5 us
  waiting for transfers between devices: 59.2 us -> 55.3 us
  Pallas kernels: 13.6 us -> 11.7 us
    ppermute x9 -> x12, starting transfers between devices: 25 us -> 35.4 us  [send(): return lax.ppermute(value, 'dp', pairs)]
    all_to_all x2 -> x1, waiting for transfers between devices: 13.6 us -> 5.17 us  [exchange_y(): lax.all_to_all(value, 'dp', 0, 0, axis_index_groups=groups, tiled=True)]
    ppermute x9 -> x12, waiting for transfers between devices: 16.8 us -> 22.3 us  [send(): return lax.ppermute(value, 'dp', pairs)]
    all_to_all x2 -> x1, starting transfers between devices: 8.64 us -> 3.48 us  [exchange_y(): lax.all_to_all(value, 'dp', 0, 0, axis_index_groups=groups, tiled=True)]
    unnamed x12 -> x16, local copies, waits for them, and re-layouts: 3.17 us -> 4.33 us
  transfers between devices with their start and end apart: 13 -> 15, of which waited for: 8 -> 9; matrix products, arithmetic and copies ran while one was open for 0% -> 0% of each run, Pallas kernels for 5% -> 4%
where the time goes in v7:
time: 139 us; the launch traced here: 137 us
  starting transfers between devices  64.5 us (46%)
  waiting for transfers between devices  55.3 us (40%)
  Pallas kernels  11.7 us (8%)
  local copies, waits for them, and re-layouts  4.33 us (3%)
    ppermute x12, starting transfers between devices, send(): return lax.ppermute(value, 'dp', pairs)  35.4 us
    all_to_all x2, waiting for transfers between devices, exchange(): lax.all_to_all(value, 'expert', 0, 0, tiled=True).reshape(payload.shape)  27.8 us
    all_to_all x2, starting transfers between devices, exchange(): lax.all_to_all(value, 'expert', 0, 0, tiled=True).reshape(payload.shape)  25.6 us
    ppermute x12, waiting for transfers between devices, send(): return lax.ppermute(value, 'dp', pairs)  22.3 us
    all_to_all x1, waiting for transfers between devices, exchange_y(): lax.all_to_all(value, 'dp', 0, 0, axis_index_groups=groups, tiled=True)  5.17 us
    unnamed x16, local copies, waits for them, and re-layouts  4.33 us
    all_to_all x1, starting transfers between devices, exchange_y(): lax.all_to_all(value, 'dp', 0, 0, axis_index_groups=groups, tiled=True)  3.48 us
  transfers between devices with their start and end apart: 15, of which 9 were waited for; matrix products, arithmetic and copies ran while one was open for 0% of the time, Pallas kernels for 4%

profile of v7, /device:TPU:6, one launch (start us, length us, event | category | flops | bytes accessed | tf_op | source)
XLA Modules:
  0.0 137.2 jit_solution(6008277356401882262)
XLA Ops:
  0.6 2.6 %shard_map.111 = (bf16[2304,128]{1,0:T(8,128)(2,1)}, s32[128,1]{1,0:T(8,128)}) custom-call(s32[8,16]{1,0:T(8,128)} %bitcast.24, s32[8,16]{1,0:T(8,128)} %bitcast.25, s32[2,16]{1,0:T(2,128)} %bitcast.26, s32[1,64]{1,0:T(1,128)} %bitcast.27, bf16[128,192]{1,0:T(8,128)(2,1)} %bitcast.23, bf16[16,512]{1,0:T(8,128)(2,1)} %cot_hbm.1, f32[8,16]{1,0:T(8,128)} %bitcast.19), custom_call_target="tpu_custom_call" | custom-call | bytes 1048576 | tf_op jit(solution)/shard_map/pallas_call | solution.py:306
  3.2 18.8 %all-to-all-start = ((bf16[64,9,4,128]{3,2,1,0:T(4,128)(2,1)}), bf16[64,9,4,128]{3,2,1,0:T(4,128)(2,1)S(1)}, u32[]{:S(2)}, u32[]{:S(2)}) async-start(bf16[64,9,4,128]{3,2,1,0:T(4,128)(2,1)} %bitcast.22), calls=%async_computation | async-start | bytes 1179648 | tf_op jit(solution)/shard_map/all_to_all | solution.py:318
  22.0 1.4 %copy-done = bf16[1,192,4096]{2,1,0:T(8,128)(2,1)S(1)} copy-done((bf16[1,192,4096]{2,1,0:T(8,128)(2,1)S(1)}, bf16[1,192,4096]{2,1,0:T(8,128)(2,1)}, u32[]{:S(2)}) %copy-start) | copy-done | bytes 1572888
  24.3 4.9 %collective-permute-start.1 = (bf16[192,1024]{1,0:T(8,128)(2,1)}, bf16[192,1024]{1,0:T(8,128)(2,1)S(1)}, u32[]{:S(2)}, u32[]{:S(2)}) collective-permute-start(bf16[192,1024]{1,0:T(8,128)(2,1)} %get-tuple-element.26), channel_id=1, source_target_pairs={{0,384},{64,448},{128,0},{192,64},{256,128},{320,192},{384,256},{4... | collective-permute-start | bytes 1179656 | tf_op jit(solution)/shard_map/ppermute | solution.py:58
  29.2 2.5 %collective-permute-start.2 = (bf16[192,1024]{1,0:T(8,128)(2,1)S(1)}, bf16[192,1024]{1,0:T(8,128)(2,1)S(1)}, u32[]{:S(2)}, u32[]{:S(2)}) collective-permute-start(bf16[192,1024]{1,0:T(8,128)(2,1)S(1)} %get-tuple-element.27), channel_id=1, source_target_pairs={{0,256},{64,320},{128,384},{192,448},{256,0},{320,64},{384,128},{4... | collective-permute-start | bytes 1179656 | tf_op jit(solution)/shard_map/ppermute | solution.py:58
  31.8 2.9 %collective-permute-start.3 = (bf16[192,1024]{1,0:T(8,128)(2,1)S(1)}, bf16[192,1024]{1,0:T(8,128)(2,1)S(1)}, u32[]{:S(2)}, u32[]{:S(2)}) collective-permute-start(bf16[192,1024]{1,0:T(8,128)(2,1)S(1)} %get-tuple-element.28), channel_id=1, source_target_pairs={{0,128},{64,192},{128,256},{192,320},{256,384},{320,448},{384,0},{... | collective-permute-start | bytes 1179656 | tf_op jit(solution)/shard_map/ppermute | solution.py:58
  34.6 21.8 %all-to-all-done = bf16[64,9,4,128]{3,2,1,0:T(4,128)(2,1)S(1)} async-done(((bf16[64,9,4,128]{3,2,1,0:T(4,128)(2,1)}), bf16[64,9,4,128]{3,2,1,0:T(4,128)(2,1)S(1)}, u32[]{:S(2)}, u32[]{:S(2)}) %all-to-all-start) | async-done | bytes 589856 | tf_op jit(solution)/shard_map/all_to_all | solution.py:318
  56.7 1.9 %collective-permute-start = (bf16[384,512]{1,0:T(8,128)(2,1)S(1)}, bf16[384,512]{1,0:T(8,128)(2,1)S(1)}, u32[]{:S(2)}, u32[]{:S(2)}) collective-permute-start(bf16[384,512]{1,0:T(8,128)(2,1)S(1)} %get-tuple-element.24.near_ref), channel_id=1, source_target_pairs={{0,64},{64,0},{128,192},{192,128},{256,320},{320,256},{384,448},{4... | collective-permute-start | bytes 1179656 | tf_op jit(solution)/shard_map/ppermute | solution.py:58
  58.6 4.9 %collective-permute-start.4 = (bf16[192,384]{1,0:T(8,128)(2,1)S(1)}, bf16[192,384]{1,0:T(8,128)(2,1)S(1)}, u32[]{:S(2)}, u32[]{:S(2)}) collective-permute-start(bf16[192,384]{1,0:T(8,128)(2,1)S(1)} %get-tuple-element.30.refs_0_), channel_id=1, source_target_pairs={{0,384},{64,448},{128,0},{192,64},{256,128},{320,192},{384,256},{4... | collective-permute-start | bytes 442376 | tf_op jit(solution)/shard_map/ppermute | solution.py:58
  63.6 2.5 %collective-permute-start.5 = (bf16[192,384]{1,0:T(8,128)(2,1)S(1)}, bf16[192,384]{1,0:T(8,128)(2,1)S(1)}, u32[]{:S(2)}, u32[]{:S(2)}) collective-permute-start(bf16[192,384]{1,0:T(8,128)(2,1)S(1)} %get-tuple-element.30.refs_0_), channel_id=1, source_target_pairs={{0,256},{64,320},{128,384},{192,448},{256,0},{320,64},{384,128},{4... | collective-permute-start | bytes 442376 | tf_op jit(solution)/shard_map/ppermute | solution.py:58
  66.1 2.9 %collective-permute-start.6 = (bf16[192,384]{1,0:T(8,128)(2,1)S(1)}, bf16[192,384]{1,0:T(8,128)(2,1)S(1)}, u32[]{:S(2)}, u32[]{:S(2)}) collective-permute-start(bf16[192,384]{1,0:T(8,128)(2,1)S(1)} %get-tuple-element.30.refs_0_), channel_id=1, source_target_pairs={{0,128},{64,192},{128,256},{192,320},{256,384},{320,448},{384,0},{... | collective-permute-start | bytes 442376 | tf_op jit(solution)/shard_map/ppermute | solution.py:58
  69.0 1.2 shard_map.114
  71.1 2.5 %collective-permute-done.5.refs_2_ = bf16[192,384]{1,0:T(8,128)(2,1)S(1)} collective-permute-done((bf16[192,384]{1,0:T(8,128)(2,1)S(1)}, bf16[192,384]{1,0:T(8,128)(2,1)S(1)}, u32[]{:S(2)}, u32[]{:S(2)}) %collective-permute-start.5) | collective-permute-done | bytes 147488 | tf_op jit(solution)/shard_map/ppermute | solution.py:58
  73.7 2.4 %collective-permute-done.6.refs_3_ = bf16[192,384]{1,0:T(8,128)(2,1)S(1)} collective-permute-done((bf16[192,384]{1,0:T(8,128)(2,1)S(1)}, bf16[192,384]{1,0:T(8,128)(2,1)S(1)}, u32[]{:S(2)}, u32[]{:S(2)}) %collective-permute-start.6) | collective-permute-done | bytes 147488 | tf_op jit(solution)/shard_map/ppermute | solution.py:58
  76.1 1.0 shard_map.115
  77.1 3.5 %all-to-all-start.1 = ((bf16[4,208,384]{2,1,0:T(8,128)(2,1)}), bf16[4,208,384]{2,1,0:T(8,128)(2,1)S(1)}, u32[]{:S(2)}, u32[]{:S(2)}) async-start(bf16[4,208,384]{2,1,0:T(8,128)(2,1)} %shard_map.115), calls=%async_computation.1 | async-start | bytes 1277952 | tf_op jit(solution)/shard_map/all_to_all | solution.py:63
  81.2 1.9 %collective-permute-start.7 = (bf16[384,512]{1,0:T(8,128)(2,1)S(1)}, bf16[384,512]{1,0:T(8,128)(2,1)S(1)}, u32[]{:S(2)}, u32[]{:S(2)}) collective-permute-start(bf16[384,512]{1,0:T(8,128)(2,1)S(1)} %shard_map.116), channel_id=1, source_target_pairs={{0,64},{64,0},{128,192},{192,128},{256,320},{320,256},{384,448},{4... | collective-permute-start | bytes 1179656 | tf_op jit(solution)/shard_map/ppermute | solution.py:58
  83.1 1.7 %collective-permute-done.7.refs_8_ = bf16[384,512]{1,0:T(8,128)(2,1)S(1)} collective-permute-done((bf16[384,512]{1,0:T(8,128)(2,1)S(1)}, bf16[384,512]{1,0:T(8,128)(2,1)S(1)}, u32[]{:S(2)}, u32[]{:S(2)}) %collective-permute-start.7) | collective-permute-done | bytes 393248 | tf_op jit(solution)/shard_map/ppermute | solution.py:58
  86.4 5.2 %all-to-all-done.1.back_ref = bf16[4,208,384]{2,1,0:T(8,128)(2,1)S(1)} async-done(((bf16[4,208,384]{2,1,0:T(8,128)(2,1)}), bf16[4,208,384]{2,1,0:T(8,128)(2,1)S(1)}, u32[]{:S(2)}, u32[]{:S(2)}) %all-to-all-start.1) | async-done | bytes 639008 | tf_op jit(solution)/shard_map/all_to_all | solution.py:63
  91.5 1.2 shard_map.118
  92.8 6.8 %all-to-all-start.2 = ((bf16[64,9,4,128]{3,2,1,0:T(4,128)(2,1)}), bf16[64,9,4,128]{3,2,1,0:T(4,128)(2,1)S(1)}, u32[]{:S(2)}, u32[]{:S(2)}) async-start(bf16[64,9,4,128]{3,2,1,0:T(4,128)(2,1)} %bitcast.10), calls=%async_computation.2 | async-start | bytes 1179648 | tf_op jit(solution)/shard_map/all_to_all | solution.py:318
  99.6 1.1 copy-done.7
  101.7 2.5 %collective-permute-start.8 = (bf16[192,1024]{1,0:T(8,128)(2,1)S(1)}, bf16[192,1024]{1,0:T(8,128)(2,1)S(1)}, u32[]{:S(2)}, u32[]{:S(2)}) collective-permute-start(bf16[192,1024]{1,0:T(8,128)(2,1)S(1)} %get-tuple-element.33), channel_id=1, source_target_pairs={{0,128},{64,192},{128,256},{192,320},{256,384},{320,448},{384,0},{... | collective-permute-start | bytes 1179656 | tf_op jit(solution)/shard_map/ppermute | solution.py:58
  104.2 4.0 %collective-permute-start.9 = (bf16[192,1024]{1,0:T(8,128)(2,1)S(1)}, bf16[192,1024]{1,0:T(8,128)(2,1)S(1)}, u32[]{:S(2)}, u32[]{:S(2)}) collective-permute-start(bf16[192,1024]{1,0:T(8,128)(2,1)S(1)} %get-tuple-element.34), channel_id=1, source_target_pairs={{0,256},{64,320},{128,384},{192,448},{256,0},{320,64},{384,128},{4... | collective-permute-start | bytes 1179656 | tf_op jit(solution)/shard_map/ppermute | solution.py:58
  108.1 2.5 %collective-permute-start.10 = (bf16[192,1024]{1,0:T(8,128)(2,1)S(1)}, bf16[192,1024]{1,0:T(8,128)(2,1)S(1)}, u32[]{:S(2)}, u32[]{:S(2)}) collective-permute-start(bf16[192,1024]{1,0:T(8,128)(2,1)S(1)} %get-tuple-element.35), channel_id=1, source_target_pairs={{0,384},{64,448},{128,0},{192,64},{256,128},{320,192},{384,256},{4... | collective-permute-start | bytes 1179656 | tf_op jit(solution)/shard_map/ppermute | solution.py:58
  110.7 11.9 %collective-permute-done.8.refs_1_ = bf16[192,1024]{1,0:T(8,128)(2,1)S(1)} collective-permute-done((bf16[192,1024]{1,0:T(8,128)(2,1)S(1)}, bf16[192,1024]{1,0:T(8,128)(2,1)S(1)}, u32[]{:S(2)}, u32[]{:S(2)}) %collective-permute-start.8) | collective-permute-done | bytes 393248 | tf_op jit(solution)/shard_map/ppermute | solution.py:58
  122.6 2.5 %collective-permute-done.10.refs_3_ = bf16[192,1024]{1,0:T(8,128)(2,1)S(1)} collective-permute-done((bf16[192,1024]{1,0:T(8,128)(2,1)S(1)}, bf16[192,1024]{1,0:T(8,128)(2,1)S(1)}, u32[]{:S(2)}, u32[]{:S(2)}) %collective-permute-start.10) | collective-permute-done | bytes 393248 | tf_op jit(solution)/shard_map/ppermute | solution.py:58
  125.2 1.3 shard_map.120
  126.4 6.0 %all-to-all-done.2 = bf16[64,9,4,128]{3,2,1,0:T(4,128)(2,1)S(1)} async-done(((bf16[64,9,4,128]{3,2,1,0:T(4,128)(2,1)}), bf16[64,9,4,128]{3,2,1,0:T(4,128)(2,1)S(1)}, u32[]{:S(2)}, u32[]{:S(2)}) %all-to-all-start.2) | async-done | bytes 589856 | tf_op jit(solution)/shard_map/all_to_all | solution.py:318
  132.5 1.1 shard_map.121
  133.6 1.9 %collective-permute-start.11 = (f32[8,16]{1,0:T(8,128)S(1)}, f32[8,16]{1,0:T(8,128)S(1)}, u32[]{:S(2)}, u32[]{:S(2)}) collective-permute-start(f32[8,16]{1,0:T(8,128)S(1)} %get-tuple-element.41), channel_id=1, source_target_pairs={{0,64},{64,0},{128,192},{192,128},{256,320},{320,256},{384,448},{4... | collective-permute-start | bytes 1544 | tf_op jit(solution)/shard_map/ppermute | solution.py:58
  135.5 1.1 collective-permute-done.11
  (26 shorter events, 5.8 us)
Async XLA Ops:
  3.2 53.2 %all-to-all-start = ((bf16[64,9,4,128]{3,2,1,0:T(4,128)(2,1)}), bf16[64,9,4,128]{3,2,1,0:T(4,128)(2,1)S(1)}, u32[]{:S(2)}, u32[]{:S(2)}) async-start(bf16[64,9,4,128]{3,2,1,0:T(4,128)(2,1)} %bitcast.22), calls=%async_computation | async-start | bytes 1179648 | tf_op jit(solution)/shard_map/all_to_all | solution.py:318
  22.0 1.4 %copy-start = (bf16[1,192,4096]{2,1,0:T(8,128)(2,1)S(1)}, bf16[1,192,4096]{2,1,0:T(8,128)(2,1)}, u32[]{:S(2)}) copy-start(bf16[1,192,4096]{2,1,0:T(8,128)(2,1)} %param.9) | copy-start | bytes 4718596
  24.3 39.3 %collective-permute-start.1 = (bf16[192,1024]{1,0:T(8,128)(2,1)}, bf16[192,1024]{1,0:T(8,128)(2,1)S(1)}, u32[]{:S(2)}, u32[]{:S(2)}) collective-permute-start(bf16[192,1024]{1,0:T(8,128)(2,1)} %get-tuple-element.26), channel_id=1, source_target_pairs={{0,384},{64,448},{128,0},{192,64},{256,128},{320,192},{384,256},{4... | collective-permute-start | bytes 1179656 | tf_op jit(solution)/shard_map/ppermute | solution.py:58
  29.2 36.9 %collective-permute-start.2 = (bf16[192,1024]{1,0:T(8,128)(2,1)S(1)}, bf16[192,1024]{1,0:T(8,128)(2,1)S(1)}, u32[]{:S(2)}, u32[]{:S(2)}) collective-permute-start(bf16[192,1024]{1,0:T(8,128)(2,1)S(1)} %get-tuple-element.27), channel_id=1, source_target_pairs={{0,256},{64,320},{128,384},{192,448},{256,0},{320,64},{384,128},{4... | collective-permute-start | bytes 1179656 | tf_op jit(solution)/shard_map/ppermute | solution.py:58
  31.8 37.3 %collective-permute-start.3 = (bf16[192,1024]{1,0:T(8,128)(2,1)S(1)}, bf16[192,1024]{1,0:T(8,128)(2,1)S(1)}, u32[]{:S(2)}, u32[]{:S(2)}) collective-permute-start(bf16[192,1024]{1,0:T(8,128)(2,1)S(1)} %get-tuple-element.28), channel_id=1, source_target_pairs={{0,128},{64,192},{128,256},{192,320},{256,384},{320,448},{384,0},{... | collective-permute-start | bytes 1179656 | tf_op jit(solution)/shard_map/ppermute | solution.py:58
  56.7 12.3 %collective-permute-start = (bf16[384,512]{1,0:T(8,128)(2,1)S(1)}, bf16[384,512]{1,0:T(8,128)(2,1)S(1)}, u32[]{:S(2)}, u32[]{:S(2)}) collective-permute-start(bf16[384,512]{1,0:T(8,128)(2,1)S(1)} %get-tuple-element.24.near_ref), channel_id=1, source_target_pairs={{0,64},{64,0},{128,192},{192,128},{256,320},{320,256},{384,448},{4... | collective-permute-start | bytes 1179656 | tf_op jit(solution)/shard_map/ppermute | solution.py:58
  58.6 12.5 %collective-permute-start.4 = (bf16[192,384]{1,0:T(8,128)(2,1)S(1)}, bf16[192,384]{1,0:T(8,128)(2,1)S(1)}, u32[]{:S(2)}, u32[]{:S(2)}) collective-permute-start(bf16[192,384]{1,0:T(8,128)(2,1)S(1)} %get-tuple-element.30.refs_0_), channel_id=1, source_target_pairs={{0,384},{64,448},{128,0},{192,64},{256,128},{320,192},{384,256},{4... | collective-permute-start | bytes 442376 | tf_op jit(solution)/shard_map/ppermute | solution.py:58
  63.6 10.1 %collective-permute-start.5 = (bf16[192,384]{1,0:T(8,128)(2,1)S(1)}, bf16[192,384]{1,0:T(8,128)(2,1)S(1)}, u32[]{:S(2)}, u32[]{:S(2)}) collective-permute-start(bf16[192,384]{1,0:T(8,128)(2,1)S(1)} %get-tuple-element.30.refs_0_), channel_id=1, source_target_pairs={{0,256},{64,320},{128,384},{192,448},{256,0},{320,64},{384,128},{4... | collective-permute-start | bytes 442376 | tf_op jit(solution)/shard_map/ppermute | solution.py:58
  66.1 10.0 %collective-permute-start.6 = (bf16[192,384]{1,0:T(8,128)(2,1)S(1)}, bf16[192,384]{1,0:T(8,128)(2,1)S(1)}, u32[]{:S(2)}, u32[]{:S(2)}) collective-permute-start(bf16[192,384]{1,0:T(8,128)(2,1)S(1)} %get-tuple-element.30.refs_0_), channel_id=1, source_target_pairs={{0,128},{64,192},{128,256},{192,320},{256,384},{320,448},{384,0},{... | collective-permute-start | bytes 442376 | tf_op jit(solution)/shard_map/ppermute | solution.py:58
  70.2 0.9 copy-start.6
  76.1 5.1 %copy-start.1 = (bf16[192,384]{1,0:T(8,128)(2,1)}, bf16[192,384]{1,0:T(8,128)(2,1)S(1)}, u32[]{:S(2)}) copy-start(bf16[192,384]{1,0:T(8,128)(2,1)S(1)} %collective-permute-done.6.refs_3_) | copy-start | bytes 442372
  77.1 14.4 %all-to-all-start.1 = ((bf16[4,208,384]{2,1,0:T(8,128)(2,1)}), bf16[4,208,384]{2,1,0:T(8,128)(2,1)S(1)}, u32[]{:S(2)}, u32[]{:S(2)}) async-start(bf16[4,208,384]{2,1,0:T(8,128)(2,1)} %shard_map.115), calls=%async_computation.1 | async-start | bytes 1277952 | tf_op jit(solution)/shard_map/all_to_all | solution.py:63
  81.2 3.6 %collective-permute-start.7 = (bf16[384,512]{1,0:T(8,128)(2,1)S(1)}, bf16[384,512]{1,0:T(8,128)(2,1)S(1)}, u32[]{:S(2)}, u32[]{:S(2)}) collective-permute-start(bf16[384,512]{1,0:T(8,128)(2,1)S(1)} %shard_map.116), channel_id=1, source_target_pairs={{0,64},{64,0},{128,192},{192,128},{256,320},{320,256},{384,448},{4... | collective-permute-start | bytes 1179656 | tf_op jit(solution)/shard_map/ppermute | solution.py:58
  84.8 0.9 copy-start.2
  86.4 13.2 %copy-start.3 = (bf16[192,384]{1,0:T(8,128)(2,1)S(1)}, bf16[192,384]{1,0:T(8,128)(2,1)}, u32[]{:S(2)}) copy-start(bf16[192,384]{1,0:T(8,128)(2,1)} %copy-done.1) | copy-start | bytes 442372
  92.8 39.7 %all-to-all-start.2 = ((bf16[64,9,4,128]{3,2,1,0:T(4,128)(2,1)}), bf16[64,9,4,128]{3,2,1,0:T(4,128)(2,1)S(1)}, u32[]{:S(2)}, u32[]{:S(2)}) async-start(bf16[64,9,4,128]{3,2,1,0:T(4,128)(2,1)} %bitcast.10), calls=%async_computation.2 | async-start | bytes 1179648 | tf_op jit(solution)/shard_map/all_to_all | solution.py:318
  99.6 1.1 copy-start.7
  101.7 20.9 %collective-permute-start.8 = (bf16[192,1024]{1,0:T(8,128)(2,1)S(1)}, bf16[192,1024]{1,0:T(8,128)(2,1)S(1)}, u32[]{:S(2)}, u32[]{:S(2)}) collective-permute-start(bf16[192,1024]{1,0:T(8,128)(2,1)S(1)} %get-tuple-element.33), channel_id=1, source_target_pairs={{0,128},{64,192},{128,256},{192,320},{256,384},{320,448},{384,0},{... | collective-permute-start | bytes 1179656 | tf_op jit(solution)/shard_map/ppermute | solution.py:58
  104.2 18.5 %collective-permute-start.9 = (bf16[192,1024]{1,0:T(8,128)(2,1)S(1)}, bf16[192,1024]{1,0:T(8,128)(2,1)S(1)}, u32[]{:S(2)}, u32[]{:S(2)}) collective-permute-start(bf16[192,1024]{1,0:T(8,128)(2,1)S(1)} %get-tuple-element.34), channel_id=1, source_target_pairs={{0,256},{64,320},{128,384},{192,448},{256,0},{320,64},{384,128},{4... | collective-permute-start | bytes 1179656 | tf_op jit(solution)/shard_map/ppermute | solution.py:58
  108.1 17.0 %collective-permute-start.10 = (bf16[192,1024]{1,0:T(8,128)(2,1)S(1)}, bf16[192,1024]{1,0:T(8,128)(2,1)S(1)}, u32[]{:S(2)}, u32[]{:S(2)}) collective-permute-start(bf16[192,1024]{1,0:T(8,128)(2,1)S(1)} %get-tuple-element.35), channel_id=1, source_target_pairs={{0,384},{64,448},{128,0},{192,64},{256,128},{320,192},{384,256},{4... | collective-permute-start | bytes 1179656 | tf_op jit(solution)/shard_map/ppermute | solution.py:58
  125.2 7.3 %copy-start.4 = (s32[128,1]{1,0:T(8,128)S(1)}, s32[128,1]{1,0:T(8,128)}, u32[]{:S(2)}) copy-start(s32[128,1]{1,0:T(8,128)} %get-tuple-element.37.slot_ref) | copy-start | bytes 1540
  125.2 7.3 %copy-start.5 = (f32[16,8]{0,1:T(8,128)S(1)}, f32[16,8]{0,1:T(8,128)}, u32[]{:S(2)}) copy-start(f32[16,8]{0,1:T(8,128)} %param.10) | copy-start | bytes 1540
  133.6 3.0 %collective-permute-start.11 = (f32[8,16]{1,0:T(8,128)S(1)}, f32[8,16]{1,0:T(8,128)S(1)}, u32[]{:S(2)}, u32[]{:S(2)}) collective-permute-start(f32[8,16]{1,0:T(8,128)S(1)} %get-tuple-element.41), channel_id=1, source_target_pairs={{0,64},{64,0},{128,192},{192,128},{256,320},{320,256},{384,448},{4... | collective-permute-start | bytes 1544 | tf_op jit(solution)/shard_map/ppermute | solution.py:58

commit v8 on v5

--- a/solution.py
+++ b/solution.py
@@ -190,38 +190,40 @@
 
 
 def backward(here_ref, near_ref, far_ref, *refs):
-    w_refs, out_ref = refs[:-1], refs[-1]
+    w_refs, (out_ref, both_ref) = refs[:-2], refs[-2:]
     here, feats = here_ref[0], near_ref.shape[1]
     near, far = core_columns(here, 0, feats), core_columns(here, 1, feats)
     for step in range(NY):
         w_ref = w_refs[step]
         part = dot(w_ref[:, near], near_ref[...], 1, 1) + dot(w_ref[:, far], far_ref[...], 1, 1)
         out_ref[chip(here, step)] = part.astype(BF)
+    core = lax.rem(here, 2)
+    both_ref[core] = near_ref[...]
+    both_ref[1 - core] = far_ref[...]
 
 
 def forward(other, here_ref, *refs):
-    act_refs, w_refs, out_ref = refs[:NY], refs[NY:-1], refs[-1]
+    act_refs, w_refs, more, out_ref = refs[:NY], refs[NY : 2 * NY], refs[2 * NY : -1], refs[-1]
     columns = core_columns(here_ref[0], other, out_ref.shape[1])
-    total = None
+    total = more[0][...].astype(F32) if more else None
     for act_ref, w_ref in zip(act_refs, w_refs):
         part = dot(act_ref[...], w_ref[:, columns], 0, 0)
         total = part if total is None else total + part
     out_ref[...] = total.astype(out_ref.dtype)
 
 
-def leave(back_ref, own_ref, swapped_ref, sent_ref, rows_ref, flat_ref):
+def leave(back_ref, wide_ref, sent_ref, rows_ref, flat_ref):
     back = sum(back_ref[y].astype(F32) for y in range(NY))
-    pack(rows_ref, flat_ref, own_ref[...] + swapped_ref[...].astype(F32), back.T)
+    pack(rows_ref, flat_ref, wide_ref[...], back.T)
     sent_ref[...] = rows_ref[...].astype(BF)
 
 
-def weights_back(here_ref, near_ref, far_ref, *refs):
-    act_refs, outs = refs[:NY], refs[NY:]
-    here, feats = here_ref[0], near_ref.shape[1]
-    near, far = core_columns(here, 0, feats), core_columns(here, 1, feats)
-    for act_ref, out_ref in zip(act_refs, outs):
-        out_ref[:, near] = dot(act_ref[...], near_ref[...], 1, 0).astype(BF)
-        out_ref[:, far] = dot(act_ref[...], far_ref[...], 1, 0).astype(BF)
+def weights_back(both_ref, *refs):
+    feats = both_ref.shape[2]
+    for act_ref, out_ref in zip(refs[:NY], refs[NY:]):
+        for core in range(2):
+            part = dot(act_ref[...], both_ref[core], 1, 0)
+            out_ref[:, core * feats : (core + 1) * feats] = part.astype(BF)
 
 
 def collect(got_ref, slot_ref, gate_ref, act_ref, mixed_ref, back_ref, gate_out_ref, rows_ref, flat_ref):
@@ -288,26 +290,27 @@
     )(got)
     far_grad = send(grad, 0, 1)
     all_acts = [own_act] + [send(own_act, NY - step, 0) for step in range(1, NY)]
-    back = call(backward, shape((NY, hidden, slots)), [SM] + [VM] * (2 + NY), flops=flops)(
-        here, grad, far_grad, *weights
-    )
-    back = exchange_y(back)
-
-    def part(other, dtype):
+    parts, both = call(
+        backward,
+        [shape((NY, hidden, slots)), shape((2, slots, feats))],
+        [SM] + [VM] * (2 + NY),
+        flops=flops,
+    )(here, grad, far_grad, *weights)
+    back = exchange_y(parts)
+
+    def part(other, dtype, *more):
         return call(
             functools.partial(forward, other),
             shape((slots, feats), dtype),
-            [SM] + [VM] * (2 * NY),
+            [SM] + [VM] * (2 * NY + len(more)),
             flops=flops // 2,
-        )(here, *all_acts, *weights)
-
-    swapped = send(part(1, BF), 0, 1)
-    returned = call(leave, payload, [VM] * 3, scratch=scratch)(back, part(0, F32), swapped)
+        )(here, *all_acts, *weights, *more)
+
+    wide = part(0, F32, send(part(1, BF), 0, 1))
+    returned = call(leave, payload, [VM] * 2, scratch=scratch)(back, wide)
     home = exchange(returned)
 
-    pieces = call(weights_back, pieces_shape, [SM] + [VM] * (2 + NY), flops=flops)(
-        here, grad, far_grad, *all_acts
-    )
+    pieces = call(weights_back, pieces_shape, [VM] * (1 + NY), flops=flops)(both, *all_acts)
     joined = [pieces[0]] + [send(pieces[step], step, 0) for step in range(1, NY)]
     weight_grad = call(
         join_gradient, shape((hidden, 2 * NY * feats)), [SM] + [VM] * NY, moved=3 << 20

time: 139 us -> 137 us (0.986)
  local copies, waits for them, and re-layouts: 5.27 us -> 3.14 us
    unnamed x20 -> x12, local copies, waits for them, and re-layouts: 4.67 us -> 2.55 us
    ppermute x11, waiting for transfers between devices: 15.2 us -> 17.2 us  [send(): return lax.ppermute(value, 'dp', pairs)]
  transfers between devices with their start and end apart: 14 -> 14, of which waited for: 6 -> 7; matrix products, arithmetic and copies ran while one was open for 0% -> 0% of each run, Pallas kernels for 5% -> 5%
where the time goes in v8:
time: 137 us; the launch traced here: 135 us
  starting transfers between devices  62.7 us (46%)
  waiting for transfers between devices  48.9 us (36%)
  Pallas kernels  11.4 us (8%)
  blocking collectives  8 us (6%)
  local copies, waits for them, and re-layouts  3.14 us (2%)
    ppermute x11, starting transfers between devices, send(): return lax.ppermute(value, 'dp', pairs)  33.6 us
    all_to_all x2, waiting for transfers between devices, exchange(): lax.all_to_all(value, 'expert', 0, 0, tiled=True).reshape(payload.shape)  27.8 us
    all_to_all x2, starting transfers between devices, exchange(): lax.all_to_all(value, 'expert', 0, 0, tiled=True).reshape(payload.shape)  25.6 us
    ppermute x11, waiting for transfers between devices, send(): return lax.ppermute(value, 'dp', pairs)  17.2 us
    all_to_all x1, blocking collectives, on_device(): gate_parts = lax.all_to_all(gate_parts, 'dp', 0, 0, tiled=True)  8 us
    all_to_all x1, waiting for transfers between devices, exchange_y(): lax.all_to_all(value, 'dp', 0, 0, axis_index_groups=groups, tiled=True)  3.89 us
    all_to_all x1, starting transfers between devices, exchange_y(): lax.all_to_all(value, 'dp', 0, 0, axis_index_groups=groups, tiled=True)  3.54 us
  transfers between devices with their start and end apart: 14, of which 7 were waited for; matrix products, arithmetic and copies ran while one was open for 0% of the time, Pallas kernels for 5%

profile of v8, /device:TPU:6, one launch (start us, length us, event | category | flops | bytes accessed | tf_op | source)
XLA Modules:
  0.0 135.1 jit_solution(14295705598550835096)
XLA Ops:
  0.6 2.6 %shard_map.111 = (bf16[2304,128]{1,0:T(8,128)(2,1)}, s32[128,1]{1,0:T(8,128)}) custom-call(s32[8,16]{1,0:T(8,128)} %bitcast.25, s32[8,16]{1,0:T(8,128)} %bitcast.26, s32[2,16]{1,0:T(2,128)} %bitcast.27, s32[1,64]{1,0:T(1,128)} %bitcast.28, bf16[128,192]{1,0:T(8,128)(2,1)} %bitcast.19, bf16[16,512]{1,0:T(8,128)(2,1)} %cot_hbm.1, f32[8,16]{1,0:T(8,128)} %bitcast.21), custom_call_target="tpu_custom_call" | custom-call | bytes 1048576 | tf_op jit(solution)/shard_map/pallas_call | solution.py:272
  3.2 18.8 %all-to-all-start = ((bf16[64,9,4,128]{3,2,1,0:T(4,128)(2,1)}), bf16[64,9,4,128]{3,2,1,0:T(4,128)(2,1)S(1)}, u32[]{:S(2)}, u32[]{:S(2)}) async-start(bf16[64,9,4,128]{3,2,1,0:T(4,128)(2,1)} %bitcast.24), calls=%async_computation | async-start | bytes 1179648 | tf_op jit(solution)/shard_map/all_to_all | solution.py:284
  22.0 1.4 %copy-done = bf16[1,192,4096]{2,1,0:T(8,128)(2,1)S(1)} copy-done((bf16[1,192,4096]{2,1,0:T(8,128)(2,1)S(1)}, bf16[1,192,4096]{2,1,0:T(8,128)(2,1)}, u32[]{:S(2)}) %copy-start) | copy-done | bytes 1572888
  23.4 0.8 shard_map.113
  24.3 4.9 %collective-permute-start.1 = (bf16[192,1024]{1,0:T(8,128)(2,1)}, bf16[192,1024]{1,0:T(8,128)(2,1)S(1)}, u32[]{:S(2)}, u32[]{:S(2)}) collective-permute-start(bf16[192,1024]{1,0:T(8,128)(2,1)} %get-tuple-element.26), channel_id=1, source_target_pairs={{0,384},{64,448},{128,0},{192,64},{256,128},{320,192},{384,256},{4... | collective-permute-start | bytes 1179656 | tf_op jit(solution)/shard_map/ppermute | solution.py:57
  29.2 2.5 %collective-permute-start.2 = (bf16[192,1024]{1,0:T(8,128)(2,1)S(1)}, bf16[192,1024]{1,0:T(8,128)(2,1)S(1)}, u32[]{:S(2)}, u32[]{:S(2)}) collective-permute-start(bf16[192,1024]{1,0:T(8,128)(2,1)S(1)} %get-tuple-element.27), channel_id=1, source_target_pairs={{0,256},{64,320},{128,384},{192,448},{256,0},{320,64},{384,128},{4... | collective-permute-start | bytes 1179656 | tf_op jit(solution)/shard_map/ppermute | solution.py:57
  31.8 2.9 %collective-permute-start.3 = (bf16[192,1024]{1,0:T(8,128)(2,1)S(1)}, bf16[192,1024]{1,0:T(8,128)(2,1)S(1)}, u32[]{:S(2)}, u32[]{:S(2)}) collective-permute-start(bf16[192,1024]{1,0:T(8,128)(2,1)S(1)} %get-tuple-element.28), channel_id=1, source_target_pairs={{0,128},{64,192},{128,256},{192,320},{256,384},{320,448},{384,0},{... | collective-permute-start | bytes 1179656 | tf_op jit(solution)/shard_map/ppermute | solution.py:57
  34.6 21.8 %all-to-all-done = bf16[64,9,4,128]{3,2,1,0:T(4,128)(2,1)S(1)} async-done(((bf16[64,9,4,128]{3,2,1,0:T(4,128)(2,1)}), bf16[64,9,4,128]{3,2,1,0:T(4,128)(2,1)S(1)}, u32[]{:S(2)}, u32[]{:S(2)}) %all-to-all-start) | async-done | bytes 589856 | tf_op jit(solution)/shard_map/all_to_all | solution.py:284
  56.7 1.9 %collective-permute-start = (bf16[384,512]{1,0:T(8,128)(2,1)S(1)}, bf16[384,512]{1,0:T(8,128)(2,1)S(1)}, u32[]{:S(2)}, u32[]{:S(2)}) collective-permute-start(bf16[384,512]{1,0:T(8,128)(2,1)S(1)} %get-tuple-element.24.near_ref), channel_id=1, source_target_pairs={{0,64},{64,0},{128,192},{192,128},{256,320},{320,256},{384,448},{4... | collective-permute-start | bytes 1179656 | tf_op jit(solution)/shard_map/ppermute | solution.py:57
  58.6 4.9 %collective-permute-start.4 = (bf16[192,384]{1,0:T(8,128)(2,1)S(1)}, bf16[192,384]{1,0:T(8,128)(2,1)S(1)}, u32[]{:S(2)}, u32[]{:S(2)}) collective-permute-start(bf16[192,384]{1,0:T(8,128)(2,1)S(1)} %get-tuple-element.30.refs_0_), channel_id=1, source_target_pairs={{0,384},{64,448},{128,0},{192,64},{256,128},{320,192},{384,256},{4... | collective-permute-start | bytes 442376 | tf_op jit(solution)/shard_map/ppermute | solution.py:57
  63.6 2.5 %collective-permute-start.5 = (bf16[192,384]{1,0:T(8,128)(2,1)S(1)}, bf16[192,384]{1,0:T(8,128)(2,1)S(1)}, u32[]{:S(2)}, u32[]{:S(2)}) collective-permute-start(bf16[192,384]{1,0:T(8,128)(2,1)S(1)} %get-tuple-element.30.refs_0_), channel_id=1, source_target_pairs={{0,256},{64,320},{128,384},{192,448},{256,0},{320,64},{384,128},{4... | collective-permute-start | bytes 442376 | tf_op jit(solution)/shard_map/ppermute | solution.py:57
  66.1 2.9 %collective-permute-start.6 = (bf16[192,384]{1,0:T(8,128)(2,1)S(1)}, bf16[192,384]{1,0:T(8,128)(2,1)S(1)}, u32[]{:S(2)}, u32[]{:S(2)}) collective-permute-start(bf16[192,384]{1,0:T(8,128)(2,1)S(1)} %get-tuple-element.30.refs_0_), channel_id=1, source_target_pairs={{0,128},{64,192},{128,256},{192,320},{256,384},{320,448},{384,0},{... | collective-permute-start | bytes 442376 | tf_op jit(solution)/shard_map/ppermute | solution.py:57
  69.0 2.1 %shard_map.114 = (bf16[4,192,384]{2,1,0:T(8,128)(2,1)}, bf16[2,384,512]{2,1,0:T(8,128)(2,1)S(1)}) custom-call(s32[1]{0:T(128)} %bitcast.here_ref, bf16[384,512]{1,0:T(8,128)(2,1)S(1)} %get-tuple-element.24.near_ref, bf16[384,512]{1,0:T(8,128)(2,1)S(1)} %collective-permute-done.far_ref, bf16[192,1024]{1,0:T(8,128)(2,1)S(1)} %get-tuple-element.25.refs_0_.refs_4_, ...), custom_call_target="tpu_custom_call" | custom-call | flops 603979776 | bytes 1048576 | tf_op jit(solution)/shard_map/pallas_call | solution.py:293
  71.1 3.5 %all-to-all-start.1 = ((bf16[4,192,384]{2,1,0:T(8,128)(2,1)}), bf16[4,192,384]{2,1,0:T(8,128)(2,1)S(1)}, u32[]{:S(2)}, u32[]{:S(2)}) async-start(bf16[4,192,384]{2,1,0:T(8,128)(2,1)} %get-tuple-element.29), calls=%async_computation.1 | async-start | bytes 1179648 | tf_op jit(solution)/shard_map/all_to_all | solution.py:62
  74.7 1.4 %collective-permute-done.6.refs_3_ = bf16[192,384]{1,0:T(8,128)(2,1)S(1)} collective-permute-done((bf16[192,384]{1,0:T(8,128)(2,1)S(1)}, bf16[192,384]{1,0:T(8,128)(2,1)S(1)}, u32[]{:S(2)}, u32[]{:S(2)}) %collective-permute-start.6) | collective-permute-done | bytes 147488 | tf_op jit(solution)/shard_map/ppermute | solution.py:57
  76.7 1.9 %collective-permute-start.7 = (bf16[384,512]{1,0:T(8,128)(2,1)S(1)}, bf16[384,512]{1,0:T(8,128)(2,1)S(1)}, u32[]{:S(2)}, u32[]{:S(2)}) collective-permute-start(bf16[384,512]{1,0:T(8,128)(2,1)S(1)} %shard_map.115), channel_id=1, source_target_pairs={{0,64},{64,0},{128,192},{192,128},{256,320},{320,256},{384,448},{4... | collective-permute-start | bytes 1179656 | tf_op jit(solution)/shard_map/ppermute | solution.py:57
  78.6 1.7 %collective-permute-done.7.refs_8_ = bf16[384,512]{1,0:T(8,128)(2,1)S(1)} collective-permute-done((bf16[384,512]{1,0:T(8,128)(2,1)S(1)}, bf16[384,512]{1,0:T(8,128)(2,1)S(1)}, u32[]{:S(2)}, u32[]{:S(2)}) %collective-permute-start.7) | collective-permute-done | bytes 393248 | tf_op jit(solution)/shard_map/ppermute | solution.py:57
  80.3 0.6 shard_map.116.wide_ref
  80.9 3.9 %all-to-all-done.1.back_ref = bf16[4,192,384]{2,1,0:T(8,128)(2,1)S(1)} async-done(((bf16[4,192,384]{2,1,0:T(8,128)(2,1)}), bf16[4,192,384]{2,1,0:T(8,128)(2,1)S(1)}, u32[]{:S(2)}, u32[]{:S(2)}) %all-to-all-start.1) | async-done | bytes 589856 | tf_op jit(solution)/shard_map/all_to_all | solution.py:62
  84.8 1.2 shard_map.117
  86.0 6.8 %all-to-all-start.2 = ((bf16[64,9,4,128]{3,2,1,0:T(4,128)(2,1)}), bf16[64,9,4,128]{3,2,1,0:T(4,128)(2,1)S(1)}, u32[]{:S(2)}, u32[]{:S(2)}) async-start(bf16[64,9,4,128]{3,2,1,0:T(4,128)(2,1)} %bitcast.10), calls=%async_computation.2 | async-start | bytes 1179648 | tf_op jit(solution)/shard_map/all_to_all | solution.py:284
  92.8 1.1 copy-done.5
  93.9 1.0 shard_map.118
  94.9 2.5 %collective-permute-start.8 = (bf16[192,1024]{1,0:T(8,128)(2,1)S(1)}, bf16[192,1024]{1,0:T(8,128)(2,1)S(1)}, u32[]{:S(2)}, u32[]{:S(2)}) collective-permute-start(bf16[192,1024]{1,0:T(8,128)(2,1)S(1)} %get-tuple-element.33), channel_id=1, source_target_pairs={{0,128},{64,192},{128,256},{192,320},{256,384},{320,448},{384,0},{... | collective-permute-start | bytes 1179656 | tf_op jit(solution)/shard_map/ppermute | solution.py:57
  97.4 4.1 %collective-permute-start.9 = (bf16[192,1024]{1,0:T(8,128)(2,1)S(1)}, bf16[192,1024]{1,0:T(8,128)(2,1)S(1)}, u32[]{:S(2)}, u32[]{:S(2)}) collective-permute-start(bf16[192,1024]{1,0:T(8,128)(2,1)S(1)} %get-tuple-element.34), channel_id=1, source_target_pairs={{0,256},{64,320},{128,384},{192,448},{256,0},{320,64},{384,128},{4... | collective-permute-start | bytes 1179656 | tf_op jit(solution)/shard_map/ppermute | solution.py:57
  101.5 2.5 %collective-permute-start.10 = (bf16[192,1024]{1,0:T(8,128)(2,1)S(1)}, bf16[192,1024]{1,0:T(8,128)(2,1)S(1)}, u32[]{:S(2)}, u32[]{:S(2)}) collective-permute-start(bf16[192,1024]{1,0:T(8,128)(2,1)S(1)} %get-tuple-element.35), channel_id=1, source_target_pairs={{0,384},{64,448},{128,0},{192,64},{256,128},{320,192},{384,256},{4... | collective-permute-start | bytes 1179656 | tf_op jit(solution)/shard_map/ppermute | solution.py:57
  104.0 11.5 %collective-permute-done.8.refs_1_ = bf16[192,1024]{1,0:T(8,128)(2,1)S(1)} collective-permute-done((bf16[192,1024]{1,0:T(8,128)(2,1)S(1)}, bf16[192,1024]{1,0:T(8,128)(2,1)S(1)}, u32[]{:S(2)}, u32[]{:S(2)}) %collective-permute-start.8) | collective-permute-done | bytes 393248 | tf_op jit(solution)/shard_map/ppermute | solution.py:57
  115.6 2.5 %collective-permute-done.10.refs_3_ = bf16[192,1024]{1,0:T(8,128)(2,1)S(1)} collective-permute-done((bf16[192,1024]{1,0:T(8,128)(2,1)S(1)}, bf16[192,1024]{1,0:T(8,128)(2,1)S(1)}, u32[]{:S(2)}, u32[]{:S(2)}) %collective-permute-start.10) | collective-permute-done | bytes 393248 | tf_op jit(solution)/shard_map/ppermute | solution.py:57
  118.1 1.3 shard_map.119
  119.4 6.0 %all-to-all-done.2 = bf16[64,9,4,128]{3,2,1,0:T(4,128)(2,1)S(1)} async-done(((bf16[64,9,4,128]{3,2,1,0:T(4,128)(2,1)}), bf16[64,9,4,128]{3,2,1,0:T(4,128)(2,1)S(1)}, u32[]{:S(2)}, u32[]{:S(2)}) %all-to-all-start.2) | async-done | bytes 589856 | tf_op jit(solution)/shard_map/all_to_all | solution.py:284
  125.4 1.0 shard_map.120
  126.5 8.0 %all_to_all.20 = f32[8,8,128]{2,1,0:T(8,128)S(1)} all-to-all(f32[8,8,128]{2,1,0:T(8,128)S(1)} %get-tuple-element.41), channel_id=1, replica_groups=mesh['dp'=8,'expert'=64] {'dp'}, dimensions={0} | all-to-all | bytes 65536 | tf_op jit(solution)/shard_map/all_to_all | solution.py:326
  (21 shorter events, 1.5 us)
Async XLA Ops:
  3.2 53.2 %all-to-all-start = ((bf16[64,9,4,128]{3,2,1,0:T(4,128)(2,1)}), bf16[64,9,4,128]{3,2,1,0:T(4,128)(2,1)S(1)}, u32[]{:S(2)}, u32[]{:S(2)}) async-start(bf16[64,9,4,128]{3,2,1,0:T(4,128)(2,1)} %bitcast.24), calls=%async_computation | async-start | bytes 1179648 | tf_op jit(solution)/shard_map/all_to_all | solution.py:284
  22.0 1.4 %copy-start = (bf16[1,192,4096]{2,1,0:T(8,128)(2,1)S(1)}, bf16[1,192,4096]{2,1,0:T(8,128)(2,1)}, u32[]{:S(2)}) copy-start(bf16[1,192,4096]{2,1,0:T(8,128)(2,1)} %param.9) | copy-start | bytes 4718596
  24.3 39.3 %collective-permute-start.1 = (bf16[192,1024]{1,0:T(8,128)(2,1)}, bf16[192,1024]{1,0:T(8,128)(2,1)S(1)}, u32[]{:S(2)}, u32[]{:S(2)}) collective-permute-start(bf16[192,1024]{1,0:T(8,128)(2,1)} %get-tuple-element.26), channel_id=1, source_target_pairs={{0,384},{64,448},{128,0},{192,64},{256,128},{320,192},{384,256},{4... | collective-permute-start | bytes 1179656 | tf_op jit(solution)/shard_map/ppermute | solution.py:57
  29.2 36.9 %collective-permute-start.2 = (bf16[192,1024]{1,0:T(8,128)(2,1)S(1)}, bf16[192,1024]{1,0:T(8,128)(2,1)S(1)}, u32[]{:S(2)}, u32[]{:S(2)}) collective-permute-start(bf16[192,1024]{1,0:T(8,128)(2,1)S(1)} %get-tuple-element.27), channel_id=1, source_target_pairs={{0,256},{64,320},{128,384},{192,448},{256,0},{320,64},{384,128},{4... | collective-permute-start | bytes 1179656 | tf_op jit(solution)/shard_map/ppermute | solution.py:57
  31.8 37.3 %collective-permute-start.3 = (bf16[192,1024]{1,0:T(8,128)(2,1)S(1)}, bf16[192,1024]{1,0:T(8,128)(2,1)S(1)}, u32[]{:S(2)}, u32[]{:S(2)}) collective-permute-start(bf16[192,1024]{1,0:T(8,128)(2,1)S(1)} %get-tuple-element.28), channel_id=1, source_target_pairs={{0,128},{64,192},{128,256},{192,320},{256,384},{320,448},{384,0},{... | collective-permute-start | bytes 1179656 | tf_op jit(solution)/shard_map/ppermute | solution.py:57
  56.7 12.3 %collective-permute-start = (bf16[384,512]{1,0:T(8,128)(2,1)S(1)}, bf16[384,512]{1,0:T(8,128)(2,1)S(1)}, u32[]{:S(2)}, u32[]{:S(2)}) collective-permute-start(bf16[384,512]{1,0:T(8,128)(2,1)S(1)} %get-tuple-element.24.near_ref), channel_id=1, source_target_pairs={{0,64},{64,0},{128,192},{192,128},{256,320},{320,256},{384,448},{4... | collective-permute-start | bytes 1179656 | tf_op jit(solution)/shard_map/ppermute | solution.py:57
  58.6 16.0 %collective-permute-start.4 = (bf16[192,384]{1,0:T(8,128)(2,1)S(1)}, bf16[192,384]{1,0:T(8,128)(2,1)S(1)}, u32[]{:S(2)}, u32[]{:S(2)}) collective-permute-start(bf16[192,384]{1,0:T(8,128)(2,1)S(1)} %get-tuple-element.30.refs_0_), channel_id=1, source_target_pairs={{0,384},{64,448},{128,0},{192,64},{256,128},{320,192},{384,256},{4... | collective-permute-start | bytes 442376 | tf_op jit(solution)/shard_map/ppermute | solution.py:57
  63.6 11.1 %collective-permute-start.5 = (bf16[192,384]{1,0:T(8,128)(2,1)S(1)}, bf16[192,384]{1,0:T(8,128)(2,1)S(1)}, u32[]{:S(2)}, u32[]{:S(2)}) collective-permute-start(bf16[192,384]{1,0:T(8,128)(2,1)S(1)} %get-tuple-element.30.refs_0_), channel_id=1, source_target_pairs={{0,256},{64,320},{128,384},{192,448},{256,0},{320,64},{384,128},{4... | collective-permute-start | bytes 442376 | tf_op jit(solution)/shard_map/ppermute | solution.py:57
  66.1 10.0 %collective-permute-start.6 = (bf16[192,384]{1,0:T(8,128)(2,1)S(1)}, bf16[192,384]{1,0:T(8,128)(2,1)S(1)}, u32[]{:S(2)}, u32[]{:S(2)}) collective-permute-start(bf16[192,384]{1,0:T(8,128)(2,1)S(1)} %get-tuple-element.30.refs_0_), channel_id=1, source_target_pairs={{0,128},{64,192},{128,256},{192,320},{256,384},{320,448},{384,0},{... | collective-permute-start | bytes 442376 | tf_op jit(solution)/shard_map/ppermute | solution.py:57
  71.1 3.5 %copy-start.4 = (bf16[2,384,512]{2,1,0:T(8,128)(2,1)}, bf16[2,384,512]{2,1,0:T(8,128)(2,1)S(1)}, u32[]{:S(2)}) copy-start(bf16[2,384,512]{2,1,0:T(8,128)(2,1)S(1)} %get-tuple-element.31.both_ref) | copy-start | bytes 2359300
  71.1 13.7 %all-to-all-start.1 = ((bf16[4,192,384]{2,1,0:T(8,128)(2,1)}), bf16[4,192,384]{2,1,0:T(8,128)(2,1)S(1)}, u32[]{:S(2)}, u32[]{:S(2)}) async-start(bf16[4,192,384]{2,1,0:T(8,128)(2,1)} %get-tuple-element.29), calls=%async_computation.1 | async-start | bytes 1179648 | tf_op jit(solution)/shard_map/all_to_all | solution.py:62
  76.7 3.6 %collective-permute-start.7 = (bf16[384,512]{1,0:T(8,128)(2,1)S(1)}, bf16[384,512]{1,0:T(8,128)(2,1)S(1)}, u32[]{:S(2)}, u32[]{:S(2)}) collective-permute-start(bf16[384,512]{1,0:T(8,128)(2,1)S(1)} %shard_map.115), channel_id=1, source_target_pairs={{0,64},{64,0},{128,192},{192,128},{256,320},{320,256},{384,448},{4... | collective-permute-start | bytes 1179656 | tf_op jit(solution)/shard_map/ppermute | solution.py:57
  86.0 39.4 %all-to-all-start.2 = ((bf16[64,9,4,128]{3,2,1,0:T(4,128)(2,1)}), bf16[64,9,4,128]{3,2,1,0:T(4,128)(2,1)S(1)}, u32[]{:S(2)}, u32[]{:S(2)}) async-start(bf16[64,9,4,128]{3,2,1,0:T(4,128)(2,1)} %bitcast.10), calls=%async_computation.2 | async-start | bytes 1179648 | tf_op jit(solution)/shard_map/all_to_all | solution.py:284
  92.8 1.1 copy-start.5
  94.9 20.6 %collective-permute-start.8 = (bf16[192,1024]{1,0:T(8,128)(2,1)S(1)}, bf16[192,1024]{1,0:T(8,128)(2,1)S(1)}, u32[]{:S(2)}, u32[]{:S(2)}) collective-permute-start(bf16[192,1024]{1,0:T(8,128)(2,1)S(1)} %get-tuple-element.33), channel_id=1, source_target_pairs={{0,128},{64,192},{128,256},{192,320},{256,384},{320,448},{384,0},{... | collective-permute-start | bytes 1179656 | tf_op jit(solution)/shard_map/ppermute | solution.py:57
  97.4 18.2 %collective-permute-start.9 = (bf16[192,1024]{1,0:T(8,128)(2,1)S(1)}, bf16[192,1024]{1,0:T(8,128)(2,1)S(1)}, u32[]{:S(2)}, u32[]{:S(2)}) collective-permute-start(bf16[192,1024]{1,0:T(8,128)(2,1)S(1)} %get-tuple-element.34), channel_id=1, source_target_pairs={{0,256},{64,320},{128,384},{192,448},{256,0},{320,64},{384,128},{4... | collective-permute-start | bytes 1179656 | tf_op jit(solution)/shard_map/ppermute | solution.py:57
  101.5 16.6 %collective-permute-start.10 = (bf16[192,1024]{1,0:T(8,128)(2,1)S(1)}, bf16[192,1024]{1,0:T(8,128)(2,1)S(1)}, u32[]{:S(2)}, u32[]{:S(2)}) collective-permute-start(bf16[192,1024]{1,0:T(8,128)(2,1)S(1)} %get-tuple-element.35), channel_id=1, source_target_pairs={{0,384},{64,448},{128,0},{192,64},{256,128},{320,192},{384,256},{4... | collective-permute-start | bytes 1179656 | tf_op jit(solution)/shard_map/ppermute | solution.py:57
  118.1 7.3 %copy-start.1 = (bf16[16,8,192]{2,1,0:T(8,128)(2,1)S(1)}, bf16[16,8,192]{2,1,0:T(8,128)(2,1)}, u32[]{:S(2)}) copy-start(bf16[16,8,192]{2,1,0:T(8,128)(2,1)} %param.8) | copy-start | bytes 147460
  118.1 7.3 %copy-start.2 = (s32[128,1]{1,0:T(8,128)S(1)}, s32[128,1]{1,0:T(8,128)}, u32[]{:S(2)}) copy-start(s32[128,1]{1,0:T(8,128)} %get-tuple-element.37.slot_ref) | copy-start | bytes 1540
  118.1 7.3 %copy-start.3 = (f32[16,8]{0,1:T(8,128)S(1)}, f32[16,8]{0,1:T(8,128)}, u32[]{:S(2)}) copy-start(f32[16,8]{0,1:T(8,128)} %param.10) | copy-start | bytes 1540
